TPU v7x, 32 devices: a whole 2x2x4 slice. The times are simulated.
32 devices in a mesh: groups: 2 (over x), expert: 16 (over z, y, core).
Axes of the slice: x: 2, y: 2, z: 4, core: 2. Of those that a mesh axis runs over, the one named last changes fastest.
Arguments:
- tokens: bfloat16 [4096, 4096], P(('groups', 'expert')), parts along dimension 0, may hold values from -6 to 6
- routes: int32 [4096, 4], P(('groups', 'expert')), parts along dimension 0, may hold values from 0 to 7, all different within a row; in each aligned block of 128 rows (0 to 127, 128 to 255, ...) at most 64 rows name the same one
- route_weights: float32 [4096, 4], P(('groups', 'expert')), parts along dimension 0, may hold values from 0.1 to 1
- gate_weight: bfloat16 [4096, 7168], P(None, 'expert'), may hold values from -0.09375 to 0.09375
- up_weight: bfloat16 [4096, 7168], P(None, 'expert'), may hold values from -0.09375 to 0.09375
- down_weight: bfloat16 [896, 32768], P(None, 'expert'), may hold values from -0.1875 to 0.1875
Outputs:
- mixed: bfloat16 [4096, 4096], P(('groups', 'expert')), parts along dimension 0
There are 2 independent parts, one for each index of `groups`. A program takes and returns all parts, laid end to end along the dimension named above; an argument that names none is the same for every part. Nothing has to cross between parts.
Inputs may be any that keep to these rules, and one draw needn't show every extreme that they name: `routes`: each row names 4 different experts; in each aligned block of 128 rows (the rows of one device) every expert is named by exactly 64 rows.
All inputs are finite; a program needn't handle non-finite values.
Results may differ from a plain program's by a relative error of at most 0.008.
Values may be sent and summed in bfloat16 or wider, within the bound.
No kernel may reach another device: no remote copies, remote signals or barrier semaphores. Data moves between devices by JAX's collectives and lax.ppermute only.
A program may use at most 128 MiB of HBM per device.

v0:
```python
import functools

import jax
import jax.experimental.pallas as pl
import jax.experimental.pallas.tpu as pltpu
import jax.numpy as jnp
from jax import lax
from jax.sharding import PartitionSpec as P

CROSS_ROWS = 40
LANES = 128
LIMIT = 12 << 20


def swapped(x, axis, apart):
    return lax.ppermute(x, axis, [(i, i ^ 1 << apart) for i in range(lax.axis_size(axis))])


def dot32(a, b):
    return jnp.dot(a, b, preferred_element_type=jnp.float32)


def expert_hidden(rows, gate_part, up_part, parity):
    gate = dot32(rows, gate_part)
    upval = dot32(rows, up_part)
    hidden = (jax.nn.silu(gate) * upval).astype(jnp.bfloat16)
    partner = swapped(hidden, "expert", 0)
    return jnp.where(
        parity == 0, jnp.concatenate([hidden, partner], 1), jnp.concatenate([partner, hidden], 1)
    )


def dispatched(tokens, routes, route_weights, gate_weight, up_weight, down_weight):
    tok_rows, top_count = routes.shape
    width = tokens.shape[1]
    half_width = down_weight.shape[1]
    devices = lax.axis_size("expert")
    experts = devices // 2
    capacity = tok_rows * top_count // experts
    parity = lax.axis_index("expert") % 2
    flat = routes.reshape(-1)
    onehot = (flat[:, None] == jnp.arange(experts, dtype=jnp.int32)[None, :]).astype(jnp.int32)
    before = jnp.cumsum(onehot, axis=0) - onehot
    slot_of = jnp.sum(before * onehot, axis=1)
    position = flat * capacity + slot_of
    assign_ids = jnp.arange(flat.shape[0], dtype=jnp.int32) // top_count
    owner = jnp.zeros((experts * capacity,), jnp.int32).at[position].set(assign_ids)
    gathered = tokens[owner]
    outgoing = jnp.broadcast_to(
        gathered.reshape(experts, 1, capacity, width), (experts, 2, capacity, width)
    )
    outgoing = outgoing.reshape(devices, capacity, width)
    received = lax.all_to_all(outgoing, "expert", split_axis=0, concat_axis=0, tiled=True)
    count, items, _ = received.shape
    hidden = expert_hidden(received.reshape(count * items, width), gate_weight, up_weight, parity)
    produced = dot32(hidden, down_weight).astype(jnp.bfloat16)
    returned = lax.all_to_all(
        produced.reshape(count, items, half_width),
        "expert",
        split_axis=0,
        concat_axis=0,
        tiled=True,
    )
    returned = returned.reshape(experts, 2, capacity, half_width).transpose(0, 2, 1, 3)
    expert_rows = returned.reshape(experts * capacity, width)
    picked = expert_rows[position].reshape(tok_rows, top_count, width)
    mixed = jnp.einsum("tk,tkd->td", route_weights, picked.astype(jnp.float32))
    return mixed.astype(jnp.bfloat16)


def along_line(x, pairs):
    moves = [((a * 2 + s) * 2 + c, (b * 2 + s) * 2 + c) for a, b in pairs for s in (0, 1) for c in (0, 1)]
    return lax.ppermute(x, "expert", moves)


OUTER = [(0, 1), (1, 0), (2, 3), (3, 2)]
MIDDLE = [(1, 2), (2, 1)]
OUT = [(1, 0), (2, 3)]
IN = [(0, 1), (3, 2)]
ENDS = [(0, 3), (3, 0)]


def contract(a, b, da, db):
    return lax.dot_general(a, b, (((da,), (db,)), ((), ())), preferred_element_type=jnp.float32)


def iota(shape, dim):
    return lax.broadcasted_iota(jnp.int32, shape, dim)


def eye(n):
    return (iota((n, n), 0) == iota((n, n), 1)).astype(jnp.bfloat16)


def scale_of(ext, expert, experts):
    lane = iota(ext.shape, 1)
    mine = (lane % experts == expert) & (lane < 3 * experts)
    return jnp.sum(jnp.where(mine, ext.astype(jnp.float32), 0.0), axis=1, keepdims=True)


def prepare_kernel(experts, idx, routes, weights, tokens, *refs):
    *chunks, order_out, held, sem = refs
    fetch = pltpu.make_async_copy(tokens, held, sem)
    fetch.start()
    rows, width = tokens.shape
    size = rows // len(chunks)
    f32, bf16 = jnp.float32, jnp.bfloat16
    full = jnp.zeros((experts, rows), f32)
    for k in range(routes.shape[0]):
        full += jnp.where(iota((experts, rows), 0) == routes[k : k + 1], weights[k : k + 1], 0.0)
    high = full.astype(bf16).astype(f32)
    mid = (full - high).astype(bf16).astype(f32)
    parts = jnp.concatenate([high, mid, full - high - mid], 0).astype(bf16)
    spread = (iota((3 * experts, LANES), 0) == iota((3 * experts, LANES), 1)).astype(bf16)
    ext = contract(parts, spread, 0, 0).astype(bf16)
    gray = jnp.zeros((1, rows), jnp.int32)
    bit = jnp.zeros((1, rows), jnp.int32)
    for z in range(experts // 2):
        named = jnp.zeros((1, rows), jnp.int32)
        for k in range(routes.shape[0]):
            named += (routes[k : k + 1] == idx[5] + 2 * z).astype(jnp.int32)
        bit = bit ^ named
        gray = gray * 2 + bit
    across = jnp.broadcast_to(gray.astype(f32), (rows, rows))
    first, second = iota((rows, rows), 0), iota((rows, rows), 1)
    top = jnp.where(first[:8] == 0, across[:8], 0.0).astype(bf16)
    down = contract(top, jnp.ones((8, rows), bf16), 0, 0)
    ahead = (down < across) | ((down == across) & (first < second))
    rank = jnp.sum(ahead.astype(f32), axis=0, keepdims=True).astype(jnp.int32)
    target = rank % len(chunks) * size + rank // len(chunks)
    order = (first == target).astype(bf16)
    order_out[...] = order
    ext = dot32(order, ext).astype(bf16)
    for q, chunk in enumerate(chunks):
        chunk[:, width:] = ext[q * size : (q + 1) * size]
    fetch.wait()
    step = 1024
    for n in range(0, width, step):
        moved = dot32(order, held[:, n : n + step]).astype(bf16)
        for q, chunk in enumerate(chunks):
            chunk[:, n : n + step] = moved[q * size : (q + 1) * size]


def pick_kernel(experts, mode, idx, *refs):
    *blocks, own_out, cross_out, pick_out = refs
    total = blocks[0].shape[1]
    rows = blocks[0].shape[0] * (len(blocks) if mode == "both" else 1)
    own_rows, cross_rows = own_out.shape[0], cross_out.shape[0]
    inner = idx[3] == 1

    def load(cols):
        if mode == "both":
            return jnp.concatenate([b[:, cols] for b in blocks], 0)
        if mode == "either":
            return jnp.where(inner, blocks[0][:, cols], blocks[1][:, cols])
        return blocks[0][:, cols]

    ext = load(slice(total - LANES, total))

    def picks(expert, count):
        mask = jnp.broadcast_to(scale_of(ext, expert, experts) > 0, (rows, LANES)).astype(jnp.bfloat16)
        upto = (iota((rows, rows), 0) <= iota((rows, rows), 1)).astype(jnp.bfloat16)
        place = contract(mask, upto, 0, 0)[:count]
        named = contract(mask, eye(rows), 0, 0)[:count]
        slot = iota((count, rows), 0).astype(jnp.float32)
        return ((named > 0.5) & (place - 1.0 == slot)).astype(jnp.float32)

    own = picks(idx[1], own_rows) if mode == "both" else eye(rows).astype(jnp.float32)
    pick = jnp.concatenate([own, picks(idx[2], cross_rows)], 0).astype(jnp.bfloat16)
    pick_out[...] = pick
    step = total // 3
    for n in range(0, total, step):
        got = dot32(pick, load(slice(n, n + step)))
        own_out[:, n : n + step] = got[:own_rows].astype(jnp.bfloat16)
        cross_out[:, n : n + step] = got[own_rows:].astype(jnp.bfloat16)


def expert_kernel(experts, idx, own, cross, ga, gb, ua, ub, da, db, own_out, cross_out, hidden):
    own_rows, total = own.shape
    width = total - LANES
    core, expert = idx[0], idx[1]
    half = ga.shape[0]
    x = jnp.concatenate([own[:, :width], cross[:, :width]], 0)
    ext = jnp.concatenate([own[:, width:], cross[:, width:]], 0)
    scale = scale_of(ext, expert, experts)
    for place, g, u in ((core, ga, ua), (1 - core, gb, ub)):
        gate = contract(x, g[...], 1, 1)
        upval = contract(x, u[...], 1, 1)
        hidden[place] = (gate / (1.0 + jnp.exp(-gate)) * upval * scale).astype(jnp.bfloat16)
    step = 512
    cols = da.shape[1]
    for n in range(0, 2 * cols, step):
        d, m = (da, n) if n < cols else (db, n - cols)
        made = dot32(hidden[0], d[:half, m : m + step]) + dot32(hidden[1], d[half:, m : m + step])
        own_out[:, n : n + step] = made[:own_rows].astype(jnp.bfloat16)
        cross_out[:, n : n + step] = made[own_rows:].astype(jnp.bfloat16)


def combine_kernel(first, idx, pick, own, cross, *refs):
    *more, out = refs
    width = own.shape[1]
    rows = slice(first, first + out.shape[0])
    step = 1024
    for n in range(0, width, step):
        cols = slice(n, n + step)
        got = contract(pick[...], jnp.concatenate([own[:, cols], cross[:, cols]], 0), 0, 0)[rows]
        for ref in more:
            got += ref[:, cols].astype(jnp.float32)
        out[:, cols] = got.astype(jnp.bfloat16)


def finish_kernel(half, idx, order, pick, own, cross, *refs):
    *more, out, held, sems = refs
    width = own.shape[1]
    step = 1024
    copies = []
    for i, n in enumerate(range(0, width, step)):
        cols = slice(n, n + step)
        got = contract(pick[...], jnp.concatenate([own[:, cols], cross[:, cols]], 0), 0, 0)
        sums = [sum(r[:, cols].astype(jnp.float32) for r in part) for part in (more[:half], more[half:])]
        got = (got + jnp.concatenate(sums, 0)).astype(jnp.bfloat16)
        held[i] = contract(order[...], got, 0, 0).astype(jnp.bfloat16)
        to = pl.ds(pl.multiple_of((idx[4] + n) % width, step), step)
        copies.append(pltpu.make_async_copy(held.at[i], out.at[:, to], sems.at[i]))
        copies[-1].start()
    for c in copies:
        c.wait()


def fence_kernel(idx):
    pass


def run_copies(sems, pairs):
    copies = [pltpu.make_async_copy(s, d, sems.at[i]) for i, (s, d) in enumerate(pairs)]
    for c in copies:
        c.start()
    for c in copies:
        c.wait()


def fetch_kernel(idx, *refs):
    count = len(refs) // 2
    run_copies(refs[-1], zip(refs[:count], refs[count:-1]))


def call(name, kernel, outs, idx, token, args, passes=(), scratch=(), cost=1, left=(), away=False):
    vmem, anywhere = pl.BlockSpec(memory_space=pltpu.VMEM), pl.BlockSpec(memory_space=pl.ANY)
    through = [token, *passes]
    first = 1 + len(args) + len(left)

    def body(*refs):
        ins, rest = refs[:first], refs[first + len(through) :]
        kernel(*ins, *rest[: len(outs)], *rest[len(outs) + len(through) :])

    got = pl.pallas_call(
        body,
        out_shape=[*outs, *(jax.ShapeDtypeStruct(x.shape, x.dtype) for x in through)],
        in_specs=[pl.BlockSpec(memory_space=pltpu.SMEM)]
        + [vmem] * len(args)
        + [anywhere] * len(left)
        + [anywhere] * len(through),
        out_specs=[anywhere if away else vmem] * len(outs) + [anywhere] * len(through),
        input_output_aliases={first + i: len(outs) + i for i in range(len(through))},
        scratch_shapes=list(scratch),
        name=name,
        compiler_params=pltpu.CompilerParams(vmem_limit_bytes=LIMIT),
        cost_estimate=pl.CostEstimate(flops=1, bytes_accessed=cost, transcendentals=0),
    )(idx, *args, *left, *through)
    return got[: len(outs)], got[len(outs)], got[len(outs) + 1 :]


ORDER = [
    ["prep", "EA", "MB", "EB"],
    ["P0", "NA", "Y0"],
    ["f", "OB", "+wg", "+wu"],
    ["W"],
    ["f", "MA"],
    ["P1", "Y1", "QA"],
    ["P2B", "Y2B", "NB"],
    ["F0", "OA"],
    ["P3A", "Y3A", "+Y1"],
    ["F2B", "R2B"],
    ["f", "QB", "+Y3A"],
    ["P2A"],
    ["f", "Y2A"],
    ["F3A"],
    ["C2B", "I2B"],
    ["P3B", "Y3B", "+Y2A"],
    ["F1", "R3A"],
    ["F3B", "+I2B"],
    ["D2B", "R3B"],
    ["C3A", "I3A", "S2B"],
    ["F2A"],
    ["C3B", "I3B", "R2A", "+R3A"],
    ["D3A", "S3A"],
    ["C2A", "R1", "I2A", "+S2B"],
    ["D3B", "S3B", "+R2A"],
    ["D1A", "S1A", "R0"],
    ["D2A", "+R1"],
    ["D1B", "S2A", "S1B", "+I2A"],
    ["fin"],
]


def lined(tokens, routes, route_weights, gate_weight, up_weight, down_weight):
    tok_rows, top_count = routes.shape
    width = tokens.shape[1]
    devices = lax.axis_size("expert")
    experts = devices // 2
    capacity = tok_rows * top_count // experts
    half = gate_weight.shape[1]
    index = lax.axis_index("expert")
    core, side, line = index % 2, index // 2 % 2, index // 4
    inner = ((line == 1) | (line == 2)).astype(jnp.int32)
    idx = jnp.stack(
        [core, 2 * line + side, 2 * line + 1 - side, inner, core * down_weight.shape[1], 1 - side]
    ).astype(jnp.int32)
    rows = tok_rows // 2
    total = width + LANES
    bf16 = jnp.bfloat16

    def in_hbm(x):
        return pltpu.with_memory_space_constraint(x, pltpu.HBM)

    def like(*shape):
        return jax.ShapeDtypeStruct(shape, bf16)

    gate, up = gate_weight.T, up_weight.T

    val = {}
    for name, w in (("wg", gate), ("wu", up), ("wd", down_weight)):
        with jax.named_scope("move_" + name):
            val[name] = swapped(w, "expert", 0)
    steps = {name for name, *_ in ORDER}
    slots = {name[1:] for name in steps if name[0] == "P"}

    def kernel_of(name):
        kind, q = name[:-1], name[-1]
        if name == "prep":
            return (
                functools.partial(prepare_kernel, experts),
                [like(rows, total), like(rows, total), like(tok_rows, tok_rows)],
                [in_hbm(routes.T), in_hbm(route_weights.T)],
                [pltpu.VMEM(tokens.shape, bf16), pltpu.SemaphoreType.DMA],
            )
        if name[0] == "P":
            slot = name[1:]
            if slot in ("0", "1"):
                blocks, mode = [["payA", "payB"], ["EA", "EB"]][int(slot)], "both"
                own, cross, size = capacity, capacity, tok_rows
            else:
                blocks = {"1": ["E" + q], "2": ["M" + q, "O" + q], "3": ["N" + q, "Q" + q]}[slot[0]]
                mode = "one" if len(blocks) == 1 else "either"
                own, cross, size = rows, CROSS_ROWS, rows
            return (
                functools.partial(pick_kernel, experts, mode),
                [like(own, total), like(cross, total), like(own + cross, size)],
                [val[b] for b in blocks],
                [],
            )
        if name[0] == "F":
            own, cross = val["own" + name[1:]], val["Y" + name[1:]]
            weights = [gate, val["vg"], up, val["vu"], down_weight, val["vd"]]
            weights = [pltpu.with_memory_space_constraint(w, pltpu.VMEM) for w in weights]
            args = [own, cross, *weights]
            return (
                functools.partial(expert_kernel, experts),
                [like(own.shape[0], width), like(cross.shape[0], width)],
                args,
                [pltpu.VMEM((2, own.shape[0] + cross.shape[0], half), bf16)],
            )
        if name == "W":
            outs = [pltpu.VMEM(w.shape, bf16) for w in (gate, up, down_weight)]
            return fetch_kernel, outs, [], [pltpu.SemaphoreType.DMA((3,))]
        if name == "fin":
            made = [val["order"], val["pick0"], val["made0"], val["R0"]]
            made += [val[s + q] for q in "AB" for s in ("S1", "S2", "X3") if s + q in val]
            counts = [sum(s + q in val for s in ("S1", "S2", "X3")) for q in "AB"]
            parts = width // 1024
            scratch = [pltpu.VMEM((parts, tok_rows, 1024), bf16), pltpu.SemaphoreType.DMA((parts,))]
            return functools.partial(finish_kernel, counts[0]), [like(tok_rows, width)], made, scratch
        slot = name[1:] if name[1:] in slots else name[1]
        made = [val[s + slot] for s in ("pick", "made", "R")]
        made += [val[x] for x in {"D2": ["I2" + q], "D3": ["I3" + q], "D1": ["S3" + q]}.get(kind, [])]
        first = rows if slot == name[1] and q == "B" else 0
        return functools.partial(combine_kernel, first), [like(rows, width)], made, []

    def keep(name, got):
        slot = name[1:]
        if name == "prep":
            val["payA"], val["payB"], val["order"] = got
        elif name[0] == "P":
            val["own" + slot], val["cross" + slot], val["pick" + slot] = got
        elif name == "W":
            val["vg"], val["vu"], val["vd"] = got
        elif name[0] == "F":
            val["made" + slot], val["back" + slot] = got
        else:
            val[name] = got[0]

    def move_of(name):
        kind, slot, q = name[0], name[1:], name[-1]
        if kind == "Y":
            return "cross" + slot, lambda x: swapped(x, "expert", 1)
        if kind == "R":
            return "back" + slot, lambda x: swapped(x, "expert", 1)
        source, pairs = {
            "E": ("pay" + q, OUTER),
            "M": ("pay" + q, MIDDLE),
            "O": ("M" + q, OUT),
            "N": ("E" + q, MIDDLE),
            "Q": ("N" + q, OUT),
            "I2": ("C2" + q, IN),
            "S2": ("D2" + q, MIDDLE),
            "X3": ("C3" + q, ENDS),
            "I3": ("C3" + q, IN),
            "S3": (("D3" if "D3" + q in steps else "C3") + q, MIDDLE),
            "S1": ("D1" + q, OUTER),
        }[name[:-1]]
        return source, lambda x: along_line(x, pairs)

    token = jnp.zeros((8, LANES), jnp.float32)
    for name, *moves in ORDER:
        done = [m[1:] for m in moves if m[0] == "+"]
        moves = [m for m in moves if m[0] != "+"]
        sources = {m: move_of(m)[0] for m in moves}
        passed = sorted({s for s in [*sources.values(), *done] if s in val})
        if name == "f":
            _, token, through = call("fence", fence_kernel, [], idx, token, [], passes=[val[s] for s in passed])
        else:
            kernel, outs, args, scratch = kernel_of(name)
            cost = sum(x.size * x.dtype.itemsize for x in [*args, *outs]) if name[0] == "F" else 1
            through = [val[s] for s in passed]
            left = {"prep": [in_hbm(tokens)], "W": [val["wg"], val["wu"], val["wd"]]}.get(name, [])
            got, token, through = call(name, kernel, outs, idx, token, args, through, scratch, cost, left, name == "fin")
            keep(name, got)
        val.update(zip(passed, through))
        for m in moves:
            with jax.named_scope("move_" + m):
                val[m] = move_of(m)[1](val[sources[m]])
    return val["fin"]


def solution(mesh):
    body = lined if mesh.shape["expert"] == 16 else dispatched
    return jax.shard_map(
        body,
        mesh=mesh,
        in_specs=(
            P(("groups", "expert"), None),
            P(("groups", "expert"), None),
            P(("groups", "expert"), None),
            P(None, "expert"),
            P(None, "expert"),
            P(None, "expert"),
        ),
        out_specs=P(("groups", "expert"), None),
        check_vma=False,
    )
```

profile of v0, /device:TPU:0, one launch (start us, length us, event | category | flops | bytes accessed | tf_op | source)
XLA Modules:
  0.0 164.1 jit_solution(5293474508927983530)
XLA Ops:
  1.1 2.6 %prep.1 = (bf16[64,4224]{1,0:T(8,128)(2,1)S(1)}, bf16[64,4224]{1,0:T(8,128)(2,1)S(1)}, bf16[128,128]{1,0:T(8,128)(2,1)S(1)}, f32[8,128]{1,0:T(8,128)S(1)}) custom-call(s32[6]{0:T(128)S(1)} %stack.31.refs_0_, s32[4,128]{1,0:T(4,128)} %bitcast.24, f32[4,128]{1,0:T(4,128)} %bitcast.25, bf16[128,4096]{1,0:T(8,128)(2,1)} %refs_3_.1, ...), custom_call_target="tpu_custom_call", output_to_operand_aliasing={{3}: (4, {})} | custom-call | flops 1 | bytes 1 | tf_op jit(solution)/shard_map/prep/pallas_call | solution.py:256
  3.7 2.6 %collective-permute-start = (bf16[64,4224]{1,0:T(8,128)(2,1)S(1)}, bf16[64,4224]{1,0:T(8,128)(2,1)S(1)}, u32[]{:S(2)}, u32[]{:S(2)}) collective-permute-start(bf16[64,4224]{1,0:T(8,128)(2,1)S(1)} %get-tuple-element.106.refs_1_.refs_2_), channel_id=1, source_target_pairs={{0,4},{1,5},{2,6},{3,7},{4,0},{5,1},{6,2},{7,3},{8,12},{9,13},{10,... | collective-permute-start | bytes 1622024 | tf_op jit(solution)/shard_map/move_EA/ppermute | solution.py:73
  7.0 12.3 %collective-permute-done.refs_4_ = bf16[64,4224]{1,0:T(8,128)(2,1)S(1)} collective-permute-done((bf16[64,4224]{1,0:T(8,128)(2,1)S(1)}, bf16[64,4224]{1,0:T(8,128)(2,1)S(1)}, u32[]{:S(2)}, u32[]{:S(2)}) %collective-permute-start) | collective-permute-done | bytes 540704 | tf_op jit(solution)/shard_map/move_EA/ppermute | solution.py:73
  19.2 1.7 %collective-permute-start.7 = (bf16[64,4224]{1,0:T(8,128)(2,1)S(1)}, bf16[64,4224]{1,0:T(8,128)(2,1)S(1)}, u32[]{:S(2)}, u32[]{:S(2)}) collective-permute-start(bf16[64,4224]{1,0:T(8,128)(2,1)S(1)} %get-tuple-element.107.refs_2_), channel_id=1, source_target_pairs={{0,4},{1,5},{2,6},{3,7},{4,0},{5,1},{6,2},{7,3},{8,12},{9,13},{10,... | collective-permute-start | bytes 1622024 | tf_op jit(solution)/shard_map/move_EB/ppermute | solution.py:73
  24.8 1.6 collective-permute-start.1
  26.4 5.0 %W.1 = (bf16[448,4096]{1,0:T(8,128)(2,1)S(1)}, bf16[448,4096]{1,0:T(8,128)(2,1)S(1)}, bf16[896,2048]{1,0:T(8,128)(2,1)S(1)}, f32[8,128]{1,0:T(8,128)S(1)}) custom-call(s32[6]{0:T(128)S(1)} %stack.31.refs_0_, bf16[448,4096]{1,0:T(8,128)(2,1)} %get-tuple-element.113.refs_1_, ...), custom_call_target="tpu_custom_call", output_to_operand_aliasing={{3}: (4, {})} | custom-call | flops 1 | bytes 1 | tf_op jit(solution)/shard_map/W/pallas_call | solution.py:256
  32.8 1.6 collective-permute-done.7.refs_2_.refs_4_
  36.9 1.8 %collective-permute-start.11 = (bf16[64,4224]{1,0:T(8,128)(2,1)S(1)}, bf16[64,4224]{1,0:T(8,128)(2,1)S(1)}, u32[]{:S(2)}, u32[]{:S(2)}) collective-permute-start(bf16[64,4224]{1,0:T(8,128)(2,1)S(1)} %get-tuple-element.131), channel_id=1, source_target_pairs={{0,2},{1,3},{2,0},{3,1},{4,6},{5,7},{6,4},{7,5},{8,10},{9,11},{10,... | collective-permute-start | bytes 1622024 | tf_op jit(solution)/shard_map/move_Y1/ppermute | solution.py:16
  38.7 7.3 %collective-permute-done.6.refs_2_ = bf16[64,4224]{1,0:T(8,128)(2,1)S(1)} collective-permute-done((bf16[64,4224]{1,0:T(8,128)(2,1)S(1)}, bf16[64,4224]{1,0:T(8,128)(2,1)S(1)}, u32[]{:S(2)}, u32[]{:S(2)}) %collective-permute-start.6) | collective-permute-done | bytes 540704 | tf_op jit(solution)/shard_map/move_OB/ppermute | solution.py:73
  47.9 1.8 %collective-permute-start.12 = (bf16[40,4224]{1,0:T(8,128)(2,1)S(1)}, bf16[40,4224]{1,0:T(8,128)(2,1)S(1)}, u32[]{:S(2)}, u32[]{:S(2)}) collective-permute-start(bf16[40,4224]{1,0:T(8,128)(2,1)S(1)} %get-tuple-element.134), channel_id=1, source_target_pairs={{0,2},{1,3},{2,0},{3,1},{4,6},{5,7},{6,4},{7,5},{8,10},{9,11},{10,... | collective-permute-start | bytes 1013768 | tf_op jit(solution)/shard_map/move_Y2B/ppermute | solution.py:16
  49.7 6.2 %F0.1 = (bf16[64,4096]{1,0:T(8,128)(2,1)S(1)}, bf16[64,4096]{1,0:T(8,128)(2,1)S(1)}, f32[8,128]{1,0:T(8,128)S(1)}, bf16[64,4224]{1,0:T(8,128)(2,1)S(1)}) custom-call(s32[6]{0:T(128)S(1)} %stack.31.refs_0_, bf16[64,4224]{1,0:T(8,128)(2,1)S(1)} %get-tuple-element.110.refs_1_, ...), custom_call_target="tpu_custom_call", output_to_operand_aliasing={{2}: (9, {}), {3}: (10, {})} | custom-call | flops 1 | bytes 24150016 | tf_op jit(solution)/shard_map/F0/pallas_call | solution.py:256
  59.3 6.1 %F2B.1 = (bf16[64,4096]{1,0:T(8,128)(2,1)S(1)}, bf16[40,4096]{1,0:T(8,128)(2,1)S(1)}, f32[8,128]{1,0:T(8,128)S(1)}) custom-call(s32[6]{0:T(128)S(1)} %stack.31.refs_0_, bf16[64,4224]{1,0:T(8,128)(2,1)S(1)} %get-tuple-element.133.refs_1_, bf16[40,4224]{1,0:T(8,128)(2,1)S(1)} %collective-permute-done.12.refs_2_, ...), custom_call_target="tpu_custom_call", output_to_operand_aliasing={{2}: (9, {})} | custom-call | flops 1 | bytes 23750656 | tf_op jit(solution)/shard_map/F2B/pallas_call | solution.py:256
  65.4 1.3 collective-permute-done.14.refs_3_
  67.3 1.5 collective-permute-start.15
  68.7 1.3 collective-permute-start.16
  73.1 6.1 %F3A.1 = (bf16[64,4096]{1,0:T(8,128)(2,1)S(1)}, bf16[40,4096]{1,0:T(8,128)(2,1)S(1)}, f32[8,128]{1,0:T(8,128)S(1)}) custom-call(s32[6]{0:T(128)S(1)} %stack.31.refs_0_, bf16[64,4224]{1,0:T(8,128)(2,1)S(1)} %get-tuple-element.143.refs_1_, bf16[40,4224]{1,0:T(8,128)(2,1)S(1)} %get-tuple-element.144.refs_2_, ...), custom_call_target="tpu_custom_call", output_to_operand_aliasing={{2}: (9, {})} | custom-call | flops 1 | bytes 23750656 | tf_op jit(solution)/shard_map/F3A/pallas_call | solution.py:256
  80.3 5.1 %collective-permute-start.21 = (bf16[64,4096]{1,0:T(8,128)(2,1)S(1)}, bf16[64,4096]{1,0:T(8,128)(2,1)S(1)}, u32[]{:S(2)}, u32[]{:S(2)}) collective-permute-start(bf16[64,4096]{1,0:T(8,128)(2,1)S(1)} %get-tuple-element.165), channel_id=1, source_target_pairs={{0,4},{1,5},{2,6},{3,7},{12,8},{13,9},{14,10},{15,11},{16,20},{17,... | collective-permute-start | bytes 1572872 | tf_op jit(solution)/shard_map/move_I2B/ppermute | solution.py:73
  86.7 1.8 %collective-permute-start.20 = (bf16[40,4224]{1,0:T(8,128)(2,1)S(1)}, bf16[40,4224]{1,0:T(8,128)(2,1)S(1)}, u32[]{:S(2)}, u32[]{:S(2)}) collective-permute-start(bf16[40,4224]{1,0:T(8,128)(2,1)S(1)} %get-tuple-element.163), channel_id=1, source_target_pairs={{0,2},{1,3},{2,0},{3,1},{4,6},{5,7},{6,4},{7,5},{8,10},{9,11},{10,... | collective-permute-start | bytes 1013768 | tf_op jit(solution)/shard_map/move_Y3B/ppermute | solution.py:16
  88.5 6.2 %F1.1 = (bf16[64,4096]{1,0:T(8,128)(2,1)S(1)}, bf16[64,4096]{1,0:T(8,128)(2,1)S(1)}, f32[8,128]{1,0:T(8,128)S(1)}, bf16[40,4096]{1,0:T(8,128)(2,1)S(1)}) custom-call(s32[6]{0:T(128)S(1)} %stack.31.refs_0_, bf16[64,4224]{1,0:T(8,128)(2,1)S(1)} %get-tuple-element.128.refs_1_, ...), custom_call_target="tpu_custom_call", output_to_operand_aliasing={{2}: (9, {}), {3}: (10, {})} | custom-call | flops 1 | bytes 24150016 | tf_op jit(solution)/shard_map/F1/pallas_call | solution.py:256
  95.6 6.1 %F3B.1 = (bf16[64,4096]{1,0:T(8,128)(2,1)S(1)}, bf16[40,4096]{1,0:T(8,128)(2,1)S(1)}, f32[8,128]{1,0:T(8,128)S(1)}, bf16[64,4096]{1,0:T(8,128)(2,1)S(1)}) custom-call(s32[6]{0:T(128)S(1)} %stack.31.refs_0_, bf16[64,4224]{1,0:T(8,128)(2,1)S(1)} %get-tuple-element.162.refs_1_, ...), custom_call_target="tpu_custom_call", output_to_operand_aliasing={{2}: (9, {}), {3}: (10, {})} | custom-call | flops 1 | bytes 23750656 | tf_op jit(solution)/shard_map/F3B/pallas_call | solution.py:256
  102.5 2.5 %collective-permute-start.22 = (bf16[40,4096]{1,0:T(8,128)(2,1)S(1)}, bf16[40,4096]{1,0:T(8,128)(2,1)S(1)}, u32[]{:S(2)}, u32[]{:S(2)}) collective-permute-start(bf16[40,4096]{1,0:T(8,128)(2,1)S(1)} %get-tuple-element.175), channel_id=1, source_target_pairs={{0,2},{1,3},{2,0},{3,1},{4,6},{5,7},{6,4},{7,5},{8,10},{9,11},{10,... | collective-permute-start | bytes 983048 | tf_op jit(solution)/shard_map/move_R3B/ppermute | solution.py:16
  106.0 2.2 %collective-permute-start.24 = (bf16[64,4096]{1,0:T(8,128)(2,1)S(1)}, bf16[64,4096]{1,0:T(8,128)(2,1)S(1)}, u32[]{:S(2)}, u32[]{:S(2)}) collective-permute-start(bf16[64,4096]{1,0:T(8,128)(2,1)S(1)} %get-tuple-element.180), channel_id=1, source_target_pairs={{0,4},{1,5},{2,6},{3,7},{12,8},{13,9},{14,10},{15,11},{16,20},{17,... | collective-permute-start | bytes 1572872 | tf_op jit(solution)/shard_map/move_I3A/ppermute | solution.py:73
  109.1 6.1 %F2A.1 = (bf16[64,4096]{1,0:T(8,128)(2,1)S(1)}, bf16[40,4096]{1,0:T(8,128)(2,1)S(1)}, f32[8,128]{1,0:T(8,128)S(1)}) custom-call(s32[6]{0:T(128)S(1)} %stack.31.refs_0_, bf16[64,4224]{1,0:T(8,128)(2,1)S(1)} %get-tuple-element.157.refs_1_, bf16[40,4224]{1,0:T(8,128)(2,1)S(1)} %get-tuple-element.158.refs_2_, ...), custom_call_target="tpu_custom_call", output_to_operand_aliasing={{2}: (9, {})} | custom-call | flops 1 | bytes 23750656 | tf_op jit(solution)/shard_map/F2A/pallas_call | solution.py:256
  116.1 4.1 %collective-permute-start.28 = (bf16[64,4096]{1,0:T(8,128)(2,1)S(1)}, bf16[64,4096]{1,0:T(8,128)(2,1)S(1)}, u32[]{:S(2)}, u32[]{:S(2)}) collective-permute-start(bf16[64,4096]{1,0:T(8,128)(2,1)S(1)} %get-tuple-element.187), channel_id=1, source_target_pairs={{0,4},{1,5},{2,6},{3,7},{12,8},{13,9},{14,10},{15,11},{16,20},{17,... | collective-permute-start | bytes 1572872 | tf_op jit(solution)/shard_map/move_I3B/ppermute | solution.py:73
  121.9 8.2 %collective-permute-done.23.refs_3_.refs_6_ = bf16[40,4096]{1,0:T(8,128)(2,1)S(1)} collective-permute-done((bf16[40,4096]{1,0:T(8,128)(2,1)S(1)}, bf16[40,4096]{1,0:T(8,128)(2,1)S(1)}, u32[]{:S(2)}, u32[]{:S(2)}) %collective-permute-start.23) | collective-permute-done | bytes 327712 | tf_op jit(solution)/shard_map/move_R2A/ppermute | solution.py:16
  131.1 1.3 collective-permute-start.31
  134.0 9.9 %collective-permute-done.26.refs_3_.refs_6_ = bf16[64,4096]{1,0:T(8,128)(2,1)S(1)} collective-permute-done((bf16[64,4096]{1,0:T(8,128)(2,1)S(1)}, bf16[64,4096]{1,0:T(8,128)(2,1)S(1)}, u32[]{:S(2)}, u32[]{:S(2)}) %collective-permute-start.26) | collective-permute-done | bytes 524320 | tf_op jit(solution)/shard_map/move_R1/ppermute | solution.py:16
  147.7 4.0 %collective-permute-start.34 = (bf16[64,4096]{1,0:T(8,128)(2,1)S(1)}, bf16[64,4096]{1,0:T(8,128)(2,1)S(1)}, u32[]{:S(2)}, u32[]{:S(2)}) collective-permute-start(bf16[64,4096]{1,0:T(8,128)(2,1)S(1)} %get-tuple-element.201), channel_id=1, source_target_pairs={{0,4},{1,5},{2,6},{3,7},{4,0},{5,1},{6,2},{7,3},{8,12},{9,13},{10,... | collective-permute-start | bytes 1572872 | tf_op jit(solution)/shard_map/move_S1B/ppermute | solution.py:73
  151.7 2.5 %collective-permute-done.29.refs_4_ = bf16[64,4096]{1,0:T(8,128)(2,1)S(1)} collective-permute-done((bf16[64,4096]{1,0:T(8,128)(2,1)S(1)}, bf16[64,4096]{1,0:T(8,128)(2,1)S(1)}, u32[]{:S(2)}, u32[]{:S(2)}) %collective-permute-start.29) | collective-permute-done | bytes 524320 | tf_op jit(solution)/shard_map/move_R0/ppermute | solution.py:16
  154.1 1.8 %collective-permute-done.30.refs_5_ = bf16[64,4096]{1,0:T(8,128)(2,1)S(1)} collective-permute-done((bf16[64,4096]{1,0:T(8,128)(2,1)S(1)}, bf16[64,4096]{1,0:T(8,128)(2,1)S(1)}, u32[]{:S(2)}, u32[]{:S(2)}) %collective-permute-start.30) | collective-permute-done | bytes 524320 | tf_op jit(solution)/shard_map/move_S1A/ppermute | solution.py:73
  155.9 5.6 %collective-permute-done.34.refs_7_ = bf16[64,4096]{1,0:T(8,128)(2,1)S(1)} collective-permute-done((bf16[64,4096]{1,0:T(8,128)(2,1)S(1)}, bf16[64,4096]{1,0:T(8,128)(2,1)S(1)}, u32[]{:S(2)}, u32[]{:S(2)}) %collective-permute-start.34) | collective-permute-done | bytes 524320 | tf_op jit(solution)/shard_map/move_S1B/ppermute | solution.py:73
  161.5 2.4 %fin.1 = (bf16[128,4096]{1,0:T(8,128)(2,1)}, f32[8,128]{1,0:T(8,128)S(1)}) custom-call(s32[6]{0:T(128)S(1)} %stack.31.refs_0_, bf16[128,128]{1,0:T(8,128)(2,1)S(1)} %get-tuple-element.105.refs_1_, bf16[128,128]{1,0:T(8,128)(2,1)S(1)} %get-tuple-element.109.refs_2_, bf16[64,4096]{1,0:T(8,128)(2,1)S(1)} %get-tuple-element.126.refs_3_, ...), custom_call_target="tpu_custom_call", output_to_operand_aliasing={{1}: (9, {})} | custom-call | flops 1 | bytes 1 | tf_op jit(solution)/shard_map/fin/pallas_call | solution.py:256
  (75 shorter events, 32.8 us)
Async XLA Ops:
  0.0 22.9 %collective-permute-start.3 = (bf16[448,4096]{1,0:T(8,128)(2,1)}, bf16[448,4096]{1,0:T(8,128)(2,1)}, u32[]{:S(2)}, u32[]{:S(2)}) collective-permute-start(bf16[448,4096]{1,0:T(8,128)(2,1)} %bitcast.10), channel_id=1, source_target_pairs={{0,1},{1,0},{2,3},{3,2},{4,5},{5,4},{6,7},{7,6},{8,9},{9,8},{10,11... | collective-permute-start | bytes 11010056 | tf_op jit(solution)/shard_map/move_wg/ppermute | solution.py:16
  0.5 22.5 %collective-permute-start.4 = (bf16[448,4096]{1,0:T(8,128)(2,1)}, bf16[448,4096]{1,0:T(8,128)(2,1)}, u32[]{:S(2)}, u32[]{:S(2)}) collective-permute-start(bf16[448,4096]{1,0:T(8,128)(2,1)} %bitcast.17), channel_id=1, source_target_pairs={{0,1},{1,0},{2,3},{3,2},{4,5},{5,4},{6,7},{7,6},{8,9},{9,8},{10,11... | collective-permute-start | bytes 11010056 | tf_op jit(solution)/shard_map/move_wu/ppermute | solution.py:16
  0.5 25.9 %collective-permute-start.5 = (bf16[896,2048]{1,0:T(8,128)(2,1)}, bf16[896,2048]{1,0:T(8,128)(2,1)}, u32[]{:S(2)}, u32[]{:S(2)}) collective-permute-start(bf16[896,2048]{1,0:T(8,128)(2,1)} %refs_7_.11), channel_id=1, source_target_pairs={{0,1},{1,0},{2,3},{3,2},{4,5},{5,4},{6,7},{7,6},{8,9},{9,8},{10,11... | collective-permute-start | bytes 11010056 | tf_op jit(solution)/shard_map/move_wd/ppermute | solution.py:16
  3.7 15.6 %collective-permute-start = (bf16[64,4224]{1,0:T(8,128)(2,1)S(1)}, bf16[64,4224]{1,0:T(8,128)(2,1)S(1)}, u32[]{:S(2)}, u32[]{:S(2)}) collective-permute-start(bf16[64,4224]{1,0:T(8,128)(2,1)S(1)} %get-tuple-element.106.refs_1_.refs_2_), channel_id=1, source_target_pairs={{0,4},{1,5},{2,6},{3,7},{4,0},{5,1},{6,2},{7,3},{8,12},{9,13},{10,... | collective-permute-start | bytes 1622024 | tf_op jit(solution)/shard_map/move_EA/ppermute | solution.py:73
  6.3 15.9 %collective-permute-start.2 = (bf16[64,4224]{1,0:T(8,128)(2,1)S(1)}, bf16[64,4224]{1,0:T(8,128)(2,1)S(1)}, u32[]{:S(2)}, u32[]{:S(2)}) collective-permute-start(bf16[64,4224]{1,0:T(8,128)(2,1)S(1)} %get-tuple-element.107.refs_2_), channel_id=1, source_target_pairs={{4,8},{5,9},{6,10},{7,11},{8,4},{9,5},{10,6},{11,7},{20,24},{21,25... | collective-permute-start | bytes 1622024 | tf_op jit(solution)/shard_map/move_MB/ppermute | solution.py:73
  19.2 15.2 %collective-permute-start.7 = (bf16[64,4224]{1,0:T(8,128)(2,1)S(1)}, bf16[64,4224]{1,0:T(8,128)(2,1)S(1)}, u32[]{:S(2)}, u32[]{:S(2)}) collective-permute-start(bf16[64,4224]{1,0:T(8,128)(2,1)S(1)} %get-tuple-element.107.refs_2_), channel_id=1, source_target_pairs={{0,4},{1,5},{2,6},{3,7},{4,0},{5,1},{6,2},{7,3},{8,12},{9,13},{10,... | collective-permute-start | bytes 1622024 | tf_op jit(solution)/shard_map/move_EB/ppermute | solution.py:73
  22.2 12.2 %collective-permute-start.8 = (bf16[64,4224]{1,0:T(8,128)(2,1)S(1)}, bf16[64,4224]{1,0:T(8,128)(2,1)S(1)}, u32[]{:S(2)}, u32[]{:S(2)}) collective-permute-start(bf16[64,4224]{1,0:T(8,128)(2,1)S(1)} %get-tuple-element.120.refs_1_), channel_id=1, source_target_pairs={{4,8},{5,9},{6,10},{7,11},{8,4},{9,5},{10,6},{11,7},{20,24},{21,25... | collective-permute-start | bytes 1622024 | tf_op jit(solution)/shard_map/move_NA/ppermute | solution.py:73
  23.5 22.5 %collective-permute-start.6 = (bf16[64,4224]{1,0:T(8,128)(2,1)S(1)}, bf16[64,4224]{1,0:T(8,128)(2,1)S(1)}, u32[]{:S(2)}, u32[]{:S(2)}) collective-permute-start(bf16[64,4224]{1,0:T(8,128)(2,1)S(1)} %get-tuple-element.119.refs_1_), channel_id=1, source_target_pairs={{4,0},{5,1},{6,2},{7,3},{8,12},{9,13},{10,14},{11,15},{20,16},{21,... | collective-permute-start | bytes 1622024 | tf_op jit(solution)/shard_map/move_OB/ppermute | solution.py:73
  24.8 23.1 %collective-permute-start.1 = (bf16[64,4224]{1,0:T(8,128)(2,1)S(1)}, bf16[64,4224]{1,0:T(8,128)(2,1)S(1)}, u32[]{:S(2)}, u32[]{:S(2)}) collective-permute-start(bf16[64,4224]{1,0:T(8,128)(2,1)S(1)} %get-tuple-element.111), channel_id=1, source_target_pairs={{0,2},{1,3},{2,0},{3,1},{4,6},{5,7},{6,4},{7,5},{8,10},{9,11},{10,... | collective-permute-start | bytes 1622024 | tf_op jit(solution)/shard_map/move_Y0/ppermute | solution.py:16
  32.0 17.7 %collective-permute-start.9 = (bf16[64,4224]{1,0:T(8,128)(2,1)S(1)}, bf16[64,4224]{1,0:T(8,128)(2,1)S(1)}, u32[]{:S(2)}, u32[]{:S(2)}) collective-permute-start(bf16[64,4224]{1,0:T(8,128)(2,1)S(1)} %get-tuple-element.125), channel_id=1, source_target_pairs={{4,8},{5,9},{6,10},{7,11},{8,4},{9,5},{10,6},{11,7},{20,24},{21,25... | collective-permute-start | bytes 1622024 | tf_op jit(solution)/shard_map/move_MA/ppermute | solution.py:73
  35.6 21.6 %collective-permute-start.10 = (bf16[64,4224]{1,0:T(8,128)(2,1)S(1)}, bf16[64,4224]{1,0:T(8,128)(2,1)S(1)}, u32[]{:S(2)}, u32[]{:S(2)}) collective-permute-start(bf16[64,4224]{1,0:T(8,128)(2,1)S(1)} %get-tuple-element.129.refs_1_), channel_id=1, source_target_pairs={{4,0},{5,1},{6,2},{7,3},{8,12},{9,13},{10,14},{11,15},{20,16},{21,... | collective-permute-start | bytes 1622024 | tf_op jit(solution)/shard_map/move_QA/ppermute | solution.py:73
  36.9 20.3 %collective-permute-start.11 = (bf16[64,4224]{1,0:T(8,128)(2,1)S(1)}, bf16[64,4224]{1,0:T(8,128)(2,1)S(1)}, u32[]{:S(2)}, u32[]{:S(2)}) collective-permute-start(bf16[64,4224]{1,0:T(8,128)(2,1)S(1)} %get-tuple-element.131), channel_id=1, source_target_pairs={{0,2},{1,3},{2,0},{3,1},{4,6},{5,7},{6,4},{7,5},{8,10},{9,11},{10,... | collective-permute-start | bytes 1622024 | tf_op jit(solution)/shard_map/move_Y1/ppermute | solution.py:16
  47.2 19.5 %collective-permute-start.13 = (bf16[64,4224]{1,0:T(8,128)(2,1)S(1)}, bf16[64,4224]{1,0:T(8,128)(2,1)S(1)}, u32[]{:S(2)}, u32[]{:S(2)}) collective-permute-start(bf16[64,4224]{1,0:T(8,128)(2,1)S(1)} %get-tuple-element.137), channel_id=1, source_target_pairs={{4,8},{5,9},{6,10},{7,11},{8,4},{9,5},{10,6},{11,7},{20,24},{21,25... | collective-permute-start | bytes 1622024 | tf_op jit(solution)/shard_map/move_NB/ppermute | solution.py:73
  47.9 11.4 %collective-permute-start.12 = (bf16[40,4224]{1,0:T(8,128)(2,1)S(1)}, bf16[40,4224]{1,0:T(8,128)(2,1)S(1)}, u32[]{:S(2)}, u32[]{:S(2)}) collective-permute-start(bf16[40,4224]{1,0:T(8,128)(2,1)S(1)} %get-tuple-element.134), channel_id=1, source_target_pairs={{0,2},{1,3},{2,0},{3,1},{4,6},{5,7},{6,4},{7,5},{8,10},{9,11},{10,... | collective-permute-start | bytes 1013768 | tf_op jit(solution)/shard_map/move_Y2B/ppermute | solution.py:16
  55.9 14.8 %collective-permute-start.17 = (bf16[64,4224]{1,0:T(8,128)(2,1)S(1)}, bf16[64,4224]{1,0:T(8,128)(2,1)S(1)}, u32[]{:S(2)}, u32[]{:S(2)}) collective-permute-start(bf16[64,4224]{1,0:T(8,128)(2,1)S(1)} %get-tuple-element.145.refs_1_), channel_id=1, source_target_pairs={{4,0},{5,1},{6,2},{7,3},{8,12},{9,13},{10,14},{11,15},{20,16},{21,... | collective-permute-start | bytes 1622024 | tf_op jit(solution)/shard_map/move_OA/ppermute | solution.py:73
  67.3 18.2 %collective-permute-start.15 = (bf16[64,4224]{1,0:T(8,128)(2,1)S(1)}, bf16[64,4224]{1,0:T(8,128)(2,1)S(1)}, u32[]{:S(2)}, u32[]{:S(2)}) collective-permute-start(bf16[64,4224]{1,0:T(8,128)(2,1)S(1)} %get-tuple-element.139.refs_1_), channel_id=1, source_target_pairs={{4,0},{5,1},{6,2},{7,3},{8,12},{9,13},{10,14},{11,15},{20,16},{21,... | collective-permute-start | bytes 1622024 | tf_op jit(solution)/shard_map/move_QB/ppermute | solution.py:73
  68.7 10.7 %collective-permute-start.16 = (bf16[40,4096]{1,0:T(8,128)(2,1)S(1)}, bf16[40,4096]{1,0:T(8,128)(2,1)S(1)}, u32[]{:S(2)}, u32[]{:S(2)}) collective-permute-start(bf16[40,4096]{1,0:T(8,128)(2,1)S(1)} %get-tuple-element.142), channel_id=1, source_target_pairs={{0,2},{1,3},{2,0},{3,1},{4,6},{5,7},{6,4},{7,5},{8,10},{9,11},{10,... | collective-permute-start | bytes 983048 | tf_op jit(solution)/shard_map/move_R2B/ppermute | solution.py:16
  72.5 13.0 %collective-permute-start.18 = (bf16[40,4224]{1,0:T(8,128)(2,1)S(1)}, bf16[40,4224]{1,0:T(8,128)(2,1)S(1)}, u32[]{:S(2)}, u32[]{:S(2)}) collective-permute-start(bf16[40,4224]{1,0:T(8,128)(2,1)S(1)} %get-tuple-element.152), channel_id=1, source_target_pairs={{0,2},{1,3},{2,0},{3,1},{4,6},{5,7},{6,4},{7,5},{8,10},{9,11},{10,... | collective-permute-start | bytes 1013768 | tf_op jit(solution)/shard_map/move_Y2A/ppermute | solution.py:16
  80.3 14.8 %collective-permute-start.21 = (bf16[64,4096]{1,0:T(8,128)(2,1)S(1)}, bf16[64,4096]{1,0:T(8,128)(2,1)S(1)}, u32[]{:S(2)}, u32[]{:S(2)}) collective-permute-start(bf16[64,4096]{1,0:T(8,128)(2,1)S(1)} %get-tuple-element.165), channel_id=1, source_target_pairs={{0,4},{1,5},{2,6},{3,7},{12,8},{13,9},{14,10},{15,11},{16,20},{17,... | collective-permute-start | bytes 1572872 | tf_op jit(solution)/shard_map/move_I2B/ppermute | solution.py:73
  94.8 10.3 %collective-permute-start.19 = (bf16[40,4096]{1,0:T(8,128)(2,1)S(1)}, bf16[40,4096]{1,0:T(8,128)(2,1)S(1)}, u32[]{:S(2)}, u32[]{:S(2)}) collective-permute-start(bf16[40,4096]{1,0:T(8,128)(2,1)S(1)} %get-tuple-element.161), channel_id=1, source_target_pairs={{0,2},{1,3},{2,0},{3,1},{4,6},{5,7},{6,4},{7,5},{8,10},{9,11},{10,... | collective-permute-start | bytes 983048 | tf_op jit(solution)/shard_map/move_R3A/ppermute | solution.py:16
  102.5 12.7 %collective-permute-start.22 = (bf16[40,4096]{1,0:T(8,128)(2,1)S(1)}, bf16[40,4096]{1,0:T(8,128)(2,1)S(1)}, u32[]{:S(2)}, u32[]{:S(2)}) collective-permute-start(bf16[40,4096]{1,0:T(8,128)(2,1)S(1)} %get-tuple-element.175), channel_id=1, source_target_pairs={{0,2},{1,3},{2,0},{3,1},{4,6},{5,7},{6,4},{7,5},{8,10},{9,11},{10,... | collective-permute-start | bytes 983048 | tf_op jit(solution)/shard_map/move_R3B/ppermute | solution.py:16
  106.0 14.4 %collective-permute-start.24 = (bf16[64,4096]{1,0:T(8,128)(2,1)S(1)}, bf16[64,4096]{1,0:T(8,128)(2,1)S(1)}, u32[]{:S(2)}, u32[]{:S(2)}) collective-permute-start(bf16[64,4096]{1,0:T(8,128)(2,1)S(1)} %get-tuple-element.180), channel_id=1, source_target_pairs={{0,4},{1,5},{2,6},{3,7},{12,8},{13,9},{14,10},{15,11},{16,20},{17,... | collective-permute-start | bytes 1572872 | tf_op jit(solution)/shard_map/move_I3A/ppermute | solution.py:73
  108.2 13.7 %collective-permute-start.25 = (bf16[64,4096]{1,0:T(8,128)(2,1)S(1)}, bf16[64,4096]{1,0:T(8,128)(2,1)S(1)}, u32[]{:S(2)}, u32[]{:S(2)}) collective-permute-start(bf16[64,4096]{1,0:T(8,128)(2,1)S(1)} %get-tuple-element.183), channel_id=1, source_target_pairs={{4,8},{5,9},{6,10},{7,11},{8,4},{9,5},{10,6},{11,7},{20,24},{21,25... | collective-permute-start | bytes 1572872 | tf_op jit(solution)/shard_map/move_S2B/ppermute | solution.py:73
  116.1 16.2 %collective-permute-start.28 = (bf16[64,4096]{1,0:T(8,128)(2,1)S(1)}, bf16[64,4096]{1,0:T(8,128)(2,1)S(1)}, u32[]{:S(2)}, u32[]{:S(2)}) collective-permute-start(bf16[64,4096]{1,0:T(8,128)(2,1)S(1)} %get-tuple-element.187), channel_id=1, source_target_pairs={{0,4},{1,5},{2,6},{3,7},{12,8},{13,9},{14,10},{15,11},{16,20},{17,... | collective-permute-start | bytes 1572872 | tf_op jit(solution)/shard_map/move_I3B/ppermute | solution.py:73
  120.3 9.9 %collective-permute-start.23 = (bf16[40,4096]{1,0:T(8,128)(2,1)S(1)}, bf16[40,4096]{1,0:T(8,128)(2,1)S(1)}, u32[]{:S(2)}, u32[]{:S(2)}) collective-permute-start(bf16[40,4096]{1,0:T(8,128)(2,1)S(1)} %get-tuple-element.178), channel_id=1, source_target_pairs={{0,2},{1,3},{2,0},{3,1},{4,6},{5,7},{6,4},{7,5},{8,10},{9,11},{10,... | collective-permute-start | bytes 983048 | tf_op jit(solution)/shard_map/move_R2A/ppermute | solution.py:16
  121.2 12.8 %collective-permute-start.27 = (bf16[64,4096]{1,0:T(8,128)(2,1)S(1)}, bf16[64,4096]{1,0:T(8,128)(2,1)S(1)}, u32[]{:S(2)}, u32[]{:S(2)}) collective-permute-start(bf16[64,4096]{1,0:T(8,128)(2,1)S(1)} %get-tuple-element.186), channel_id=1, source_target_pairs={{4,8},{5,9},{6,10},{7,11},{8,4},{9,5},{10,6},{11,7},{20,24},{21,25... | collective-permute-start | bytes 1572872 | tf_op jit(solution)/shard_map/move_S3A/ppermute | solution.py:73
  131.0 12.9 %collective-permute-start.26 = (bf16[64,4096]{1,0:T(8,128)(2,1)S(1)}, bf16[64,4096]{1,0:T(8,128)(2,1)S(1)}, u32[]{:S(2)}, u32[]{:S(2)}) collective-permute-start(bf16[64,4096]{1,0:T(8,128)(2,1)S(1)} %get-tuple-element.185), channel_id=1, source_target_pairs={{0,2},{1,3},{2,0},{3,1},{4,6},{5,7},{6,4},{7,5},{8,10},{9,11},{10,... | collective-permute-start | bytes 1572872 | tf_op jit(solution)/shard_map/move_R1/ppermute | solution.py:16
  131.1 14.0 %collective-permute-start.31 = (bf16[64,4096]{1,0:T(8,128)(2,1)S(1)}, bf16[64,4096]{1,0:T(8,128)(2,1)S(1)}, u32[]{:S(2)}, u32[]{:S(2)}) collective-permute-start(bf16[64,4096]{1,0:T(8,128)(2,1)S(1)} %get-tuple-element.194), channel_id=1, source_target_pairs={{0,4},{1,5},{2,6},{3,7},{12,8},{13,9},{14,10},{15,11},{16,20},{17,... | collective-permute-start | bytes 1572872 | tf_op jit(solution)/shard_map/move_I2A/ppermute | solution.py:73
  133.3 12.6 %collective-permute-start.32 = (bf16[64,4096]{1,0:T(8,128)(2,1)S(1)}, bf16[64,4096]{1,0:T(8,128)(2,1)S(1)}, u32[]{:S(2)}, u32[]{:S(2)}) collective-permute-start(bf16[64,4096]{1,0:T(8,128)(2,1)S(1)} %get-tuple-element.197), channel_id=1, source_target_pairs={{4,8},{5,9},{6,10},{7,11},{8,4},{9,5},{10,6},{11,7},{20,24},{21,25... | collective-permute-start | bytes 1572872 | tf_op jit(solution)/shard_map/move_S3B/ppermute | solution.py:73
  144.9 9.2 %collective-permute-start.29 = (bf16[64,4096]{1,0:T(8,128)(2,1)S(1)}, bf16[64,4096]{1,0:T(8,128)(2,1)S(1)}, u32[]{:S(2)}, u32[]{:S(2)}) collective-permute-start(bf16[64,4096]{1,0:T(8,128)(2,1)S(1)} %get-tuple-element.191), channel_id=1, source_target_pairs={{0,2},{1,3},{2,0},{3,1},{4,6},{5,7},{6,4},{7,5},{8,10},{9,11},{10,... | collective-permute-start | bytes 1572872 | tf_op jit(solution)/shard_map/move_R0/ppermute | solution.py:16
  145.0 10.9 %collective-permute-start.30 = (bf16[64,4096]{1,0:T(8,128)(2,1)S(1)}, bf16[64,4096]{1,0:T(8,128)(2,1)S(1)}, u32[]{:S(2)}, u32[]{:S(2)}) collective-permute-start(bf16[64,4096]{1,0:T(8,128)(2,1)S(1)} %get-tuple-element.192), channel_id=1, source_target_pairs={{0,4},{1,5},{2,6},{3,7},{4,0},{5,1},{6,2},{7,3},{8,12},{9,13},{10,... | collective-permute-start | bytes 1572872 | tf_op jit(solution)/shard_map/move_S1A/ppermute | solution.py:73
  147.7 13.9 %collective-permute-start.34 = (bf16[64,4096]{1,0:T(8,128)(2,1)S(1)}, bf16[64,4096]{1,0:T(8,128)(2,1)S(1)}, u32[]{:S(2)}, u32[]{:S(2)}) collective-permute-start(bf16[64,4096]{1,0:T(8,128)(2,1)S(1)} %get-tuple-element.201), channel_id=1, source_target_pairs={{0,4},{1,5},{2,6},{3,7},{4,0},{5,1},{6,2},{7,3},{8,12},{9,13},{10,... | collective-permute-start | bytes 1572872 | tf_op jit(solution)/shard_map/move_S1B/ppermute | solution.py:73
  (6 other events, 90.9 us)
where the time goes:
time: 165 us; the launch traced here: 164 us
  Pallas kernels  65.4 us (40%)
  waiting for transfers between devices  51.7 us (31%)
  starting transfers between devices  46.2 us (28%)
    pallas_call x29, Pallas kernels, call(): pl.pallas_call(body, out_shape=[*outs, *(jax.ShapeDtypeStruct(x.shape, x....  65.4 us
    ppermute x20, starting transfers between devices, along_line(): return lax.ppermute(x, 'expert', moves)  32.5 us
    ppermute x20, waiting for transfers between devices, along_line(): return lax.ppermute(x, 'expert', moves)  29.2 us
    ppermute x15, waiting for transfers between devices, swapped(): lax.ppermute(x, axis, [(i, i ^ 1 << apart) for i in range(lax.axis_size(a...  22.6 us
    ppermute x15, starting transfers between devices, swapped(): lax.ppermute(x, axis, [(i, i ^ 1 << apart) for i in range(lax.axis_size(a...  13.7 us
  transfers between devices with their start and end apart: 35, of which 12 were waited for; matrix products, arithmetic and copies ran while one was open for 0% of the time, Pallas kernels for 38%

commit v1 on v0

--- a/solution.py
+++ b/solution.py
@@ -182,11 +182,14 @@
     half = ga.shape[0]
     x = jnp.concatenate([own[:, :width], cross[:, :width]], 0)
     ext = jnp.concatenate([own[:, width:], cross[:, width:]], 0)
-    scale = scale_of(ext, expert, experts)
+    lane = iota((8, LANES), 1)
+    mine = ((lane % experts == expert) & (lane < 3 * experts)).astype(jnp.bfloat16)
+    scale = contract(mine, ext, 1, 1)[:1]
     for place, g, u in ((core, ga, ua), (1 - core, gb, ub)):
-        gate = contract(x, g[...], 1, 1)
-        upval = contract(x, u[...], 1, 1)
-        hidden[place] = (gate / (1.0 + jnp.exp(-gate)) * upval * scale).astype(jnp.bfloat16)
+        gate = contract(g[...], x, 1, 1)
+        upval = contract(u[...], x, 1, 1)
+        made = gate / (1.0 + jnp.exp(-gate)) * upval * scale
+        hidden[place] = made.T.astype(jnp.bfloat16)
     step = 512
     cols = da.shape[1]
     for n in range(0, 2 * cols, step):
@@ -276,8 +279,8 @@
     ["f", "OB", "+wg", "+wu"],
     ["W"],
     ["f", "MA"],
-    ["P1", "Y1", "QA"],
-    ["P2B", "Y2B", "NB"],
+    ["P1", "Y1"],
+    ["P2B", "QA", "Y2B", "NB"],
     ["F0", "OA"],
     ["P3A", "Y3A", "+Y1"],
     ["F2B", "R2B"],

time: 165 us -> 169 us (1.024)
  starting transfers between devices: 46.2 us -> 51.7 us
  Pallas kernels: 65.4 us -> 63.4 us
    ppermute x20, waiting for transfers between devices: 29.2 us -> 35.9 us  [along_line(): return lax.ppermute(x, 'expert', moves)]
    ppermute x15, waiting for transfers between devices: 22.6 us -> 16.8 us  [swapped(): lax.ppermute(x, axis, [(i, i ^ 1 << apart) for i in range(lax.axis_size(a...]
    ppermute x20, starting transfers between devices: 32.5 us -> 36.6 us  [along_line(): return lax.ppermute(x, 'expert', moves)]
    pallas_call x29, Pallas kernels: 65.4 us -> 63.4 us  [call(): pl.pallas_call(body, out_shape=[*outs, *(jax.ShapeDtypeStruct(x.shape, x....]
  transfers between devices with their start and end apart: 35 -> 35, of which waited for: 12 -> 12; matrix products, arithmetic and copies ran while one was open for 0% -> 0% of each run, Pallas kernels for 38% -> 36%
where the time goes in v1:
time: 169 us
  Pallas kernels  63.4 us (38%)
  waiting for transfers between devices  52.7 us (31%)
  starting transfers between devices  51.7 us (31%)
    pallas_call x29, Pallas kernels, call(): pl.pallas_call(body, out_shape=[*outs, *(jax.ShapeDtypeStruct(x.shape, x....  63.4 us
    ppermute x20, starting transfers between devices, along_line(): return lax.ppermute(x, 'expert', moves)  36.6 us
    ppermute x20, waiting for transfers between devices, along_line(): return lax.ppermute(x, 'expert', moves)  35.9 us
    ppermute x15, waiting for transfers between devices, swapped(): lax.ppermute(x, axis, [(i, i ^ 1 << apart) for i in range(lax.axis_size(a...  16.8 us
    ppermute x15, starting transfers between devices, swapped(): lax.ppermute(x, axis, [(i, i ^ 1 << apart) for i in range(lax.axis_size(a...  15.1 us
  transfers between devices with their start and end apart: 35, of which 12 were waited for; matrix products, arithmetic and copies ran while one was open for 0% of the time, Pallas kernels for 36%

profile of v1, /device:TPU:0, one launch (start us, length us, event | category | flops | bytes accessed | tf_op | source)
XLA Modules:
  0.0 168.5 jit_solution(8026508344424587549)
XLA Ops:
  1.1 2.6 %prep.1 = (bf16[64,4224]{1,0:T(8,128)(2,1)S(1)}, bf16[64,4224]{1,0:T(8,128)(2,1)S(1)}, bf16[128,128]{1,0:T(8,128)(2,1)S(1)}, f32[8,128]{1,0:T(8,128)S(1)}) custom-call(s32[6]{0:T(128)S(1)} %stack.31.refs_0_, s32[4,128]{1,0:T(4,128)} %bitcast.24, f32[4,128]{1,0:T(4,128)} %bitcast.25, bf16[128,4096]{1,0:T(8,128)(2,1)} %refs_3_.1, ...), custom_call_target="tpu_custom_call", output_to_operand_aliasing={{3}: (4, {})} | custom-call | flops 1 | bytes 1 | tf_op jit(solution)/shard_map/prep/pallas_call | solution.py:259
  3.7 2.6 %collective-permute-start = (bf16[64,4224]{1,0:T(8,128)(2,1)S(1)}, bf16[64,4224]{1,0:T(8,128)(2,1)S(1)}, u32[]{:S(2)}, u32[]{:S(2)}) collective-permute-start(bf16[64,4224]{1,0:T(8,128)(2,1)S(1)} %get-tuple-element.106.refs_1_.refs_2_), channel_id=1, source_target_pairs={{0,4},{1,5},{2,6},{3,7},{4,0},{5,1},{6,2},{7,3},{8,12},{9,13},{10,... | collective-permute-start | bytes 1622024 | tf_op jit(solution)/shard_map/move_EA/ppermute | solution.py:73
  7.0 12.3 %collective-permute-done.refs_4_ = bf16[64,4224]{1,0:T(8,128)(2,1)S(1)} collective-permute-done((bf16[64,4224]{1,0:T(8,128)(2,1)S(1)}, bf16[64,4224]{1,0:T(8,128)(2,1)S(1)}, u32[]{:S(2)}, u32[]{:S(2)}) %collective-permute-start) | collective-permute-done | bytes 540704 | tf_op jit(solution)/shard_map/move_EA/ppermute | solution.py:73
  19.2 1.7 %collective-permute-start.7 = (bf16[64,4224]{1,0:T(8,128)(2,1)S(1)}, bf16[64,4224]{1,0:T(8,128)(2,1)S(1)}, u32[]{:S(2)}, u32[]{:S(2)}) collective-permute-start(bf16[64,4224]{1,0:T(8,128)(2,1)S(1)} %get-tuple-element.107.refs_2_), channel_id=1, source_target_pairs={{0,4},{1,5},{2,6},{3,7},{4,0},{5,1},{6,2},{7,3},{8,12},{9,13},{10,... | collective-permute-start | bytes 1622024 | tf_op jit(solution)/shard_map/move_EB/ppermute | solution.py:73
  24.8 1.6 collective-permute-start.1
  26.4 5.0 %W.1 = (bf16[448,4096]{1,0:T(8,128)(2,1)S(1)}, bf16[448,4096]{1,0:T(8,128)(2,1)S(1)}, bf16[896,2048]{1,0:T(8,128)(2,1)S(1)}, f32[8,128]{1,0:T(8,128)S(1)}) custom-call(s32[6]{0:T(128)S(1)} %stack.31.refs_0_, bf16[448,4096]{1,0:T(8,128)(2,1)} %get-tuple-element.113.refs_1_, ...), custom_call_target="tpu_custom_call", output_to_operand_aliasing={{3}: (4, {})} | custom-call | flops 1 | bytes 1 | tf_op jit(solution)/shard_map/W/pallas_call | solution.py:259
  32.8 1.6 collective-permute-done.7.refs_2_.refs_4_
  35.6 1.8 %collective-permute-start.11 = (bf16[64,4224]{1,0:T(8,128)(2,1)S(1)}, bf16[64,4224]{1,0:T(8,128)(2,1)S(1)}, u32[]{:S(2)}, u32[]{:S(2)}) collective-permute-start(bf16[64,4224]{1,0:T(8,128)(2,1)S(1)} %get-tuple-element.131), channel_id=1, source_target_pairs={{0,2},{1,3},{2,0},{3,1},{4,6},{5,7},{6,4},{7,5},{8,10},{9,11},{10,... | collective-permute-start | bytes 1622024 | tf_op jit(solution)/shard_map/move_Y1/ppermute | solution.py:16
  37.4 7.5 %collective-permute-done.6.refs_2_ = bf16[64,4224]{1,0:T(8,128)(2,1)S(1)} collective-permute-done((bf16[64,4224]{1,0:T(8,128)(2,1)S(1)}, bf16[64,4224]{1,0:T(8,128)(2,1)S(1)}, u32[]{:S(2)}, u32[]{:S(2)}) %collective-permute-start.6) | collective-permute-done | bytes 540704 | tf_op jit(solution)/shard_map/move_OB/ppermute | solution.py:73
  48.2 1.5 collective-permute-start.12
  49.7 5.9 %F0.1 = (bf16[64,4096]{1,0:T(8,128)(2,1)S(1)}, bf16[64,4096]{1,0:T(8,128)(2,1)S(1)}, f32[8,128]{1,0:T(8,128)S(1)}, bf16[64,4224]{1,0:T(8,128)(2,1)S(1)}) custom-call(s32[6]{0:T(128)S(1)} %stack.31.refs_0_, bf16[64,4224]{1,0:T(8,128)(2,1)S(1)} %get-tuple-element.110.refs_1_, ...), custom_call_target="tpu_custom_call", output_to_operand_aliasing={{2}: (9, {}), {3}: (10, {})} | custom-call | flops 1 | bytes 24150016 | tf_op jit(solution)/shard_map/F0/pallas_call | solution.py:259
  56.9 4.4 %collective-permute-done.10.refs_2_ = bf16[64,4224]{1,0:T(8,128)(2,1)S(1)} collective-permute-done((bf16[64,4224]{1,0:T(8,128)(2,1)S(1)}, bf16[64,4224]{1,0:T(8,128)(2,1)S(1)}, u32[]{:S(2)}, u32[]{:S(2)}) %collective-permute-start.10) | collective-permute-done | bytes 540704 | tf_op jit(solution)/shard_map/move_QA/ppermute | solution.py:73
  62.5 1.3 collective-permute-start.14
  63.8 5.8 %F2B.1 = (bf16[64,4096]{1,0:T(8,128)(2,1)S(1)}, bf16[40,4096]{1,0:T(8,128)(2,1)S(1)}, f32[8,128]{1,0:T(8,128)S(1)}) custom-call(s32[6]{0:T(128)S(1)} %stack.31.refs_0_, bf16[64,4224]{1,0:T(8,128)(2,1)S(1)} %get-tuple-element.133.refs_1_, bf16[40,4224]{1,0:T(8,128)(2,1)S(1)} %collective-permute-done.12.refs_2_, ...), custom_call_target="tpu_custom_call", output_to_operand_aliasing={{2}: (9, {})} | custom-call | flops 1 | bytes 23750656 | tf_op jit(solution)/shard_map/F2B/pallas_call | solution.py:259
  71.1 1.5 collective-permute-start.15
  77.0 5.8 %F3A.1 = (bf16[64,4096]{1,0:T(8,128)(2,1)S(1)}, bf16[40,4096]{1,0:T(8,128)(2,1)S(1)}, f32[8,128]{1,0:T(8,128)S(1)}) custom-call(s32[6]{0:T(128)S(1)} %stack.31.refs_0_, bf16[64,4224]{1,0:T(8,128)(2,1)S(1)} %get-tuple-element.143.refs_1_, bf16[40,4224]{1,0:T(8,128)(2,1)S(1)} %get-tuple-element.144.refs_2_, ...), custom_call_target="tpu_custom_call", output_to_operand_aliasing={{2}: (9, {})} | custom-call | flops 1 | bytes 23750656 | tf_op jit(solution)/shard_map/F3A/pallas_call | solution.py:259
  84.0 4.3 %collective-permute-start.21 = (bf16[64,4096]{1,0:T(8,128)(2,1)S(1)}, bf16[64,4096]{1,0:T(8,128)(2,1)S(1)}, u32[]{:S(2)}, u32[]{:S(2)}) collective-permute-start(bf16[64,4096]{1,0:T(8,128)(2,1)S(1)} %get-tuple-element.165), channel_id=1, source_target_pairs={{0,4},{1,5},{2,6},{3,7},{12,8},{13,9},{14,10},{15,11},{16,20},{17,... | collective-permute-start | bytes 1572872 | tf_op jit(solution)/shard_map/move_I2B/ppermute | solution.py:73
  90.4 5.9 %F1.1 = (bf16[64,4096]{1,0:T(8,128)(2,1)S(1)}, bf16[64,4096]{1,0:T(8,128)(2,1)S(1)}, f32[8,128]{1,0:T(8,128)S(1)}, bf16[40,4096]{1,0:T(8,128)(2,1)S(1)}) custom-call(s32[6]{0:T(128)S(1)} %stack.31.refs_0_, bf16[64,4224]{1,0:T(8,128)(2,1)S(1)} %get-tuple-element.128.refs_1_, ...), custom_call_target="tpu_custom_call", output_to_operand_aliasing={{2}: (9, {}), {3}: (10, {})} | custom-call | flops 1 | bytes 24150016 | tf_op jit(solution)/shard_map/F1/pallas_call | solution.py:259
  97.6 1.7 %collective-permute-done.20.refs_2_ = bf16[40,4224]{1,0:T(8,128)(2,1)S(1)} collective-permute-done((bf16[40,4224]{1,0:T(8,128)(2,1)S(1)}, bf16[40,4224]{1,0:T(8,128)(2,1)S(1)}, u32[]{:S(2)}, u32[]{:S(2)}) %collective-permute-start.20) | collective-permute-done | bytes 337952 | tf_op jit(solution)/shard_map/move_Y3B/ppermute | solution.py:16
  99.3 5.8 %F3B.1 = (bf16[64,4096]{1,0:T(8,128)(2,1)S(1)}, bf16[40,4096]{1,0:T(8,128)(2,1)S(1)}, f32[8,128]{1,0:T(8,128)S(1)}, bf16[64,4096]{1,0:T(8,128)(2,1)S(1)}) custom-call(s32[6]{0:T(128)S(1)} %stack.31.refs_0_, bf16[64,4224]{1,0:T(8,128)(2,1)S(1)} %get-tuple-element.162.refs_1_, ...), custom_call_target="tpu_custom_call", output_to_operand_aliasing={{2}: (9, {}), {3}: (10, {})} | custom-call | flops 1 | bytes 23750656 | tf_op jit(solution)/shard_map/F3B/pallas_call | solution.py:259
  107.3 2.8 %collective-permute-start.24 = (bf16[64,4096]{1,0:T(8,128)(2,1)S(1)}, bf16[64,4096]{1,0:T(8,128)(2,1)S(1)}, u32[]{:S(2)}, u32[]{:S(2)}) collective-permute-start(bf16[64,4096]{1,0:T(8,128)(2,1)S(1)} %get-tuple-element.180), channel_id=1, source_target_pairs={{0,4},{1,5},{2,6},{3,7},{12,8},{13,9},{14,10},{15,11},{16,20},{17,... | collective-permute-start | bytes 1572872 | tf_op jit(solution)/shard_map/move_I3A/ppermute | solution.py:73
  111.0 5.8 %F2A.1 = (bf16[64,4096]{1,0:T(8,128)(2,1)S(1)}, bf16[40,4096]{1,0:T(8,128)(2,1)S(1)}, f32[8,128]{1,0:T(8,128)S(1)}) custom-call(s32[6]{0:T(128)S(1)} %stack.31.refs_0_, bf16[64,4224]{1,0:T(8,128)(2,1)S(1)} %get-tuple-element.157.refs_1_, bf16[40,4224]{1,0:T(8,128)(2,1)S(1)} %get-tuple-element.158.refs_2_, ...), custom_call_target="tpu_custom_call", output_to_operand_aliasing={{2}: (9, {})} | custom-call | flops 1 | bytes 23750656 | tf_op jit(solution)/shard_map/F2A/pallas_call | solution.py:259
  117.7 6.5 %collective-permute-start.28 = (bf16[64,4096]{1,0:T(8,128)(2,1)S(1)}, bf16[64,4096]{1,0:T(8,128)(2,1)S(1)}, u32[]{:S(2)}, u32[]{:S(2)}) collective-permute-start(bf16[64,4096]{1,0:T(8,128)(2,1)S(1)} %get-tuple-element.187), channel_id=1, source_target_pairs={{0,4},{1,5},{2,6},{3,7},{12,8},{13,9},{14,10},{15,11},{16,20},{17,... | collective-permute-start | bytes 1572872 | tf_op jit(solution)/shard_map/move_I3B/ppermute | solution.py:73
  126.7 6.4 %collective-permute-done.23.refs_3_.refs_6_ = bf16[40,4096]{1,0:T(8,128)(2,1)S(1)} collective-permute-done((bf16[40,4096]{1,0:T(8,128)(2,1)S(1)}, bf16[40,4096]{1,0:T(8,128)(2,1)S(1)}, u32[]{:S(2)}, u32[]{:S(2)}) %collective-permute-start.23) | collective-permute-done | bytes 327712 | tf_op jit(solution)/shard_map/move_R2A/ppermute | solution.py:16
  133.9 1.3 collective-permute-start.26
  135.3 1.8 %collective-permute-start.31 = (bf16[64,4096]{1,0:T(8,128)(2,1)S(1)}, bf16[64,4096]{1,0:T(8,128)(2,1)S(1)}, u32[]{:S(2)}, u32[]{:S(2)}) collective-permute-start(bf16[64,4096]{1,0:T(8,128)(2,1)S(1)} %get-tuple-element.194), channel_id=1, source_target_pairs={{0,4},{1,5},{2,6},{3,7},{12,8},{13,9},{14,10},{15,11},{16,20},{17,... | collective-permute-start | bytes 1572872 | tf_op jit(solution)/shard_map/move_I2A/ppermute | solution.py:73
  138.7 7.5 %collective-permute-done.26.refs_3_.refs_6_ = bf16[64,4096]{1,0:T(8,128)(2,1)S(1)} collective-permute-done((bf16[64,4096]{1,0:T(8,128)(2,1)S(1)}, bf16[64,4096]{1,0:T(8,128)(2,1)S(1)}, u32[]{:S(2)}, u32[]{:S(2)}) %collective-permute-start.26) | collective-permute-done | bytes 524320 | tf_op jit(solution)/shard_map/move_R1/ppermute | solution.py:16
  147.2 1.8 %collective-permute-start.29 = (bf16[64,4096]{1,0:T(8,128)(2,1)S(1)}, bf16[64,4096]{1,0:T(8,128)(2,1)S(1)}, u32[]{:S(2)}, u32[]{:S(2)}) collective-permute-start(bf16[64,4096]{1,0:T(8,128)(2,1)S(1)} %get-tuple-element.191), channel_id=1, source_target_pairs={{0,2},{1,3},{2,0},{3,1},{4,6},{5,7},{6,4},{7,5},{8,10},{9,11},{10,... | collective-permute-start | bytes 1572872 | tf_op jit(solution)/shard_map/move_R0/ppermute | solution.py:16
  152.1 5.0 %collective-permute-start.34 = (bf16[64,4096]{1,0:T(8,128)(2,1)S(1)}, bf16[64,4096]{1,0:T(8,128)(2,1)S(1)}, u32[]{:S(2)}, u32[]{:S(2)}) collective-permute-start(bf16[64,4096]{1,0:T(8,128)(2,1)S(1)} %get-tuple-element.201), channel_id=1, source_target_pairs={{0,4},{1,5},{2,6},{3,7},{4,0},{5,1},{6,2},{7,3},{8,12},{9,13},{10,... | collective-permute-start | bytes 1572872 | tf_op jit(solution)/shard_map/move_S1B/ppermute | solution.py:73
  157.1 3.2 %collective-permute-done.30.refs_5_ = bf16[64,4096]{1,0:T(8,128)(2,1)S(1)} collective-permute-done((bf16[64,4096]{1,0:T(8,128)(2,1)S(1)}, bf16[64,4096]{1,0:T(8,128)(2,1)S(1)}, u32[]{:S(2)}, u32[]{:S(2)}) %collective-permute-start.30) | collective-permute-done | bytes 524320 | tf_op jit(solution)/shard_map/move_S1A/ppermute | solution.py:73
  160.3 5.6 %collective-permute-done.34.refs_7_ = bf16[64,4096]{1,0:T(8,128)(2,1)S(1)} collective-permute-done((bf16[64,4096]{1,0:T(8,128)(2,1)S(1)}, bf16[64,4096]{1,0:T(8,128)(2,1)S(1)}, u32[]{:S(2)}, u32[]{:S(2)}) %collective-permute-start.34) | collective-permute-done | bytes 524320 | tf_op jit(solution)/shard_map/move_S1B/ppermute | solution.py:73
  165.9 2.4 %fin.1 = (bf16[128,4096]{1,0:T(8,128)(2,1)}, f32[8,128]{1,0:T(8,128)S(1)}) custom-call(s32[6]{0:T(128)S(1)} %stack.31.refs_0_, bf16[128,128]{1,0:T(8,128)(2,1)S(1)} %get-tuple-element.105.refs_1_, bf16[128,128]{1,0:T(8,128)(2,1)S(1)} %get-tuple-element.109.refs_2_, bf16[64,4096]{1,0:T(8,128)(2,1)S(1)} %get-tuple-element.126.refs_3_, ...), custom_call_target="tpu_custom_call", output_to_operand_aliasing={{1}: (9, {})} | custom-call | flops 1 | bytes 1 | tf_op jit(solution)/shard_map/fin/pallas_call | solution.py:259
  (75 shorter events, 37.1 us)
Async XLA Ops:
  0.0 22.9 %collective-permute-start.3 = (bf16[448,4096]{1,0:T(8,128)(2,1)}, bf16[448,4096]{1,0:T(8,128)(2,1)}, u32[]{:S(2)}, u32[]{:S(2)}) collective-permute-start(bf16[448,4096]{1,0:T(8,128)(2,1)} %bitcast.10), channel_id=1, source_target_pairs={{0,1},{1,0},{2,3},{3,2},{4,5},{5,4},{6,7},{7,6},{8,9},{9,8},{10,11... | collective-permute-start | bytes 11010056 | tf_op jit(solution)/shard_map/move_wg/ppermute | solution.py:16
  0.5 22.5 %collective-permute-start.4 = (bf16[448,4096]{1,0:T(8,128)(2,1)}, bf16[448,4096]{1,0:T(8,128)(2,1)}, u32[]{:S(2)}, u32[]{:S(2)}) collective-permute-start(bf16[448,4096]{1,0:T(8,128)(2,1)} %bitcast.17), channel_id=1, source_target_pairs={{0,1},{1,0},{2,3},{3,2},{4,5},{5,4},{6,7},{7,6},{8,9},{9,8},{10,11... | collective-permute-start | bytes 11010056 | tf_op jit(solution)/shard_map/move_wu/ppermute | solution.py:16
  0.5 25.9 %collective-permute-start.5 = (bf16[896,2048]{1,0:T(8,128)(2,1)}, bf16[896,2048]{1,0:T(8,128)(2,1)}, u32[]{:S(2)}, u32[]{:S(2)}) collective-permute-start(bf16[896,2048]{1,0:T(8,128)(2,1)} %refs_7_.11), channel_id=1, source_target_pairs={{0,1},{1,0},{2,3},{3,2},{4,5},{5,4},{6,7},{7,6},{8,9},{9,8},{10,11... | collective-permute-start | bytes 11010056 | tf_op jit(solution)/shard_map/move_wd/ppermute | solution.py:16
  3.7 15.6 %collective-permute-start = (bf16[64,4224]{1,0:T(8,128)(2,1)S(1)}, bf16[64,4224]{1,0:T(8,128)(2,1)S(1)}, u32[]{:S(2)}, u32[]{:S(2)}) collective-permute-start(bf16[64,4224]{1,0:T(8,128)(2,1)S(1)} %get-tuple-element.106.refs_1_.refs_2_), channel_id=1, source_target_pairs={{0,4},{1,5},{2,6},{3,7},{4,0},{5,1},{6,2},{7,3},{8,12},{9,13},{10,... | collective-permute-start | bytes 1622024 | tf_op jit(solution)/shard_map/move_EA/ppermute | solution.py:73
  6.3 15.9 %collective-permute-start.2 = (bf16[64,4224]{1,0:T(8,128)(2,1)S(1)}, bf16[64,4224]{1,0:T(8,128)(2,1)S(1)}, u32[]{:S(2)}, u32[]{:S(2)}) collective-permute-start(bf16[64,4224]{1,0:T(8,128)(2,1)S(1)} %get-tuple-element.107.refs_2_), channel_id=1, source_target_pairs={{4,8},{5,9},{6,10},{7,11},{8,4},{9,5},{10,6},{11,7},{20,24},{21,25... | collective-permute-start | bytes 1622024 | tf_op jit(solution)/shard_map/move_MB/ppermute | solution.py:73
  19.2 15.2 %collective-permute-start.7 = (bf16[64,4224]{1,0:T(8,128)(2,1)S(1)}, bf16[64,4224]{1,0:T(8,128)(2,1)S(1)}, u32[]{:S(2)}, u32[]{:S(2)}) collective-permute-start(bf16[64,4224]{1,0:T(8,128)(2,1)S(1)} %get-tuple-element.107.refs_2_), channel_id=1, source_target_pairs={{0,4},{1,5},{2,6},{3,7},{4,0},{5,1},{6,2},{7,3},{8,12},{9,13},{10,... | collective-permute-start | bytes 1622024 | tf_op jit(solution)/shard_map/move_EB/ppermute | solution.py:73
  22.2 15.2 %collective-permute-start.8 = (bf16[64,4224]{1,0:T(8,128)(2,1)S(1)}, bf16[64,4224]{1,0:T(8,128)(2,1)S(1)}, u32[]{:S(2)}, u32[]{:S(2)}) collective-permute-start(bf16[64,4224]{1,0:T(8,128)(2,1)S(1)} %get-tuple-element.120.refs_1_), channel_id=1, source_target_pairs={{4,8},{5,9},{6,10},{7,11},{8,4},{9,5},{10,6},{11,7},{20,24},{21,25... | collective-permute-start | bytes 1622024 | tf_op jit(solution)/shard_map/move_NA/ppermute | solution.py:73
  23.5 21.4 %collective-permute-start.6 = (bf16[64,4224]{1,0:T(8,128)(2,1)S(1)}, bf16[64,4224]{1,0:T(8,128)(2,1)S(1)}, u32[]{:S(2)}, u32[]{:S(2)}) collective-permute-start(bf16[64,4224]{1,0:T(8,128)(2,1)S(1)} %get-tuple-element.119.refs_1_), channel_id=1, source_target_pairs={{4,0},{5,1},{6,2},{7,3},{8,12},{9,13},{10,14},{11,15},{20,16},{21,... | collective-permute-start | bytes 1622024 | tf_op jit(solution)/shard_map/move_OB/ppermute | solution.py:73
  24.8 23.3 %collective-permute-start.1 = (bf16[64,4224]{1,0:T(8,128)(2,1)S(1)}, bf16[64,4224]{1,0:T(8,128)(2,1)S(1)}, u32[]{:S(2)}, u32[]{:S(2)}) collective-permute-start(bf16[64,4224]{1,0:T(8,128)(2,1)S(1)} %get-tuple-element.111), channel_id=1, source_target_pairs={{0,2},{1,3},{2,0},{3,1},{4,6},{5,7},{6,4},{7,5},{8,10},{9,11},{10,... | collective-permute-start | bytes 1622024 | tf_op jit(solution)/shard_map/move_Y0/ppermute | solution.py:16
  32.0 17.7 %collective-permute-start.9 = (bf16[64,4224]{1,0:T(8,128)(2,1)S(1)}, bf16[64,4224]{1,0:T(8,128)(2,1)S(1)}, u32[]{:S(2)}, u32[]{:S(2)}) collective-permute-start(bf16[64,4224]{1,0:T(8,128)(2,1)S(1)} %get-tuple-element.125), channel_id=1, source_target_pairs={{4,8},{5,9},{6,10},{7,11},{8,4},{9,5},{10,6},{11,7},{20,24},{21,25... | collective-permute-start | bytes 1622024 | tf_op jit(solution)/shard_map/move_MA/ppermute | solution.py:73
  35.6 21.3 %collective-permute-start.11 = (bf16[64,4224]{1,0:T(8,128)(2,1)S(1)}, bf16[64,4224]{1,0:T(8,128)(2,1)S(1)}, u32[]{:S(2)}, u32[]{:S(2)}) collective-permute-start(bf16[64,4224]{1,0:T(8,128)(2,1)S(1)} %get-tuple-element.131), channel_id=1, source_target_pairs={{0,2},{1,3},{2,0},{3,1},{4,6},{5,7},{6,4},{7,5},{8,10},{9,11},{10,... | collective-permute-start | bytes 1622024 | tf_op jit(solution)/shard_map/move_Y1/ppermute | solution.py:16
  46.2 15.1 %collective-permute-start.10 = (bf16[64,4224]{1,0:T(8,128)(2,1)S(1)}, bf16[64,4224]{1,0:T(8,128)(2,1)S(1)}, u32[]{:S(2)}, u32[]{:S(2)}) collective-permute-start(bf16[64,4224]{1,0:T(8,128)(2,1)S(1)} %get-tuple-element.129.refs_1_), channel_id=1, source_target_pairs={{4,0},{5,1},{6,2},{7,3},{8,12},{9,13},{10,14},{11,15},{20,16},{21,... | collective-permute-start | bytes 1622024 | tf_op jit(solution)/shard_map/move_QA/ppermute | solution.py:73
  47.5 22.2 %collective-permute-start.13 = (bf16[64,4224]{1,0:T(8,128)(2,1)S(1)}, bf16[64,4224]{1,0:T(8,128)(2,1)S(1)}, u32[]{:S(2)}, u32[]{:S(2)}) collective-permute-start(bf16[64,4224]{1,0:T(8,128)(2,1)S(1)} %get-tuple-element.137), channel_id=1, source_target_pairs={{4,8},{5,9},{6,10},{7,11},{8,4},{9,5},{10,6},{11,7},{20,24},{21,25... | collective-permute-start | bytes 1622024 | tf_op jit(solution)/shard_map/move_NB/ppermute | solution.py:73
  48.2 15.7 %collective-permute-start.12 = (bf16[40,4224]{1,0:T(8,128)(2,1)S(1)}, bf16[40,4224]{1,0:T(8,128)(2,1)S(1)}, u32[]{:S(2)}, u32[]{:S(2)}) collective-permute-start(bf16[40,4224]{1,0:T(8,128)(2,1)S(1)} %get-tuple-element.134), channel_id=1, source_target_pairs={{0,2},{1,3},{2,0},{3,1},{4,6},{5,7},{6,4},{7,5},{8,10},{9,11},{10,... | collective-permute-start | bytes 1013768 | tf_op jit(solution)/shard_map/move_Y2B/ppermute | solution.py:16
  55.6 19.3 %collective-permute-start.17 = (bf16[64,4224]{1,0:T(8,128)(2,1)S(1)}, bf16[64,4224]{1,0:T(8,128)(2,1)S(1)}, u32[]{:S(2)}, u32[]{:S(2)}) collective-permute-start(bf16[64,4224]{1,0:T(8,128)(2,1)S(1)} %get-tuple-element.145.refs_1_), channel_id=1, source_target_pairs={{4,0},{5,1},{6,2},{7,3},{8,12},{9,13},{10,14},{11,15},{20,16},{21,... | collective-permute-start | bytes 1622024 | tf_op jit(solution)/shard_map/move_OA/ppermute | solution.py:73
  71.1 17.2 %collective-permute-start.15 = (bf16[64,4224]{1,0:T(8,128)(2,1)S(1)}, bf16[64,4224]{1,0:T(8,128)(2,1)S(1)}, u32[]{:S(2)}, u32[]{:S(2)}) collective-permute-start(bf16[64,4224]{1,0:T(8,128)(2,1)S(1)} %get-tuple-element.139.refs_1_), channel_id=1, source_target_pairs={{4,0},{5,1},{6,2},{7,3},{8,12},{9,13},{10,14},{11,15},{20,16},{21,... | collective-permute-start | bytes 1622024 | tf_op jit(solution)/shard_map/move_QB/ppermute | solution.py:73
  72.6 10.5 %collective-permute-start.16 = (bf16[40,4096]{1,0:T(8,128)(2,1)S(1)}, bf16[40,4096]{1,0:T(8,128)(2,1)S(1)}, u32[]{:S(2)}, u32[]{:S(2)}) collective-permute-start(bf16[40,4096]{1,0:T(8,128)(2,1)S(1)} %get-tuple-element.142), channel_id=1, source_target_pairs={{0,2},{1,3},{2,0},{3,1},{4,6},{5,7},{6,4},{7,5},{8,10},{9,11},{10,... | collective-permute-start | bytes 983048 | tf_op jit(solution)/shard_map/move_R2B/ppermute | solution.py:16
  76.7 11.6 %collective-permute-start.18 = (bf16[40,4224]{1,0:T(8,128)(2,1)S(1)}, bf16[40,4224]{1,0:T(8,128)(2,1)S(1)}, u32[]{:S(2)}, u32[]{:S(2)}) collective-permute-start(bf16[40,4224]{1,0:T(8,128)(2,1)S(1)} %get-tuple-element.152), channel_id=1, source_target_pairs={{0,2},{1,3},{2,0},{3,1},{4,6},{5,7},{6,4},{7,5},{8,10},{9,11},{10,... | collective-permute-start | bytes 1013768 | tf_op jit(solution)/shard_map/move_Y2A/ppermute | solution.py:16
  84.0 13.6 %collective-permute-start.21 = (bf16[64,4096]{1,0:T(8,128)(2,1)S(1)}, bf16[64,4096]{1,0:T(8,128)(2,1)S(1)}, u32[]{:S(2)}, u32[]{:S(2)}) collective-permute-start(bf16[64,4096]{1,0:T(8,128)(2,1)S(1)} %get-tuple-element.165), channel_id=1, source_target_pairs={{0,4},{1,5},{2,6},{3,7},{12,8},{13,9},{14,10},{15,11},{16,20},{17,... | collective-permute-start | bytes 1572872 | tf_op jit(solution)/shard_map/move_I2B/ppermute | solution.py:73
  89.5 9.7 %collective-permute-start.20 = (bf16[40,4224]{1,0:T(8,128)(2,1)S(1)}, bf16[40,4224]{1,0:T(8,128)(2,1)S(1)}, u32[]{:S(2)}, u32[]{:S(2)}) collective-permute-start(bf16[40,4224]{1,0:T(8,128)(2,1)S(1)} %get-tuple-element.163), channel_id=1, source_target_pairs={{0,2},{1,3},{2,0},{3,1},{4,6},{5,7},{6,4},{7,5},{8,10},{9,11},{10,... | collective-permute-start | bytes 1013768 | tf_op jit(solution)/shard_map/move_Y3B/ppermute | solution.py:16
  96.3 10.1 %collective-permute-start.19 = (bf16[40,4096]{1,0:T(8,128)(2,1)S(1)}, bf16[40,4096]{1,0:T(8,128)(2,1)S(1)}, u32[]{:S(2)}, u32[]{:S(2)}) collective-permute-start(bf16[40,4096]{1,0:T(8,128)(2,1)S(1)} %get-tuple-element.161), channel_id=1, source_target_pairs={{0,2},{1,3},{2,0},{3,1},{4,6},{5,7},{6,4},{7,5},{8,10},{9,11},{10,... | collective-permute-start | bytes 983048 | tf_op jit(solution)/shard_map/move_R3A/ppermute | solution.py:16
  106.0 10.9 %collective-permute-start.22 = (bf16[40,4096]{1,0:T(8,128)(2,1)S(1)}, bf16[40,4096]{1,0:T(8,128)(2,1)S(1)}, u32[]{:S(2)}, u32[]{:S(2)}) collective-permute-start(bf16[40,4096]{1,0:T(8,128)(2,1)S(1)} %get-tuple-element.175), channel_id=1, source_target_pairs={{0,2},{1,3},{2,0},{3,1},{4,6},{5,7},{6,4},{7,5},{8,10},{9,11},{10,... | collective-permute-start | bytes 983048 | tf_op jit(solution)/shard_map/move_R3B/ppermute | solution.py:16
  107.3 17.8 %collective-permute-start.24 = (bf16[64,4096]{1,0:T(8,128)(2,1)S(1)}, bf16[64,4096]{1,0:T(8,128)(2,1)S(1)}, u32[]{:S(2)}, u32[]{:S(2)}) collective-permute-start(bf16[64,4096]{1,0:T(8,128)(2,1)S(1)} %get-tuple-element.180), channel_id=1, source_target_pairs={{0,4},{1,5},{2,6},{3,7},{12,8},{13,9},{14,10},{15,11},{16,20},{17,... | collective-permute-start | bytes 1572872 | tf_op jit(solution)/shard_map/move_I3A/ppermute | solution.py:73
  110.1 16.6 %collective-permute-start.25 = (bf16[64,4096]{1,0:T(8,128)(2,1)S(1)}, bf16[64,4096]{1,0:T(8,128)(2,1)S(1)}, u32[]{:S(2)}, u32[]{:S(2)}) collective-permute-start(bf16[64,4096]{1,0:T(8,128)(2,1)S(1)} %get-tuple-element.183), channel_id=1, source_target_pairs={{4,8},{5,9},{6,10},{7,11},{8,4},{9,5},{10,6},{11,7},{20,24},{21,25... | collective-permute-start | bytes 1572872 | tf_op jit(solution)/shard_map/move_S2B/ppermute | solution.py:73
  117.7 19.4 %collective-permute-start.28 = (bf16[64,4096]{1,0:T(8,128)(2,1)S(1)}, bf16[64,4096]{1,0:T(8,128)(2,1)S(1)}, u32[]{:S(2)}, u32[]{:S(2)}) collective-permute-start(bf16[64,4096]{1,0:T(8,128)(2,1)S(1)} %get-tuple-element.187), channel_id=1, source_target_pairs={{0,4},{1,5},{2,6},{3,7},{12,8},{13,9},{14,10},{15,11},{16,20},{17,... | collective-permute-start | bytes 1572872 | tf_op jit(solution)/shard_map/move_I3B/ppermute | solution.py:73
  125.9 12.8 %collective-permute-start.27 = (bf16[64,4096]{1,0:T(8,128)(2,1)S(1)}, bf16[64,4096]{1,0:T(8,128)(2,1)S(1)}, u32[]{:S(2)}, u32[]{:S(2)}) collective-permute-start(bf16[64,4096]{1,0:T(8,128)(2,1)S(1)} %get-tuple-element.186), channel_id=1, source_target_pairs={{4,8},{5,9},{6,10},{7,11},{8,4},{9,5},{10,6},{11,7},{20,24},{21,25... | collective-permute-start | bytes 1572872 | tf_op jit(solution)/shard_map/move_S3A/ppermute | solution.py:73
  133.9 12.3 %collective-permute-start.26 = (bf16[64,4096]{1,0:T(8,128)(2,1)S(1)}, bf16[64,4096]{1,0:T(8,128)(2,1)S(1)}, u32[]{:S(2)}, u32[]{:S(2)}) collective-permute-start(bf16[64,4096]{1,0:T(8,128)(2,1)S(1)} %get-tuple-element.185), channel_id=1, source_target_pairs={{0,2},{1,3},{2,0},{3,1},{4,6},{5,7},{6,4},{7,5},{8,10},{9,11},{10,... | collective-permute-start | bytes 1572872 | tf_op jit(solution)/shard_map/move_R1/ppermute | solution.py:16
  135.3 14.2 %collective-permute-start.31 = (bf16[64,4096]{1,0:T(8,128)(2,1)S(1)}, bf16[64,4096]{1,0:T(8,128)(2,1)S(1)}, u32[]{:S(2)}, u32[]{:S(2)}) collective-permute-start(bf16[64,4096]{1,0:T(8,128)(2,1)S(1)} %get-tuple-element.194), channel_id=1, source_target_pairs={{0,4},{1,5},{2,6},{3,7},{12,8},{13,9},{14,10},{15,11},{16,20},{17,... | collective-permute-start | bytes 1572872 | tf_op jit(solution)/shard_map/move_I2A/ppermute | solution.py:73
  138.0 12.4 %collective-permute-start.32 = (bf16[64,4096]{1,0:T(8,128)(2,1)S(1)}, bf16[64,4096]{1,0:T(8,128)(2,1)S(1)}, u32[]{:S(2)}, u32[]{:S(2)}) collective-permute-start(bf16[64,4096]{1,0:T(8,128)(2,1)S(1)} %get-tuple-element.197), channel_id=1, source_target_pairs={{4,8},{5,9},{6,10},{7,11},{8,4},{9,5},{10,6},{11,7},{20,24},{21,25... | collective-permute-start | bytes 1572872 | tf_op jit(solution)/shard_map/move_S3B/ppermute | solution.py:73
  147.2 9.9 %collective-permute-start.29 = (bf16[64,4096]{1,0:T(8,128)(2,1)S(1)}, bf16[64,4096]{1,0:T(8,128)(2,1)S(1)}, u32[]{:S(2)}, u32[]{:S(2)}) collective-permute-start(bf16[64,4096]{1,0:T(8,128)(2,1)S(1)} %get-tuple-element.191), channel_id=1, source_target_pairs={{0,2},{1,3},{2,0},{3,1},{4,6},{5,7},{6,4},{7,5},{8,10},{9,11},{10,... | collective-permute-start | bytes 1572872 | tf_op jit(solution)/shard_map/move_R0/ppermute | solution.py:16
  149.0 11.3 %collective-permute-start.30 = (bf16[64,4096]{1,0:T(8,128)(2,1)S(1)}, bf16[64,4096]{1,0:T(8,128)(2,1)S(1)}, u32[]{:S(2)}, u32[]{:S(2)}) collective-permute-start(bf16[64,4096]{1,0:T(8,128)(2,1)S(1)} %get-tuple-element.192), channel_id=1, source_target_pairs={{0,4},{1,5},{2,6},{3,7},{4,0},{5,1},{6,2},{7,3},{8,12},{9,13},{10,... | collective-permute-start | bytes 1572872 | tf_op jit(solution)/shard_map/move_S1A/ppermute | solution.py:73
  152.1 13.9 %collective-permute-start.34 = (bf16[64,4096]{1,0:T(8,128)(2,1)S(1)}, bf16[64,4096]{1,0:T(8,128)(2,1)S(1)}, u32[]{:S(2)}, u32[]{:S(2)}) collective-permute-start(bf16[64,4096]{1,0:T(8,128)(2,1)S(1)} %get-tuple-element.201), channel_id=1, source_target_pairs={{0,4},{1,5},{2,6},{3,7},{4,0},{5,1},{6,2},{7,3},{8,12},{9,13},{10,... | collective-permute-start | bytes 1572872 | tf_op jit(solution)/shard_map/move_S1B/ppermute | solution.py:73
  (6 other events, 90.7 us)

commit v2 on v1

--- a/solution.py
+++ b/solution.py
@@ -279,8 +279,8 @@
     ["f", "OB", "+wg", "+wu"],
     ["W"],
     ["f", "MA"],
-    ["P1", "Y1"],
-    ["P2B", "QA", "Y2B", "NB"],
+    ["P1", "Y1", "QA"],
+    ["P2B", "Y2B", "NB"],
     ["F0", "OA"],
     ["P3A", "Y3A", "+Y1"],
     ["F2B", "R2B"],

time: 169 us -> 165 us (0.976)
  starting transfers between devices: 51.7 us -> 46.2 us
    ppermute x15, waiting for transfers between devices: 16.8 us -> 26.1 us  [swapped(): lax.ppermute(x, axis, [(i, i ^ 1 << apart) for i in range(lax.axis_size(a...]
    ppermute x20, waiting for transfers between devices: 35.9 us -> 27.9 us  [along_line(): return lax.ppermute(x, 'expert', moves)]
    ppermute x20, starting transfers between devices: 36.6 us -> 31.8 us  [along_line(): return lax.ppermute(x, 'expert', moves)]
  transfers between devices with their start and end apart: 35 -> 35, of which waited for: 12 -> 11; matrix products, arithmetic and copies ran while one was open for 0% -> 0% of each run, Pallas kernels for 36% -> 37%
where the time goes in v2:
time: 165 us; the launch traced here: 164 us
  Pallas kernels  63.4 us (38%)
  waiting for transfers between devices  54 us (33%)
  starting transfers between devices  46.2 us (28%)
    pallas_call x29, Pallas kernels, call(): pl.pallas_call(body, out_shape=[*outs, *(jax.ShapeDtypeStruct(x.shape, x....  63.4 us
    ppermute x20, starting transfers between devices, along_line(): return lax.ppermute(x, 'expert', moves)  31.8 us
    ppermute x20, waiting for transfers between devices, along_line(): return lax.ppermute(x, 'expert', moves)  27.9 us
    ppermute x15, waiting for transfers between devices, swapped(): lax.ppermute(x, axis, [(i, i ^ 1 << apart) for i in range(lax.axis_size(a...  26.1 us
    ppermute x15, starting transfers between devices, swapped(): lax.ppermute(x, axis, [(i, i ^ 1 << apart) for i in range(lax.axis_size(a...  14.4 us
  transfers between devices with their start and end apart: 35, of which 11 were waited for; matrix products, arithmetic and copies ran while one was open for 0% of the time, Pallas kernels for 37%

profile of v2, /device:TPU:0, one launch (start us, length us, event | category | flops | bytes accessed | tf_op | source)
XLA Modules:
  0.0 164.4 jit_solution(2135951811707863932)
XLA Ops:
  1.1 2.6 %prep.1 = (bf16[64,4224]{1,0:T(8,128)(2,1)S(1)}, bf16[64,4224]{1,0:T(8,128)(2,1)S(1)}, bf16[128,128]{1,0:T(8,128)(2,1)S(1)}, f32[8,128]{1,0:T(8,128)S(1)}) custom-call(s32[6]{0:T(128)S(1)} %stack.31.refs_0_, s32[4,128]{1,0:T(4,128)} %bitcast.24, f32[4,128]{1,0:T(4,128)} %bitcast.25, bf16[128,4096]{1,0:T(8,128)(2,1)} %refs_3_.1, ...), custom_call_target="tpu_custom_call", output_to_operand_aliasing={{3}: (4, {})} | custom-call | flops 1 | bytes 1 | tf_op jit(solution)/shard_map/prep/pallas_call | solution.py:259
  3.7 2.6 %collective-permute-start = (bf16[64,4224]{1,0:T(8,128)(2,1)S(1)}, bf16[64,4224]{1,0:T(8,128)(2,1)S(1)}, u32[]{:S(2)}, u32[]{:S(2)}) collective-permute-start(bf16[64,4224]{1,0:T(8,128)(2,1)S(1)} %get-tuple-element.106.refs_1_.refs_2_), channel_id=1, source_target_pairs={{0,4},{1,5},{2,6},{3,7},{4,0},{5,1},{6,2},{7,3},{8,12},{9,13},{10,... | collective-permute-start | bytes 1622024 | tf_op jit(solution)/shard_map/move_EA/ppermute | solution.py:73
  7.0 12.3 %collective-permute-done.refs_4_ = bf16[64,4224]{1,0:T(8,128)(2,1)S(1)} collective-permute-done((bf16[64,4224]{1,0:T(8,128)(2,1)S(1)}, bf16[64,4224]{1,0:T(8,128)(2,1)S(1)}, u32[]{:S(2)}, u32[]{:S(2)}) %collective-permute-start) | collective-permute-done | bytes 540704 | tf_op jit(solution)/shard_map/move_EA/ppermute | solution.py:73
  19.2 1.7 %collective-permute-start.7 = (bf16[64,4224]{1,0:T(8,128)(2,1)S(1)}, bf16[64,4224]{1,0:T(8,128)(2,1)S(1)}, u32[]{:S(2)}, u32[]{:S(2)}) collective-permute-start(bf16[64,4224]{1,0:T(8,128)(2,1)S(1)} %get-tuple-element.107.refs_2_), channel_id=1, source_target_pairs={{0,4},{1,5},{2,6},{3,7},{4,0},{5,1},{6,2},{7,3},{8,12},{9,13},{10,... | collective-permute-start | bytes 1622024 | tf_op jit(solution)/shard_map/move_EB/ppermute | solution.py:73
  24.8 1.6 collective-permute-start.1
  26.4 5.0 %W.1 = (bf16[448,4096]{1,0:T(8,128)(2,1)S(1)}, bf16[448,4096]{1,0:T(8,128)(2,1)S(1)}, bf16[896,2048]{1,0:T(8,128)(2,1)S(1)}, f32[8,128]{1,0:T(8,128)S(1)}) custom-call(s32[6]{0:T(128)S(1)} %stack.31.refs_0_, bf16[448,4096]{1,0:T(8,128)(2,1)} %get-tuple-element.113.refs_1_, ...), custom_call_target="tpu_custom_call", output_to_operand_aliasing={{3}: (4, {})} | custom-call | flops 1 | bytes 1 | tf_op jit(solution)/shard_map/W/pallas_call | solution.py:259
  32.8 1.6 collective-permute-done.7.refs_2_.refs_4_
  36.9 1.8 %collective-permute-start.11 = (bf16[64,4224]{1,0:T(8,128)(2,1)S(1)}, bf16[64,4224]{1,0:T(8,128)(2,1)S(1)}, u32[]{:S(2)}, u32[]{:S(2)}) collective-permute-start(bf16[64,4224]{1,0:T(8,128)(2,1)S(1)} %get-tuple-element.131), channel_id=1, source_target_pairs={{0,2},{1,3},{2,0},{3,1},{4,6},{5,7},{6,4},{7,5},{8,10},{9,11},{10,... | collective-permute-start | bytes 1622024 | tf_op jit(solution)/shard_map/move_Y1/ppermute | solution.py:16
  38.7 7.3 %collective-permute-done.6.refs_2_ = bf16[64,4224]{1,0:T(8,128)(2,1)S(1)} collective-permute-done((bf16[64,4224]{1,0:T(8,128)(2,1)S(1)}, bf16[64,4224]{1,0:T(8,128)(2,1)S(1)}, u32[]{:S(2)}, u32[]{:S(2)}) %collective-permute-start.6) | collective-permute-done | bytes 540704 | tf_op jit(solution)/shard_map/move_OB/ppermute | solution.py:73
  47.9 1.8 %collective-permute-start.12 = (bf16[40,4224]{1,0:T(8,128)(2,1)S(1)}, bf16[40,4224]{1,0:T(8,128)(2,1)S(1)}, u32[]{:S(2)}, u32[]{:S(2)}) collective-permute-start(bf16[40,4224]{1,0:T(8,128)(2,1)S(1)} %get-tuple-element.134), channel_id=1, source_target_pairs={{0,2},{1,3},{2,0},{3,1},{4,6},{5,7},{6,4},{7,5},{8,10},{9,11},{10,... | collective-permute-start | bytes 1013768 | tf_op jit(solution)/shard_map/move_Y2B/ppermute | solution.py:16
  49.7 5.9 %F0.1 = (bf16[64,4096]{1,0:T(8,128)(2,1)S(1)}, bf16[64,4096]{1,0:T(8,128)(2,1)S(1)}, f32[8,128]{1,0:T(8,128)S(1)}, bf16[64,4224]{1,0:T(8,128)(2,1)S(1)}) custom-call(s32[6]{0:T(128)S(1)} %stack.31.refs_0_, bf16[64,4224]{1,0:T(8,128)(2,1)S(1)} %get-tuple-element.110.refs_1_, ...), custom_call_target="tpu_custom_call", output_to_operand_aliasing={{2}: (9, {}), {3}: (10, {})} | custom-call | flops 1 | bytes 24150016 | tf_op jit(solution)/shard_map/F0/pallas_call | solution.py:259
  59.3 5.8 %F2B.1 = (bf16[64,4096]{1,0:T(8,128)(2,1)S(1)}, bf16[40,4096]{1,0:T(8,128)(2,1)S(1)}, f32[8,128]{1,0:T(8,128)S(1)}) custom-call(s32[6]{0:T(128)S(1)} %stack.31.refs_0_, bf16[64,4224]{1,0:T(8,128)(2,1)S(1)} %get-tuple-element.133.refs_1_, bf16[40,4224]{1,0:T(8,128)(2,1)S(1)} %collective-permute-done.12.refs_2_, ...), custom_call_target="tpu_custom_call", output_to_operand_aliasing={{2}: (9, {})} | custom-call | flops 1 | bytes 23750656 | tf_op jit(solution)/shard_map/F2B/pallas_call | solution.py:259
  65.1 1.6 collective-permute-done.14.refs_3_
  67.3 1.5 collective-permute-start.15
  68.7 1.3 collective-permute-start.16
  72.8 5.8 %F3A.1 = (bf16[64,4096]{1,0:T(8,128)(2,1)S(1)}, bf16[40,4096]{1,0:T(8,128)(2,1)S(1)}, f32[8,128]{1,0:T(8,128)S(1)}) custom-call(s32[6]{0:T(128)S(1)} %stack.31.refs_0_, bf16[64,4224]{1,0:T(8,128)(2,1)S(1)} %get-tuple-element.143.refs_1_, bf16[40,4224]{1,0:T(8,128)(2,1)S(1)} %get-tuple-element.144.refs_2_, ...), custom_call_target="tpu_custom_call", output_to_operand_aliasing={{2}: (9, {})} | custom-call | flops 1 | bytes 23750656 | tf_op jit(solution)/shard_map/F3A/pallas_call | solution.py:259
  80.3 5.2 %collective-permute-start.21 = (bf16[64,4096]{1,0:T(8,128)(2,1)S(1)}, bf16[64,4096]{1,0:T(8,128)(2,1)S(1)}, u32[]{:S(2)}, u32[]{:S(2)}) collective-permute-start(bf16[64,4096]{1,0:T(8,128)(2,1)S(1)} %get-tuple-element.165), channel_id=1, source_target_pairs={{0,4},{1,5},{2,6},{3,7},{12,8},{13,9},{14,10},{15,11},{16,20},{17,... | collective-permute-start | bytes 1572872 | tf_op jit(solution)/shard_map/move_I2B/ppermute | solution.py:73
  86.8 1.9 %collective-permute-start.20 = (bf16[40,4224]{1,0:T(8,128)(2,1)S(1)}, bf16[40,4224]{1,0:T(8,128)(2,1)S(1)}, u32[]{:S(2)}, u32[]{:S(2)}) collective-permute-start(bf16[40,4224]{1,0:T(8,128)(2,1)S(1)} %get-tuple-element.163), channel_id=1, source_target_pairs={{0,2},{1,3},{2,0},{3,1},{4,6},{5,7},{6,4},{7,5},{8,10},{9,11},{10,... | collective-permute-start | bytes 1013768 | tf_op jit(solution)/shard_map/move_Y3B/ppermute | solution.py:16
  88.7 5.9 %F1.1 = (bf16[64,4096]{1,0:T(8,128)(2,1)S(1)}, bf16[64,4096]{1,0:T(8,128)(2,1)S(1)}, f32[8,128]{1,0:T(8,128)S(1)}, bf16[40,4096]{1,0:T(8,128)(2,1)S(1)}) custom-call(s32[6]{0:T(128)S(1)} %stack.31.refs_0_, bf16[64,4224]{1,0:T(8,128)(2,1)S(1)} %get-tuple-element.128.refs_1_, ...), custom_call_target="tpu_custom_call", output_to_operand_aliasing={{2}: (9, {}), {3}: (10, {})} | custom-call | flops 1 | bytes 24150016 | tf_op jit(solution)/shard_map/F1/pallas_call | solution.py:259
  94.8 1.3 collective-permute-done.20.refs_2_
  96.2 5.8 %F3B.1 = (bf16[64,4096]{1,0:T(8,128)(2,1)S(1)}, bf16[40,4096]{1,0:T(8,128)(2,1)S(1)}, f32[8,128]{1,0:T(8,128)S(1)}, bf16[64,4096]{1,0:T(8,128)(2,1)S(1)}) custom-call(s32[6]{0:T(128)S(1)} %stack.31.refs_0_, bf16[64,4224]{1,0:T(8,128)(2,1)S(1)} %get-tuple-element.162.refs_1_, ...), custom_call_target="tpu_custom_call", output_to_operand_aliasing={{2}: (9, {}), {3}: (10, {})} | custom-call | flops 1 | bytes 23750656 | tf_op jit(solution)/shard_map/F3B/pallas_call | solution.py:259
  102.8 2.6 %collective-permute-start.22 = (bf16[40,4096]{1,0:T(8,128)(2,1)S(1)}, bf16[40,4096]{1,0:T(8,128)(2,1)S(1)}, u32[]{:S(2)}, u32[]{:S(2)}) collective-permute-start(bf16[40,4096]{1,0:T(8,128)(2,1)S(1)} %get-tuple-element.175), channel_id=1, source_target_pairs={{0,2},{1,3},{2,0},{3,1},{4,6},{5,7},{6,4},{7,5},{8,10},{9,11},{10,... | collective-permute-start | bytes 983048 | tf_op jit(solution)/shard_map/move_R3B/ppermute | solution.py:16
  106.3 1.9 %collective-permute-start.24 = (bf16[64,4096]{1,0:T(8,128)(2,1)S(1)}, bf16[64,4096]{1,0:T(8,128)(2,1)S(1)}, u32[]{:S(2)}, u32[]{:S(2)}) collective-permute-start(bf16[64,4096]{1,0:T(8,128)(2,1)S(1)} %get-tuple-element.180), channel_id=1, source_target_pairs={{0,4},{1,5},{2,6},{3,7},{12,8},{13,9},{14,10},{15,11},{16,20},{17,... | collective-permute-start | bytes 1572872 | tf_op jit(solution)/shard_map/move_I3A/ppermute | solution.py:73
  109.1 5.8 %F2A.1 = (bf16[64,4096]{1,0:T(8,128)(2,1)S(1)}, bf16[40,4096]{1,0:T(8,128)(2,1)S(1)}, f32[8,128]{1,0:T(8,128)S(1)}) custom-call(s32[6]{0:T(128)S(1)} %stack.31.refs_0_, bf16[64,4224]{1,0:T(8,128)(2,1)S(1)} %get-tuple-element.157.refs_1_, bf16[40,4224]{1,0:T(8,128)(2,1)S(1)} %get-tuple-element.158.refs_2_, ...), custom_call_target="tpu_custom_call", output_to_operand_aliasing={{2}: (9, {})} | custom-call | flops 1 | bytes 23750656 | tf_op jit(solution)/shard_map/F2A/pallas_call | solution.py:259
  115.8 4.1 %collective-permute-start.28 = (bf16[64,4096]{1,0:T(8,128)(2,1)S(1)}, bf16[64,4096]{1,0:T(8,128)(2,1)S(1)}, u32[]{:S(2)}, u32[]{:S(2)}) collective-permute-start(bf16[64,4096]{1,0:T(8,128)(2,1)S(1)} %get-tuple-element.187), channel_id=1, source_target_pairs={{0,4},{1,5},{2,6},{3,7},{12,8},{13,9},{14,10},{15,11},{16,20},{17,... | collective-permute-start | bytes 1572872 | tf_op jit(solution)/shard_map/move_I3B/ppermute | solution.py:73
  121.6 8.8 %collective-permute-done.23.refs_3_.refs_6_ = bf16[40,4096]{1,0:T(8,128)(2,1)S(1)} collective-permute-done((bf16[40,4096]{1,0:T(8,128)(2,1)S(1)}, bf16[40,4096]{1,0:T(8,128)(2,1)S(1)}, u32[]{:S(2)}, u32[]{:S(2)}) %collective-permute-start.23) | collective-permute-done | bytes 327712 | tf_op jit(solution)/shard_map/move_R2A/ppermute | solution.py:16
  131.3 1.3 collective-permute-start.31
  134.2 10.5 %collective-permute-done.26.refs_3_.refs_6_ = bf16[64,4096]{1,0:T(8,128)(2,1)S(1)} collective-permute-done((bf16[64,4096]{1,0:T(8,128)(2,1)S(1)}, bf16[64,4096]{1,0:T(8,128)(2,1)S(1)}, u32[]{:S(2)}, u32[]{:S(2)}) %collective-permute-start.26) | collective-permute-done | bytes 524320 | tf_op jit(solution)/shard_map/move_R1/ppermute | solution.py:16
  148.5 3.6 %collective-permute-start.34 = (bf16[64,4096]{1,0:T(8,128)(2,1)S(1)}, bf16[64,4096]{1,0:T(8,128)(2,1)S(1)}, u32[]{:S(2)}, u32[]{:S(2)}) collective-permute-start(bf16[64,4096]{1,0:T(8,128)(2,1)S(1)} %get-tuple-element.201), channel_id=1, source_target_pairs={{0,4},{1,5},{2,6},{3,7},{4,0},{5,1},{6,2},{7,3},{8,12},{9,13},{10,... | collective-permute-start | bytes 1572872 | tf_op jit(solution)/shard_map/move_S1B/ppermute | solution.py:73
  152.1 2.9 %collective-permute-done.29.refs_4_ = bf16[64,4096]{1,0:T(8,128)(2,1)S(1)} collective-permute-done((bf16[64,4096]{1,0:T(8,128)(2,1)S(1)}, bf16[64,4096]{1,0:T(8,128)(2,1)S(1)}, u32[]{:S(2)}, u32[]{:S(2)}) %collective-permute-start.29) | collective-permute-done | bytes 524320 | tf_op jit(solution)/shard_map/move_R0/ppermute | solution.py:16
  156.2 5.6 %collective-permute-done.34.refs_7_ = bf16[64,4096]{1,0:T(8,128)(2,1)S(1)} collective-permute-done((bf16[64,4096]{1,0:T(8,128)(2,1)S(1)}, bf16[64,4096]{1,0:T(8,128)(2,1)S(1)}, u32[]{:S(2)}, u32[]{:S(2)}) %collective-permute-start.34) | collective-permute-done | bytes 524320 | tf_op jit(solution)/shard_map/move_S1B/ppermute | solution.py:73
  161.8 2.4 %fin.1 = (bf16[128,4096]{1,0:T(8,128)(2,1)}, f32[8,128]{1,0:T(8,128)S(1)}) custom-call(s32[6]{0:T(128)S(1)} %stack.31.refs_0_, bf16[128,128]{1,0:T(8,128)(2,1)S(1)} %get-tuple-element.105.refs_1_, bf16[128,128]{1,0:T(8,128)(2,1)S(1)} %get-tuple-element.109.refs_2_, bf16[64,4096]{1,0:T(8,128)(2,1)S(1)} %get-tuple-element.126.refs_3_, ...), custom_call_target="tpu_custom_call", output_to_operand_aliasing={{1}: (9, {})} | custom-call | flops 1 | bytes 1 | tf_op jit(solution)/shard_map/fin/pallas_call | solution.py:259
  (75 shorter events, 34.1 us)
Async XLA Ops:
  0.0 22.9 %collective-permute-start.3 = (bf16[448,4096]{1,0:T(8,128)(2,1)}, bf16[448,4096]{1,0:T(8,128)(2,1)}, u32[]{:S(2)}, u32[]{:S(2)}) collective-permute-start(bf16[448,4096]{1,0:T(8,128)(2,1)} %bitcast.10), channel_id=1, source_target_pairs={{0,1},{1,0},{2,3},{3,2},{4,5},{5,4},{6,7},{7,6},{8,9},{9,8},{10,11... | collective-permute-start | bytes 11010056 | tf_op jit(solution)/shard_map/move_wg/ppermute | solution.py:16
  0.5 22.5 %collective-permute-start.4 = (bf16[448,4096]{1,0:T(8,128)(2,1)}, bf16[448,4096]{1,0:T(8,128)(2,1)}, u32[]{:S(2)}, u32[]{:S(2)}) collective-permute-start(bf16[448,4096]{1,0:T(8,128)(2,1)} %bitcast.17), channel_id=1, source_target_pairs={{0,1},{1,0},{2,3},{3,2},{4,5},{5,4},{6,7},{7,6},{8,9},{9,8},{10,11... | collective-permute-start | bytes 11010056 | tf_op jit(solution)/shard_map/move_wu/ppermute | solution.py:16
  0.5 25.9 %collective-permute-start.5 = (bf16[896,2048]{1,0:T(8,128)(2,1)}, bf16[896,2048]{1,0:T(8,128)(2,1)}, u32[]{:S(2)}, u32[]{:S(2)}) collective-permute-start(bf16[896,2048]{1,0:T(8,128)(2,1)} %refs_7_.11), channel_id=1, source_target_pairs={{0,1},{1,0},{2,3},{3,2},{4,5},{5,4},{6,7},{7,6},{8,9},{9,8},{10,11... | collective-permute-start | bytes 11010056 | tf_op jit(solution)/shard_map/move_wd/ppermute | solution.py:16
  3.7 15.6 %collective-permute-start = (bf16[64,4224]{1,0:T(8,128)(2,1)S(1)}, bf16[64,4224]{1,0:T(8,128)(2,1)S(1)}, u32[]{:S(2)}, u32[]{:S(2)}) collective-permute-start(bf16[64,4224]{1,0:T(8,128)(2,1)S(1)} %get-tuple-element.106.refs_1_.refs_2_), channel_id=1, source_target_pairs={{0,4},{1,5},{2,6},{3,7},{4,0},{5,1},{6,2},{7,3},{8,12},{9,13},{10,... | collective-permute-start | bytes 1622024 | tf_op jit(solution)/shard_map/move_EA/ppermute | solution.py:73
  6.3 15.9 %collective-permute-start.2 = (bf16[64,4224]{1,0:T(8,128)(2,1)S(1)}, bf16[64,4224]{1,0:T(8,128)(2,1)S(1)}, u32[]{:S(2)}, u32[]{:S(2)}) collective-permute-start(bf16[64,4224]{1,0:T(8,128)(2,1)S(1)} %get-tuple-element.107.refs_2_), channel_id=1, source_target_pairs={{4,8},{5,9},{6,10},{7,11},{8,4},{9,5},{10,6},{11,7},{20,24},{21,25... | collective-permute-start | bytes 1622024 | tf_op jit(solution)/shard_map/move_MB/ppermute | solution.py:73
  19.2 15.2 %collective-permute-start.7 = (bf16[64,4224]{1,0:T(8,128)(2,1)S(1)}, bf16[64,4224]{1,0:T(8,128)(2,1)S(1)}, u32[]{:S(2)}, u32[]{:S(2)}) collective-permute-start(bf16[64,4224]{1,0:T(8,128)(2,1)S(1)} %get-tuple-element.107.refs_2_), channel_id=1, source_target_pairs={{0,4},{1,5},{2,6},{3,7},{4,0},{5,1},{6,2},{7,3},{8,12},{9,13},{10,... | collective-permute-start | bytes 1622024 | tf_op jit(solution)/shard_map/move_EB/ppermute | solution.py:73
  22.2 12.2 %collective-permute-start.8 = (bf16[64,4224]{1,0:T(8,128)(2,1)S(1)}, bf16[64,4224]{1,0:T(8,128)(2,1)S(1)}, u32[]{:S(2)}, u32[]{:S(2)}) collective-permute-start(bf16[64,4224]{1,0:T(8,128)(2,1)S(1)} %get-tuple-element.120.refs_1_), channel_id=1, source_target_pairs={{4,8},{5,9},{6,10},{7,11},{8,4},{9,5},{10,6},{11,7},{20,24},{21,25... | collective-permute-start | bytes 1622024 | tf_op jit(solution)/shard_map/move_NA/ppermute | solution.py:73
  23.5 22.5 %collective-permute-start.6 = (bf16[64,4224]{1,0:T(8,128)(2,1)S(1)}, bf16[64,4224]{1,0:T(8,128)(2,1)S(1)}, u32[]{:S(2)}, u32[]{:S(2)}) collective-permute-start(bf16[64,4224]{1,0:T(8,128)(2,1)S(1)} %get-tuple-element.119.refs_1_), channel_id=1, source_target_pairs={{4,0},{5,1},{6,2},{7,3},{8,12},{9,13},{10,14},{11,15},{20,16},{21,... | collective-permute-start | bytes 1622024 | tf_op jit(solution)/shard_map/move_OB/ppermute | solution.py:73
  24.8 23.1 %collective-permute-start.1 = (bf16[64,4224]{1,0:T(8,128)(2,1)S(1)}, bf16[64,4224]{1,0:T(8,128)(2,1)S(1)}, u32[]{:S(2)}, u32[]{:S(2)}) collective-permute-start(bf16[64,4224]{1,0:T(8,128)(2,1)S(1)} %get-tuple-element.111), channel_id=1, source_target_pairs={{0,2},{1,3},{2,0},{3,1},{4,6},{5,7},{6,4},{7,5},{8,10},{9,11},{10,... | collective-permute-start | bytes 1622024 | tf_op jit(solution)/shard_map/move_Y0/ppermute | solution.py:16
  32.0 17.7 %collective-permute-start.9 = (bf16[64,4224]{1,0:T(8,128)(2,1)S(1)}, bf16[64,4224]{1,0:T(8,128)(2,1)S(1)}, u32[]{:S(2)}, u32[]{:S(2)}) collective-permute-start(bf16[64,4224]{1,0:T(8,128)(2,1)S(1)} %get-tuple-element.125), channel_id=1, source_target_pairs={{4,8},{5,9},{6,10},{7,11},{8,4},{9,5},{10,6},{11,7},{20,24},{21,25... | collective-permute-start | bytes 1622024 | tf_op jit(solution)/shard_map/move_MA/ppermute | solution.py:73
  35.6 21.2 %collective-permute-start.10 = (bf16[64,4224]{1,0:T(8,128)(2,1)S(1)}, bf16[64,4224]{1,0:T(8,128)(2,1)S(1)}, u32[]{:S(2)}, u32[]{:S(2)}) collective-permute-start(bf16[64,4224]{1,0:T(8,128)(2,1)S(1)} %get-tuple-element.129.refs_1_), channel_id=1, source_target_pairs={{4,0},{5,1},{6,2},{7,3},{8,12},{9,13},{10,14},{11,15},{20,16},{21,... | collective-permute-start | bytes 1622024 | tf_op jit(solution)/shard_map/move_QA/ppermute | solution.py:73
  36.9 20.0 %collective-permute-start.11 = (bf16[64,4224]{1,0:T(8,128)(2,1)S(1)}, bf16[64,4224]{1,0:T(8,128)(2,1)S(1)}, u32[]{:S(2)}, u32[]{:S(2)}) collective-permute-start(bf16[64,4224]{1,0:T(8,128)(2,1)S(1)} %get-tuple-element.131), channel_id=1, source_target_pairs={{0,2},{1,3},{2,0},{3,1},{4,6},{5,7},{6,4},{7,5},{8,10},{9,11},{10,... | collective-permute-start | bytes 1622024 | tf_op jit(solution)/shard_map/move_Y1/ppermute | solution.py:16
  47.2 19.5 %collective-permute-start.13 = (bf16[64,4224]{1,0:T(8,128)(2,1)S(1)}, bf16[64,4224]{1,0:T(8,128)(2,1)S(1)}, u32[]{:S(2)}, u32[]{:S(2)}) collective-permute-start(bf16[64,4224]{1,0:T(8,128)(2,1)S(1)} %get-tuple-element.137), channel_id=1, source_target_pairs={{4,8},{5,9},{6,10},{7,11},{8,4},{9,5},{10,6},{11,7},{20,24},{21,25... | collective-permute-start | bytes 1622024 | tf_op jit(solution)/shard_map/move_NB/ppermute | solution.py:73
  47.9 11.4 %collective-permute-start.12 = (bf16[40,4224]{1,0:T(8,128)(2,1)S(1)}, bf16[40,4224]{1,0:T(8,128)(2,1)S(1)}, u32[]{:S(2)}, u32[]{:S(2)}) collective-permute-start(bf16[40,4224]{1,0:T(8,128)(2,1)S(1)} %get-tuple-element.134), channel_id=1, source_target_pairs={{0,2},{1,3},{2,0},{3,1},{4,6},{5,7},{6,4},{7,5},{8,10},{9,11},{10,... | collective-permute-start | bytes 1013768 | tf_op jit(solution)/shard_map/move_Y2B/ppermute | solution.py:16
  55.6 14.5 %collective-permute-start.17 = (bf16[64,4224]{1,0:T(8,128)(2,1)S(1)}, bf16[64,4224]{1,0:T(8,128)(2,1)S(1)}, u32[]{:S(2)}, u32[]{:S(2)}) collective-permute-start(bf16[64,4224]{1,0:T(8,128)(2,1)S(1)} %get-tuple-element.145.refs_1_), channel_id=1, source_target_pairs={{4,0},{5,1},{6,2},{7,3},{8,12},{9,13},{10,14},{11,15},{20,16},{21,... | collective-permute-start | bytes 1622024 | tf_op jit(solution)/shard_map/move_OA/ppermute | solution.py:73
  67.3 18.3 %collective-permute-start.15 = (bf16[64,4224]{1,0:T(8,128)(2,1)S(1)}, bf16[64,4224]{1,0:T(8,128)(2,1)S(1)}, u32[]{:S(2)}, u32[]{:S(2)}) collective-permute-start(bf16[64,4224]{1,0:T(8,128)(2,1)S(1)} %get-tuple-element.139.refs_1_), channel_id=1, source_target_pairs={{4,0},{5,1},{6,2},{7,3},{8,12},{9,13},{10,14},{11,15},{20,16},{21,... | collective-permute-start | bytes 1622024 | tf_op jit(solution)/shard_map/move_QB/ppermute | solution.py:73
  68.7 10.7 %collective-permute-start.16 = (bf16[40,4096]{1,0:T(8,128)(2,1)S(1)}, bf16[40,4096]{1,0:T(8,128)(2,1)S(1)}, u32[]{:S(2)}, u32[]{:S(2)}) collective-permute-start(bf16[40,4096]{1,0:T(8,128)(2,1)S(1)} %get-tuple-element.142), channel_id=1, source_target_pairs={{0,2},{1,3},{2,0},{3,1},{4,6},{5,7},{6,4},{7,5},{8,10},{9,11},{10,... | collective-permute-start | bytes 983048 | tf_op jit(solution)/shard_map/move_R2B/ppermute | solution.py:16
  71.8 13.7 %collective-permute-start.18 = (bf16[40,4224]{1,0:T(8,128)(2,1)S(1)}, bf16[40,4224]{1,0:T(8,128)(2,1)S(1)}, u32[]{:S(2)}, u32[]{:S(2)}) collective-permute-start(bf16[40,4224]{1,0:T(8,128)(2,1)S(1)} %get-tuple-element.152), channel_id=1, source_target_pairs={{0,2},{1,3},{2,0},{3,1},{4,6},{5,7},{6,4},{7,5},{8,10},{9,11},{10,... | collective-permute-start | bytes 1013768 | tf_op jit(solution)/shard_map/move_Y2A/ppermute | solution.py:16
  80.3 14.5 %collective-permute-start.21 = (bf16[64,4096]{1,0:T(8,128)(2,1)S(1)}, bf16[64,4096]{1,0:T(8,128)(2,1)S(1)}, u32[]{:S(2)}, u32[]{:S(2)}) collective-permute-start(bf16[64,4096]{1,0:T(8,128)(2,1)S(1)} %get-tuple-element.165), channel_id=1, source_target_pairs={{0,4},{1,5},{2,6},{3,7},{12,8},{13,9},{14,10},{15,11},{16,20},{17,... | collective-permute-start | bytes 1572872 | tf_op jit(solution)/shard_map/move_I2B/ppermute | solution.py:73
  86.8 9.4 %collective-permute-start.20 = (bf16[40,4224]{1,0:T(8,128)(2,1)S(1)}, bf16[40,4224]{1,0:T(8,128)(2,1)S(1)}, u32[]{:S(2)}, u32[]{:S(2)}) collective-permute-start(bf16[40,4224]{1,0:T(8,128)(2,1)S(1)} %get-tuple-element.163), channel_id=1, source_target_pairs={{0,2},{1,3},{2,0},{3,1},{4,6},{5,7},{6,4},{7,5},{8,10},{9,11},{10,... | collective-permute-start | bytes 1013768 | tf_op jit(solution)/shard_map/move_Y3B/ppermute | solution.py:16
  94.5 10.8 %collective-permute-start.19 = (bf16[40,4096]{1,0:T(8,128)(2,1)S(1)}, bf16[40,4096]{1,0:T(8,128)(2,1)S(1)}, u32[]{:S(2)}, u32[]{:S(2)}) collective-permute-start(bf16[40,4096]{1,0:T(8,128)(2,1)S(1)} %get-tuple-element.161), channel_id=1, source_target_pairs={{0,2},{1,3},{2,0},{3,1},{4,6},{5,7},{6,4},{7,5},{8,10},{9,11},{10,... | collective-permute-start | bytes 983048 | tf_op jit(solution)/shard_map/move_R3A/ppermute | solution.py:16
  102.8 12.1 %collective-permute-start.22 = (bf16[40,4096]{1,0:T(8,128)(2,1)S(1)}, bf16[40,4096]{1,0:T(8,128)(2,1)S(1)}, u32[]{:S(2)}, u32[]{:S(2)}) collective-permute-start(bf16[40,4096]{1,0:T(8,128)(2,1)S(1)} %get-tuple-element.175), channel_id=1, source_target_pairs={{0,2},{1,3},{2,0},{3,1},{4,6},{5,7},{6,4},{7,5},{8,10},{9,11},{10,... | collective-permute-start | bytes 983048 | tf_op jit(solution)/shard_map/move_R3B/ppermute | solution.py:16
  106.3 13.7 %collective-permute-start.24 = (bf16[64,4096]{1,0:T(8,128)(2,1)S(1)}, bf16[64,4096]{1,0:T(8,128)(2,1)S(1)}, u32[]{:S(2)}, u32[]{:S(2)}) collective-permute-start(bf16[64,4096]{1,0:T(8,128)(2,1)S(1)} %get-tuple-element.180), channel_id=1, source_target_pairs={{0,4},{1,5},{2,6},{3,7},{12,8},{13,9},{14,10},{15,11},{16,20},{17,... | collective-permute-start | bytes 1572872 | tf_op jit(solution)/shard_map/move_I3A/ppermute | solution.py:73
  108.2 13.4 %collective-permute-start.25 = (bf16[64,4096]{1,0:T(8,128)(2,1)S(1)}, bf16[64,4096]{1,0:T(8,128)(2,1)S(1)}, u32[]{:S(2)}, u32[]{:S(2)}) collective-permute-start(bf16[64,4096]{1,0:T(8,128)(2,1)S(1)} %get-tuple-element.183), channel_id=1, source_target_pairs={{4,8},{5,9},{6,10},{7,11},{8,4},{9,5},{10,6},{11,7},{20,24},{21,25... | collective-permute-start | bytes 1572872 | tf_op jit(solution)/shard_map/move_S2B/ppermute | solution.py:73
  115.8 16.8 %collective-permute-start.28 = (bf16[64,4096]{1,0:T(8,128)(2,1)S(1)}, bf16[64,4096]{1,0:T(8,128)(2,1)S(1)}, u32[]{:S(2)}, u32[]{:S(2)}) collective-permute-start(bf16[64,4096]{1,0:T(8,128)(2,1)S(1)} %get-tuple-element.187), channel_id=1, source_target_pairs={{0,4},{1,5},{2,6},{3,7},{12,8},{13,9},{14,10},{15,11},{16,20},{17,... | collective-permute-start | bytes 1572872 | tf_op jit(solution)/shard_map/move_I3B/ppermute | solution.py:73
  119.9 10.4 %collective-permute-start.23 = (bf16[40,4096]{1,0:T(8,128)(2,1)S(1)}, bf16[40,4096]{1,0:T(8,128)(2,1)S(1)}, u32[]{:S(2)}, u32[]{:S(2)}) collective-permute-start(bf16[40,4096]{1,0:T(8,128)(2,1)S(1)} %get-tuple-element.178), channel_id=1, source_target_pairs={{0,2},{1,3},{2,0},{3,1},{4,6},{5,7},{6,4},{7,5},{8,10},{9,11},{10,... | collective-permute-start | bytes 983048 | tf_op jit(solution)/shard_map/move_R2A/ppermute | solution.py:16
  120.9 13.3 %collective-permute-start.27 = (bf16[64,4096]{1,0:T(8,128)(2,1)S(1)}, bf16[64,4096]{1,0:T(8,128)(2,1)S(1)}, u32[]{:S(2)}, u32[]{:S(2)}) collective-permute-start(bf16[64,4096]{1,0:T(8,128)(2,1)S(1)} %get-tuple-element.186), channel_id=1, source_target_pairs={{4,8},{5,9},{6,10},{7,11},{8,4},{9,5},{10,6},{11,7},{20,24},{21,25... | collective-permute-start | bytes 1572872 | tf_op jit(solution)/shard_map/move_S3A/ppermute | solution.py:73
  131.2 13.5 %collective-permute-start.26 = (bf16[64,4096]{1,0:T(8,128)(2,1)S(1)}, bf16[64,4096]{1,0:T(8,128)(2,1)S(1)}, u32[]{:S(2)}, u32[]{:S(2)}) collective-permute-start(bf16[64,4096]{1,0:T(8,128)(2,1)S(1)} %get-tuple-element.185), channel_id=1, source_target_pairs={{0,2},{1,3},{2,0},{3,1},{4,6},{5,7},{6,4},{7,5},{8,10},{9,11},{10,... | collective-permute-start | bytes 1572872 | tf_op jit(solution)/shard_map/move_R1/ppermute | solution.py:16
  131.3 14.6 %collective-permute-start.31 = (bf16[64,4096]{1,0:T(8,128)(2,1)S(1)}, bf16[64,4096]{1,0:T(8,128)(2,1)S(1)}, u32[]{:S(2)}, u32[]{:S(2)}) collective-permute-start(bf16[64,4096]{1,0:T(8,128)(2,1)S(1)} %get-tuple-element.194), channel_id=1, source_target_pairs={{0,4},{1,5},{2,6},{3,7},{12,8},{13,9},{14,10},{15,11},{16,20},{17,... | collective-permute-start | bytes 1572872 | tf_op jit(solution)/shard_map/move_I2A/ppermute | solution.py:73
  133.5 13.3 %collective-permute-start.32 = (bf16[64,4096]{1,0:T(8,128)(2,1)S(1)}, bf16[64,4096]{1,0:T(8,128)(2,1)S(1)}, u32[]{:S(2)}, u32[]{:S(2)}) collective-permute-start(bf16[64,4096]{1,0:T(8,128)(2,1)S(1)} %get-tuple-element.197), channel_id=1, source_target_pairs={{4,8},{5,9},{6,10},{7,11},{8,4},{9,5},{10,6},{11,7},{20,24},{21,25... | collective-permute-start | bytes 1572872 | tf_op jit(solution)/shard_map/move_S3B/ppermute | solution.py:73
  145.9 10.3 %collective-permute-start.30 = (bf16[64,4096]{1,0:T(8,128)(2,1)S(1)}, bf16[64,4096]{1,0:T(8,128)(2,1)S(1)}, u32[]{:S(2)}, u32[]{:S(2)}) collective-permute-start(bf16[64,4096]{1,0:T(8,128)(2,1)S(1)} %get-tuple-element.192), channel_id=1, source_target_pairs={{0,4},{1,5},{2,6},{3,7},{4,0},{5,1},{6,2},{7,3},{8,12},{9,13},{10,... | collective-permute-start | bytes 1572872 | tf_op jit(solution)/shard_map/move_S1A/ppermute | solution.py:73
  148.5 13.2 %collective-permute-start.34 = (bf16[64,4096]{1,0:T(8,128)(2,1)S(1)}, bf16[64,4096]{1,0:T(8,128)(2,1)S(1)}, u32[]{:S(2)}, u32[]{:S(2)}) collective-permute-start(bf16[64,4096]{1,0:T(8,128)(2,1)S(1)} %get-tuple-element.201), channel_id=1, source_target_pairs={{0,4},{1,5},{2,6},{3,7},{4,0},{5,1},{6,2},{7,3},{8,12},{9,13},{10,... | collective-permute-start | bytes 1572872 | tf_op jit(solution)/shard_map/move_S1B/ppermute | solution.py:73
  (6 other events, 91.0 us)

commit v3 on v2

--- a/solution.py
+++ b/solution.py
@@ -242,6 +242,12 @@
         c.wait()
 
 
+def copy_kernel(idx, source, to, sem):
+    copy = pltpu.make_async_copy(source, to, sem)
+    copy.start()
+    copy.wait()
+
+
 def fetch_kernel(idx, *refs):
     count = len(refs) // 2
     run_copies(refs[-1], zip(refs[:count], refs[count:-1]))
@@ -275,23 +281,25 @@
 
 ORDER = [
     ["prep", "EA", "MB", "EB"],
-    ["P0", "NA", "Y0"],
-    ["f", "OB", "+wg", "+wu"],
+    ["V"],
+    ["P0"],
+    ["f", "NA", "Y0", "OB", "wd", "+wu"],
     ["W"],
     ["f", "MA"],
     ["P1", "Y1", "QA"],
     ["P2B", "Y2B", "NB"],
-    ["F0", "OA"],
+    ["F0", "OA", "+OB"],
     ["P3A", "Y3A", "+Y1"],
-    ["F2B", "R2B"],
-    ["f", "QB", "+Y3A"],
-    ["P2A"],
+    ["F2B", "QB", "R2B"],
+    ["f", "+Y3A"],
+    ["P2A", "+Y2B"],
     ["f", "Y2A"],
     ["F3A"],
     ["C2B", "I2B"],
-    ["P3B", "Y3B", "+Y2A"],
+    ["P3B"],
+    ["f", "Y3B", "+Y2A"],
     ["F1", "R3A"],
-    ["F3B", "+I2B"],
+    ["F3B"],
     ["D2B", "R3B"],
     ["C3A", "I3A", "S2B"],
     ["F2A"],
@@ -300,8 +308,8 @@
     ["C2A", "R1", "I2A", "+S2B"],
     ["D3B", "S3B", "+R2A"],
     ["D1A", "S1A", "R0"],
-    ["D2A", "+R1"],
-    ["D1B", "S2A", "S1B", "+I2A"],
+    ["D2A", "+R1", "S2A"],
+    ["D1B", "S1B"],
     ["fin"],
 ]
 
@@ -332,7 +340,7 @@
     gate, up = gate_weight.T, up_weight.T
 
     val = {}
-    for name, w in (("wg", gate), ("wu", up), ("wd", down_weight)):
+    for name, w in (("wg", gate), ("wu", up)):
         with jax.named_scope("move_" + name):
             val[name] = swapped(w, "expert", 0)
     steps = {name for name, *_ in ORDER}
@@ -373,6 +381,8 @@
                 args,
                 [pltpu.VMEM((2, own.shape[0] + cross.shape[0], half), bf16)],
             )
+        if name == "V":
+            return copy_kernel, [like(*down_weight.shape)], [], [pltpu.SemaphoreType.DMA]
         if name == "W":
             outs = [pltpu.VMEM(w.shape, bf16) for w in (gate, up, down_weight)]
             return fetch_kernel, outs, [], [pltpu.SemaphoreType.DMA((3,))]
@@ -395,6 +405,8 @@
             val["payA"], val["payB"], val["order"] = got
         elif name[0] == "P":
             val["own" + slot], val["cross" + slot], val["pick" + slot] = got
+        elif name == "V":
+            val["down"] = got[0]
         elif name == "W":
             val["vg"], val["vu"], val["vd"] = got
         elif name[0] == "F":
@@ -404,6 +416,8 @@
 
     def move_of(name):
         kind, slot, q = name[0], name[1:], name[-1]
+        if name == "wd":
+            return "down", lambda x: swapped(x, "expert", 0)
         if kind == "Y":
             return "cross" + slot, lambda x: swapped(x, "expert", 1)
         if kind == "R":
@@ -435,8 +449,10 @@
             kernel, outs, args, scratch = kernel_of(name)
             cost = sum(x.size * x.dtype.itemsize for x in [*args, *outs]) if name[0] == "F" else 1
             through = [val[s] for s in passed]
-            left = {"prep": [in_hbm(tokens)], "W": [val["wg"], val["wu"], val["wd"]]}.get(name, [])
-            got, token, through = call(name, kernel, outs, idx, token, args, through, scratch, cost, left, name == "fin")
+            left = {"prep": [in_hbm(tokens)], "V": [in_hbm(down_weight)]}.get(name, [])
+            if name == "W":
+                left = [val["wg"], val["wu"], val["wd"]]
+            got, token, through = call(name, kernel, outs, idx, token, args, through, scratch, cost, left, name in ("V", "fin"))
             keep(name, got)
         val.update(zip(passed, through))
         for m in moves:

time: 165 us -> 166 us (level)
  starting transfers between devices: 46.2 us -> 52.8 us
  waiting for transfers between devices: 54 us -> 47.6 us
    ppermute x15, waiting for transfers between devices: 26.1 us -> 13.8 us  [swapped(): lax.ppermute(x, axis, [(i, i ^ 1 << apart) for i in range(lax.axis_size(a...]
    ppermute x20, waiting for transfers between devices: 27.9 us -> 33.8 us  [along_line(): return lax.ppermute(x, 'expert', moves)]
    ppermute x20, starting transfers between devices: 31.8 us -> 35.2 us  [along_line(): return lax.ppermute(x, 'expert', moves)]
    ppermute x15, starting transfers between devices: 14.4 us -> 17.6 us  [swapped(): lax.ppermute(x, axis, [(i, i ^ 1 << apart) for i in range(lax.axis_size(a...]
    pallas_call x29 -> x31, Pallas kernels: 63.4 us -> 64.7 us  [call(): pl.pallas_call(body, out_shape=[*outs, *(jax.ShapeDtypeStruct(x.shape, x....]
  transfers between devices with their start and end apart: 35 -> 35, of which waited for: 11 -> 12; matrix products, arithmetic and copies ran while one was open for 0% -> 0% of each run, Pallas kernels for 37% -> 38%
where the time goes in v3:
time: 166 us
  Pallas kernels  64.7 us (39%)
  starting transfers between devices  52.8 us (32%)
  waiting for transfers between devices  47.6 us (29%)
    pallas_call x31, Pallas kernels, call(): pl.pallas_call(body, out_shape=[*outs, *(jax.ShapeDtypeStruct(x.shape, x....  64.7 us
    ppermute x20, starting transfers between devices, along_line(): return lax.ppermute(x, 'expert', moves)  35.2 us
    ppermute x20, waiting for transfers between devices, along_line(): return lax.ppermute(x, 'expert', moves)  33.8 us
    ppermute x15, starting transfers between devices, swapped(): lax.ppermute(x, axis, [(i, i ^ 1 << apart) for i in range(lax.axis_size(a...  17.6 us
    ppermute x15, waiting for transfers between devices, swapped(): lax.ppermute(x, axis, [(i, i ^ 1 << apart) for i in range(lax.axis_size(a...  13.8 us
  transfers between devices with their start and end apart: 35, of which 12 were waited for; matrix products, arithmetic and copies ran while one was open for 0% of the time, Pallas kernels for 38%

profile of v3, /device:TPU:0, one launch (start us, length us, event | category | flops | bytes accessed | tf_op | source)
XLA Modules:
  0.0 165.9 jit_solution(7049775835511510671)
XLA Ops:
  0.5 2.6 %prep.1 = (bf16[64,4224]{1,0:T(8,128)(2,1)S(1)}, bf16[64,4224]{1,0:T(8,128)(2,1)S(1)}, bf16[128,128]{1,0:T(8,128)(2,1)S(1)}, f32[8,128]{1,0:T(8,128)S(1)}) custom-call(s32[6]{0:T(128)S(1)} %stack.31.refs_0_, s32[4,128]{1,0:T(4,128)} %bitcast.24, f32[4,128]{1,0:T(4,128)} %bitcast.25, bf16[128,4096]{1,0:T(8,128)(2,1)} %refs_3_.1, ...), custom_call_target="tpu_custom_call", output_to_operand_aliasing={{3}: (4, {})} | custom-call | flops 1 | bytes 1 | tf_op jit(solution)/shard_map/prep/pallas_call | solution.py:265
  3.2 2.6 %collective-permute-start = (bf16[64,4224]{1,0:T(8,128)(2,1)S(1)}, bf16[64,4224]{1,0:T(8,128)(2,1)S(1)}, u32[]{:S(2)}, u32[]{:S(2)}) collective-permute-start(bf16[64,4224]{1,0:T(8,128)(2,1)S(1)} %get-tuple-element.109.refs_1_.refs_2_), channel_id=1, source_target_pairs={{0,4},{1,5},{2,6},{3,7},{4,0},{5,1},{6,2},{7,3},{8,12},{9,13},{10,... | collective-permute-start | bytes 1622024 | tf_op jit(solution)/shard_map/move_EA/ppermute | solution.py:73
  6.8 2.6 %V.1 = (bf16[896,2048]{1,0:T(8,128)(2,1)S(1)}, f32[8,128]{1,0:T(8,128)S(1)}) custom-call(s32[6]{0:T(128)S(1)} %stack.31.refs_0_, bf16[896,2048]{1,0:T(8,128)(2,1)} %refs_7_.11, f32[8,128]{1,0:T(8,128)S(1)} %get-tuple-element.111.refs_2_), custom_call_target="tpu_custom_call", output_to_operand_aliasing={{1}: (2, {})} | custom-call | flops 1 | bytes 1 | tf_op jit(solution)/shard_map/V/pallas_call | solution.py:265
  10.6 8.1 %collective-permute-done.refs_2_ = bf16[64,4224]{1,0:T(8,128)(2,1)S(1)} collective-permute-done((bf16[64,4224]{1,0:T(8,128)(2,1)S(1)}, bf16[64,4224]{1,0:T(8,128)(2,1)S(1)}, u32[]{:S(2)}, u32[]{:S(2)}) %collective-permute-start) | collective-permute-done | bytes 540704 | tf_op jit(solution)/shard_map/move_EA/ppermute | solution.py:73
  19.4 4.8 %collective-permute-start.7 = (bf16[64,4224]{1,0:T(8,128)(2,1)S(1)}, bf16[64,4224]{1,0:T(8,128)(2,1)S(1)}, u32[]{:S(2)}, u32[]{:S(2)}) collective-permute-start(bf16[64,4224]{1,0:T(8,128)(2,1)S(1)} %get-tuple-element.110.refs_2_), channel_id=1, source_target_pairs={{0,4},{1,5},{2,6},{3,7},{4,0},{5,1},{6,2},{7,3},{8,12},{9,13},{10,... | collective-permute-start | bytes 1622024 | tf_op jit(solution)/shard_map/move_EB/ppermute | solution.py:73
  26.2 1.6 collective-permute-start.3
  27.8 3.2 %W.1 = (bf16[448,4096]{1,0:T(8,128)(2,1)S(1)}, bf16[448,4096]{1,0:T(8,128)(2,1)S(1)}, bf16[896,2048]{1,0:T(8,128)(2,1)S(1)}, f32[8,128]{1,0:T(8,128)S(1)}) custom-call(s32[6]{0:T(128)S(1)} %stack.31.refs_0_, bf16[448,4096]{1,0:T(8,128)(2,1)S(1)} %collective-permute-done.4.refs_1_, ...), custom_call_target="tpu_custom_call", output_to_operand_aliasing={{3}: (4, {})} | custom-call | flops 1 | bytes 1 | tf_op jit(solution)/shard_map/W/pallas_call | solution.py:265
  32.4 4.9 %collective-permute-done.7.refs_2_.refs_4_ = bf16[64,4224]{1,0:T(8,128)(2,1)S(1)} collective-permute-done((bf16[64,4224]{1,0:T(8,128)(2,1)S(1)}, bf16[64,4224]{1,0:T(8,128)(2,1)S(1)}, u32[]{:S(2)}, u32[]{:S(2)}) %collective-permute-start.7) | collective-permute-done | bytes 540704 | tf_op jit(solution)/shard_map/move_EB/ppermute | solution.py:73
  39.9 1.6 collective-permute-start.11
  41.5 7.4 %collective-permute-done.6.refs_2_.refs_11_ = bf16[64,4224]{1,0:T(8,128)(2,1)S(1)} collective-permute-done((bf16[64,4224]{1,0:T(8,128)(2,1)S(1)}, bf16[64,4224]{1,0:T(8,128)(2,1)S(1)}, u32[]{:S(2)}, u32[]{:S(2)}) %collective-permute-start.6) | collective-permute-done | bytes 540704 | tf_op jit(solution)/shard_map/move_OB/ppermute | solution.py:73
  50.8 1.6 collective-permute-start.12
  52.4 5.9 %F0.1 = (bf16[64,4096]{1,0:T(8,128)(2,1)S(1)}, bf16[64,4096]{1,0:T(8,128)(2,1)S(1)}, f32[8,128]{1,0:T(8,128)S(1)}, bf16[64,4224]{1,0:T(8,128)(2,1)S(1)}, bf16[64,4224]{1,0:T(8,128)(2,1)S(1)}) custom-call(s32[6]{0:T(128)S(1)} %stack.31.refs_0_, ...), custom_call_target="tpu_custom_call", output_to_operand_aliasing={{2}: (9, {}), {3}: (10, {}), {4}: (11, {})} | custom-call | flops 1 | bytes 24150016 | tf_op jit(solution)/shard_map/F0/pallas_call | solution.py:265
  61.4 1.6 collective-permute-start.16
  63.0 5.8 %F2B.1 = (bf16[64,4096]{1,0:T(8,128)(2,1)S(1)}, bf16[40,4096]{1,0:T(8,128)(2,1)S(1)}, f32[8,128]{1,0:T(8,128)S(1)}, bf16[64,4224]{1,0:T(8,128)(2,1)S(1)}) custom-call(s32[6]{0:T(128)S(1)} %stack.31.refs_0_, bf16[64,4224]{1,0:T(8,128)(2,1)S(1)} %get-tuple-element.139.refs_1_, ...), custom_call_target="tpu_custom_call", output_to_operand_aliasing={{2}: (9, {}), {3}: (10, {})} | custom-call | flops 1 | bytes 23750656 | tf_op jit(solution)/shard_map/F2B/pallas_call | solution.py:265
  68.8 1.5 collective-permute-start.14
  71.7 2.7 %collective-permute-done.17.refs_2_ = bf16[64,4224]{1,0:T(8,128)(2,1)S(1)} collective-permute-done((bf16[64,4224]{1,0:T(8,128)(2,1)S(1)}, bf16[64,4224]{1,0:T(8,128)(2,1)S(1)}, u32[]{:S(2)}, u32[]{:S(2)}) %collective-permute-start.17) | collective-permute-done | bytes 540704 | tf_op jit(solution)/shard_map/move_OA/ppermute | solution.py:73
  76.7 5.8 %F3A.1 = (bf16[64,4096]{1,0:T(8,128)(2,1)S(1)}, bf16[40,4096]{1,0:T(8,128)(2,1)S(1)}, f32[8,128]{1,0:T(8,128)S(1)}) custom-call(s32[6]{0:T(128)S(1)} %stack.31.refs_0_, bf16[64,4224]{1,0:T(8,128)(2,1)S(1)} %get-tuple-element.147.refs_1_, bf16[40,4224]{1,0:T(8,128)(2,1)S(1)} %get-tuple-element.150.refs_2_, ...), custom_call_target="tpu_custom_call", output_to_operand_aliasing={{2}: (9, {})} | custom-call | flops 1 | bytes 23750656 | tf_op jit(solution)/shard_map/F3A/pallas_call | solution.py:265
  83.4 3.1 %collective-permute-start.20 = (bf16[64,4096]{1,0:T(8,128)(2,1)S(1)}, bf16[64,4096]{1,0:T(8,128)(2,1)S(1)}, u32[]{:S(2)}, u32[]{:S(2)}) collective-permute-start(bf16[64,4096]{1,0:T(8,128)(2,1)S(1)} %get-tuple-element.170), channel_id=1, source_target_pairs={{0,4},{1,5},{2,6},{3,7},{12,8},{13,9},{14,10},{15,11},{16,20},{17,... | collective-permute-start | bytes 1572872 | tf_op jit(solution)/shard_map/move_I2B/ppermute | solution.py:73
  89.5 5.9 %F1.1 = (bf16[64,4096]{1,0:T(8,128)(2,1)S(1)}, bf16[64,4096]{1,0:T(8,128)(2,1)S(1)}, f32[8,128]{1,0:T(8,128)S(1)}, bf16[40,4096]{1,0:T(8,128)(2,1)S(1)}) custom-call(s32[6]{0:T(128)S(1)} %stack.31.refs_0_, bf16[64,4224]{1,0:T(8,128)(2,1)S(1)} %get-tuple-element.134.refs_1_, ...), custom_call_target="tpu_custom_call", output_to_operand_aliasing={{2}: (9, {}), {3}: (10, {})} | custom-call | flops 1 | bytes 24150016 | tf_op jit(solution)/shard_map/F1/pallas_call | solution.py:265
  97.3 5.8 %F3B.1 = (bf16[64,4096]{1,0:T(8,128)(2,1)S(1)}, bf16[40,4096]{1,0:T(8,128)(2,1)S(1)}, f32[8,128]{1,0:T(8,128)S(1)}) custom-call(s32[6]{0:T(128)S(1)} %stack.31.refs_0_, bf16[64,4224]{1,0:T(8,128)(2,1)S(1)} %get-tuple-element.171.refs_1_, bf16[40,4224]{1,0:T(8,128)(2,1)S(1)} %collective-permute-done.21.refs_2_, ...), custom_call_target="tpu_custom_call", output_to_operand_aliasing={{2}: (9, {})} | custom-call | flops 1 | bytes 23750656 | tf_op jit(solution)/shard_map/F3B/pallas_call | solution.py:265
  105.1 3.7 %collective-permute-start.24 = (bf16[64,4096]{1,0:T(8,128)(2,1)S(1)}, bf16[64,4096]{1,0:T(8,128)(2,1)S(1)}, u32[]{:S(2)}, u32[]{:S(2)}) collective-permute-start(bf16[64,4096]{1,0:T(8,128)(2,1)S(1)} %get-tuple-element.187), channel_id=1, source_target_pairs={{0,4},{1,5},{2,6},{3,7},{12,8},{13,9},{14,10},{15,11},{16,20},{17,... | collective-permute-start | bytes 1572872 | tf_op jit(solution)/shard_map/move_I3A/ppermute | solution.py:73
  109.7 5.8 %F2A.1 = (bf16[64,4096]{1,0:T(8,128)(2,1)S(1)}, bf16[40,4096]{1,0:T(8,128)(2,1)S(1)}, f32[8,128]{1,0:T(8,128)S(1)}) custom-call(s32[6]{0:T(128)S(1)} %stack.31.refs_0_, bf16[64,4224]{1,0:T(8,128)(2,1)S(1)} %get-tuple-element.165.refs_1_, bf16[40,4224]{1,0:T(8,128)(2,1)S(1)} %get-tuple-element.166.refs_2_, ...), custom_call_target="tpu_custom_call", output_to_operand_aliasing={{2}: (9, {})} | custom-call | flops 1 | bytes 23750656 | tf_op jit(solution)/shard_map/F2A/pallas_call | solution.py:265
  116.4 4.3 %collective-permute-start.28 = (bf16[64,4096]{1,0:T(8,128)(2,1)S(1)}, bf16[64,4096]{1,0:T(8,128)(2,1)S(1)}, u32[]{:S(2)}, u32[]{:S(2)}) collective-permute-start(bf16[64,4096]{1,0:T(8,128)(2,1)S(1)} %get-tuple-element.194), channel_id=1, source_target_pairs={{0,4},{1,5},{2,6},{3,7},{12,8},{13,9},{14,10},{15,11},{16,20},{17,... | collective-permute-start | bytes 1572872 | tf_op jit(solution)/shard_map/move_I3B/ppermute | solution.py:73
  120.7 2.1 %collective-permute-start.23 = (bf16[40,4096]{1,0:T(8,128)(2,1)S(1)}, bf16[40,4096]{1,0:T(8,128)(2,1)S(1)}, u32[]{:S(2)}, u32[]{:S(2)}) collective-permute-start(bf16[40,4096]{1,0:T(8,128)(2,1)S(1)} %get-tuple-element.185), channel_id=1, source_target_pairs={{0,2},{1,3},{2,0},{3,1},{4,6},{5,7},{6,4},{7,5},{8,10},{9,11},{10,... | collective-permute-start | bytes 983048 | tf_op jit(solution)/shard_map/move_R2A/ppermute | solution.py:16
  124.4 5.0 %collective-permute-done.23.refs_3_.refs_6_ = bf16[40,4096]{1,0:T(8,128)(2,1)S(1)} collective-permute-done((bf16[40,4096]{1,0:T(8,128)(2,1)S(1)}, bf16[40,4096]{1,0:T(8,128)(2,1)S(1)}, u32[]{:S(2)}, u32[]{:S(2)}) %collective-permute-start.23) | collective-permute-done | bytes 327712 | tf_op jit(solution)/shard_map/move_R2A/ppermute | solution.py:16
  130.3 2.6 %collective-permute-start.26 = (bf16[64,4096]{1,0:T(8,128)(2,1)S(1)}, bf16[64,4096]{1,0:T(8,128)(2,1)S(1)}, u32[]{:S(2)}, u32[]{:S(2)}) collective-permute-start(bf16[64,4096]{1,0:T(8,128)(2,1)S(1)} %get-tuple-element.192), channel_id=1, source_target_pairs={{0,2},{1,3},{2,0},{3,1},{4,6},{5,7},{6,4},{7,5},{8,10},{9,11},{10,... | collective-permute-start | bytes 1572872 | tf_op jit(solution)/shard_map/move_R1/ppermute | solution.py:16
  135.8 7.0 %collective-permute-done.26.refs_3_.refs_6_ = bf16[64,4096]{1,0:T(8,128)(2,1)S(1)} collective-permute-done((bf16[64,4096]{1,0:T(8,128)(2,1)S(1)}, bf16[64,4096]{1,0:T(8,128)(2,1)S(1)}, u32[]{:S(2)}, u32[]{:S(2)}) %collective-permute-start.26) | collective-permute-done | bytes 524320 | tf_op jit(solution)/shard_map/move_R1/ppermute | solution.py:16
  143.7 2.4 %collective-permute-start.29 = (bf16[64,4096]{1,0:T(8,128)(2,1)S(1)}, bf16[64,4096]{1,0:T(8,128)(2,1)S(1)}, u32[]{:S(2)}, u32[]{:S(2)}) collective-permute-start(bf16[64,4096]{1,0:T(8,128)(2,1)S(1)} %get-tuple-element.198), channel_id=1, source_target_pairs={{0,2},{1,3},{2,0},{3,1},{4,6},{5,7},{6,4},{7,5},{8,10},{9,11},{10,... | collective-permute-start | bytes 1572872 | tf_op jit(solution)/shard_map/move_R0/ppermute | solution.py:16
  148.7 4.1 %collective-permute-start.34 = (bf16[64,4096]{1,0:T(8,128)(2,1)S(1)}, bf16[64,4096]{1,0:T(8,128)(2,1)S(1)}, u32[]{:S(2)}, u32[]{:S(2)}) collective-permute-start(bf16[64,4096]{1,0:T(8,128)(2,1)S(1)} %get-tuple-element.207), channel_id=1, source_target_pairs={{0,4},{1,5},{2,6},{3,7},{4,0},{5,1},{6,2},{7,3},{8,12},{9,13},{10,... | collective-permute-start | bytes 1572872 | tf_op jit(solution)/shard_map/move_S1B/ppermute | solution.py:73
  153.2 4.4 %collective-permute-done.30.refs_5_ = bf16[64,4096]{1,0:T(8,128)(2,1)S(1)} collective-permute-done((bf16[64,4096]{1,0:T(8,128)(2,1)S(1)}, bf16[64,4096]{1,0:T(8,128)(2,1)S(1)}, u32[]{:S(2)}, u32[]{:S(2)}) %collective-permute-start.30) | collective-permute-done | bytes 524320 | tf_op jit(solution)/shard_map/move_S1A/ppermute | solution.py:73
  157.7 5.6 %collective-permute-done.34.refs_7_ = bf16[64,4096]{1,0:T(8,128)(2,1)S(1)} collective-permute-done((bf16[64,4096]{1,0:T(8,128)(2,1)S(1)}, bf16[64,4096]{1,0:T(8,128)(2,1)S(1)}, u32[]{:S(2)}, u32[]{:S(2)}) %collective-permute-start.34) | collective-permute-done | bytes 524320 | tf_op jit(solution)/shard_map/move_S1B/ppermute | solution.py:73
  163.3 2.4 %fin.1 = (bf16[128,4096]{1,0:T(8,128)(2,1)}, f32[8,128]{1,0:T(8,128)S(1)}) custom-call(s32[6]{0:T(128)S(1)} %stack.31.refs_0_, bf16[128,128]{1,0:T(8,128)(2,1)S(1)} %get-tuple-element.108.refs_1_, bf16[128,128]{1,0:T(8,128)(2,1)S(1)} %get-tuple-element.113.refs_2_, bf16[64,4096]{1,0:T(8,128)(2,1)S(1)} %get-tuple-element.132.refs_3_, ...), custom_call_target="tpu_custom_call", output_to_operand_aliasing={{1}: (9, {})} | custom-call | flops 1 | bytes 1 | tf_op jit(solution)/shard_map/fin/pallas_call | solution.py:265
  (77 shorter events, 36.8 us)
Async XLA Ops:
  0.0 18.7 %collective-permute-start.2 = (bf16[448,4096]{1,0:T(8,128)(2,1)}, bf16[448,4096]{1,0:T(8,128)(2,1)}, u32[]{:S(2)}, u32[]{:S(2)}) collective-permute-start(bf16[448,4096]{1,0:T(8,128)(2,1)} %bitcast.10), channel_id=1, source_target_pairs={{0,1},{1,0},{2,3},{3,2},{4,5},{5,4},{6,7},{7,6},{8,9},{9,8},{10,11... | collective-permute-start | bytes 11010056 | tf_op jit(solution)/shard_map/move_wu/ppermute | solution.py:16
  3.2 15.6 %collective-permute-start = (bf16[64,4224]{1,0:T(8,128)(2,1)S(1)}, bf16[64,4224]{1,0:T(8,128)(2,1)S(1)}, u32[]{:S(2)}, u32[]{:S(2)}) collective-permute-start(bf16[64,4224]{1,0:T(8,128)(2,1)S(1)} %get-tuple-element.109.refs_1_.refs_2_), channel_id=1, source_target_pairs={{0,4},{1,5},{2,6},{3,7},{4,0},{5,1},{6,2},{7,3},{8,12},{9,13},{10,... | collective-permute-start | bytes 1622024 | tf_op jit(solution)/shard_map/move_EA/ppermute | solution.py:73
  5.8 12.9 %collective-permute-start.1 = (bf16[64,4224]{1,0:T(8,128)(2,1)S(1)}, bf16[64,4224]{1,0:T(8,128)(2,1)S(1)}, u32[]{:S(2)}, u32[]{:S(2)}) collective-permute-start(bf16[64,4224]{1,0:T(8,128)(2,1)S(1)} %get-tuple-element.110.refs_2_), channel_id=1, source_target_pairs={{4,8},{5,9},{6,10},{7,11},{8,4},{9,5},{10,6},{11,7},{20,24},{21,25... | collective-permute-start | bytes 1622024 | tf_op jit(solution)/shard_map/move_MB/ppermute | solution.py:73
  6.5 19.7 %collective-permute-start.4 = (bf16[448,4096]{1,0:T(8,128)(2,1)}, bf16[448,4096]{1,0:T(8,128)(2,1)S(1)}, u32[]{:S(2)}, u32[]{:S(2)}) collective-permute-start(bf16[448,4096]{1,0:T(8,128)(2,1)} %bitcast.17), channel_id=1, source_target_pairs={{0,1},{1,0},{2,3},{3,2},{4,5},{5,4},{6,7},{7,6},{8,9},{9,8},{10,11... | collective-permute-start | bytes 11010056 | tf_op jit(solution)/shard_map/move_wg/ppermute | solution.py:16
  19.4 17.9 %collective-permute-start.7 = (bf16[64,4224]{1,0:T(8,128)(2,1)S(1)}, bf16[64,4224]{1,0:T(8,128)(2,1)S(1)}, u32[]{:S(2)}, u32[]{:S(2)}) collective-permute-start(bf16[64,4224]{1,0:T(8,128)(2,1)S(1)} %get-tuple-element.110.refs_2_), channel_id=1, source_target_pairs={{0,4},{1,5},{2,6},{3,7},{4,0},{5,1},{6,2},{7,3},{8,12},{9,13},{10,... | collective-permute-start | bytes 1622024 | tf_op jit(solution)/shard_map/move_EB/ppermute | solution.py:73
  24.2 13.1 %collective-permute-start.8 = (bf16[64,4224]{1,0:T(8,128)(2,1)S(1)}, bf16[64,4224]{1,0:T(8,128)(2,1)S(1)}, u32[]{:S(2)}, u32[]{:S(2)}) collective-permute-start(bf16[64,4224]{1,0:T(8,128)(2,1)S(1)} %get-tuple-element.126.refs_1_), channel_id=1, source_target_pairs={{4,8},{5,9},{6,10},{7,11},{8,4},{9,5},{10,6},{11,7},{20,24},{21,25... | collective-permute-start | bytes 1622024 | tf_op jit(solution)/shard_map/move_NA/ppermute | solution.py:73
  24.9 24.0 %collective-permute-start.6 = (bf16[64,4224]{1,0:T(8,128)(2,1)S(1)}, bf16[64,4224]{1,0:T(8,128)(2,1)S(1)}, u32[]{:S(2)}, u32[]{:S(2)}) collective-permute-start(bf16[64,4224]{1,0:T(8,128)(2,1)S(1)} %get-tuple-element.125.refs_1_), channel_id=1, source_target_pairs={{4,0},{5,1},{6,2},{7,3},{8,12},{9,13},{10,14},{11,15},{20,16},{21,... | collective-permute-start | bytes 1622024 | tf_op jit(solution)/shard_map/move_OB/ppermute | solution.py:73
  26.2 24.6 %collective-permute-start.3 = (bf16[64,4224]{1,0:T(8,128)(2,1)S(1)}, bf16[64,4224]{1,0:T(8,128)(2,1)S(1)}, u32[]{:S(2)}, u32[]{:S(2)}) collective-permute-start(bf16[64,4224]{1,0:T(8,128)(2,1)S(1)} %get-tuple-element.118), channel_id=1, source_target_pairs={{0,2},{1,3},{2,0},{3,1},{4,6},{5,7},{6,4},{7,5},{8,10},{9,11},{10,... | collective-permute-start | bytes 1622024 | tf_op jit(solution)/shard_map/move_Y0/ppermute | solution.py:16
  31.6 20.8 %collective-permute-start.9 = (bf16[64,4224]{1,0:T(8,128)(2,1)S(1)}, bf16[64,4224]{1,0:T(8,128)(2,1)S(1)}, u32[]{:S(2)}, u32[]{:S(2)}) collective-permute-start(bf16[64,4224]{1,0:T(8,128)(2,1)S(1)} %get-tuple-element.131), channel_id=1, source_target_pairs={{4,8},{5,9},{6,10},{7,11},{8,4},{9,5},{10,6},{11,7},{20,24},{21,25... | collective-permute-start | bytes 1622024 | tf_op jit(solution)/shard_map/move_MA/ppermute | solution.py:73
  38.6 21.7 %collective-permute-start.10 = (bf16[64,4224]{1,0:T(8,128)(2,1)S(1)}, bf16[64,4224]{1,0:T(8,128)(2,1)S(1)}, u32[]{:S(2)}, u32[]{:S(2)}) collective-permute-start(bf16[64,4224]{1,0:T(8,128)(2,1)S(1)} %get-tuple-element.135.refs_1_), channel_id=1, source_target_pairs={{4,0},{5,1},{6,2},{7,3},{8,12},{9,13},{10,14},{11,15},{20,16},{21,... | collective-permute-start | bytes 1622024 | tf_op jit(solution)/shard_map/move_QA/ppermute | solution.py:73
  39.9 20.4 %collective-permute-start.11 = (bf16[64,4224]{1,0:T(8,128)(2,1)S(1)}, bf16[64,4224]{1,0:T(8,128)(2,1)S(1)}, u32[]{:S(2)}, u32[]{:S(2)}) collective-permute-start(bf16[64,4224]{1,0:T(8,128)(2,1)S(1)} %get-tuple-element.137), channel_id=1, source_target_pairs={{0,2},{1,3},{2,0},{3,1},{4,6},{5,7},{6,4},{7,5},{8,10},{9,11},{10,... | collective-permute-start | bytes 1622024 | tf_op jit(solution)/shard_map/move_Y1/ppermute | solution.py:16
  50.1 12.9 %collective-permute-start.13 = (bf16[64,4224]{1,0:T(8,128)(2,1)S(1)}, bf16[64,4224]{1,0:T(8,128)(2,1)S(1)}, u32[]{:S(2)}, u32[]{:S(2)}) collective-permute-start(bf16[64,4224]{1,0:T(8,128)(2,1)S(1)} %get-tuple-element.142), channel_id=1, source_target_pairs={{4,8},{5,9},{6,10},{7,11},{8,4},{9,5},{10,6},{11,7},{20,24},{21,25... | collective-permute-start | bytes 1622024 | tf_op jit(solution)/shard_map/move_NB/ppermute | solution.py:73
  50.8 12.2 %collective-permute-start.12 = (bf16[40,4224]{1,0:T(8,128)(2,1)S(1)}, bf16[40,4224]{1,0:T(8,128)(2,1)S(1)}, u32[]{:S(2)}, u32[]{:S(2)}) collective-permute-start(bf16[40,4224]{1,0:T(8,128)(2,1)S(1)} %get-tuple-element.140), channel_id=1, source_target_pairs={{0,2},{1,3},{2,0},{3,1},{4,6},{5,7},{6,4},{7,5},{8,10},{9,11},{10,... | collective-permute-start | bytes 1013768 | tf_op jit(solution)/shard_map/move_Y2B/ppermute | solution.py:16
  58.3 16.1 %collective-permute-start.17 = (bf16[64,4224]{1,0:T(8,128)(2,1)S(1)}, bf16[64,4224]{1,0:T(8,128)(2,1)S(1)}, u32[]{:S(2)}, u32[]{:S(2)}) collective-permute-start(bf16[64,4224]{1,0:T(8,128)(2,1)S(1)} %get-tuple-element.151.refs_1_), channel_id=1, source_target_pairs={{4,0},{5,1},{6,2},{7,3},{8,12},{9,13},{10,14},{11,15},{20,16},{21,... | collective-permute-start | bytes 1622024 | tf_op jit(solution)/shard_map/move_OA/ppermute | solution.py:73
  61.4 9.8 %collective-permute-start.16 = (bf16[40,4224]{1,0:T(8,128)(2,1)S(1)}, bf16[40,4224]{1,0:T(8,128)(2,1)S(1)}, u32[]{:S(2)}, u32[]{:S(2)}) collective-permute-start(bf16[40,4224]{1,0:T(8,128)(2,1)S(1)} %get-tuple-element.149), channel_id=1, source_target_pairs={{0,2},{1,3},{2,0},{3,1},{4,6},{5,7},{6,4},{7,5},{8,10},{9,11},{10,... | collective-permute-start | bytes 1013768 | tf_op jit(solution)/shard_map/move_Y3A/ppermute | solution.py:16
  68.8 17.7 %collective-permute-start.14 = (bf16[64,4224]{1,0:T(8,128)(2,1)S(1)}, bf16[64,4224]{1,0:T(8,128)(2,1)S(1)}, u32[]{:S(2)}, u32[]{:S(2)}) collective-permute-start(bf16[64,4224]{1,0:T(8,128)(2,1)S(1)} %get-tuple-element.143.refs_1_), channel_id=1, source_target_pairs={{4,0},{5,1},{6,2},{7,3},{8,12},{9,13},{10,14},{11,15},{20,16},{21,... | collective-permute-start | bytes 1622024 | tf_op jit(solution)/shard_map/move_QB/ppermute | solution.py:73
  70.3 12.2 %collective-permute-start.15 = (bf16[40,4096]{1,0:T(8,128)(2,1)S(1)}, bf16[40,4096]{1,0:T(8,128)(2,1)S(1)}, u32[]{:S(2)}, u32[]{:S(2)}) collective-permute-start(bf16[40,4096]{1,0:T(8,128)(2,1)S(1)} %get-tuple-element.146), channel_id=1, source_target_pairs={{0,2},{1,3},{2,0},{3,1},{4,6},{5,7},{6,4},{7,5},{8,10},{9,11},{10,... | collective-permute-start | bytes 983048 | tf_op jit(solution)/shard_map/move_R2B/ppermute | solution.py:16
  76.2 11.5 %collective-permute-start.18 = (bf16[40,4224]{1,0:T(8,128)(2,1)S(1)}, bf16[40,4224]{1,0:T(8,128)(2,1)S(1)}, u32[]{:S(2)}, u32[]{:S(2)}) collective-permute-start(bf16[40,4224]{1,0:T(8,128)(2,1)S(1)} %get-tuple-element.159), channel_id=1, source_target_pairs={{0,2},{1,3},{2,0},{3,1},{4,6},{5,7},{6,4},{7,5},{8,10},{9,11},{10,... | collective-permute-start | bytes 1013768 | tf_op jit(solution)/shard_map/move_Y2A/ppermute | solution.py:16
  83.4 19.7 %collective-permute-start.20 = (bf16[64,4096]{1,0:T(8,128)(2,1)S(1)}, bf16[64,4096]{1,0:T(8,128)(2,1)S(1)}, u32[]{:S(2)}, u32[]{:S(2)}) collective-permute-start(bf16[64,4096]{1,0:T(8,128)(2,1)S(1)} %get-tuple-element.170), channel_id=1, source_target_pairs={{0,4},{1,5},{2,6},{3,7},{12,8},{13,9},{14,10},{15,11},{16,20},{17,... | collective-permute-start | bytes 1572872 | tf_op jit(solution)/shard_map/move_I2B/ppermute | solution.py:73
  88.3 9.0 %collective-permute-start.21 = (bf16[40,4224]{1,0:T(8,128)(2,1)S(1)}, bf16[40,4224]{1,0:T(8,128)(2,1)S(1)}, u32[]{:S(2)}, u32[]{:S(2)}) collective-permute-start(bf16[40,4224]{1,0:T(8,128)(2,1)S(1)} %get-tuple-element.172), channel_id=1, source_target_pairs={{0,2},{1,3},{2,0},{3,1},{4,6},{5,7},{6,4},{7,5},{8,10},{9,11},{10,... | collective-permute-start | bytes 1013768 | tf_op jit(solution)/shard_map/move_Y3B/ppermute | solution.py:16
  104.0 11.5 %collective-permute-start.22 = (bf16[40,4096]{1,0:T(8,128)(2,1)S(1)}, bf16[40,4096]{1,0:T(8,128)(2,1)S(1)}, u32[]{:S(2)}, u32[]{:S(2)}) collective-permute-start(bf16[40,4096]{1,0:T(8,128)(2,1)S(1)} %get-tuple-element.182), channel_id=1, source_target_pairs={{0,2},{1,3},{2,0},{3,1},{4,6},{5,7},{6,4},{7,5},{8,10},{9,11},{10,... | collective-permute-start | bytes 983048 | tf_op jit(solution)/shard_map/move_R3B/ppermute | solution.py:16
  105.1 17.6 %collective-permute-start.24 = (bf16[64,4096]{1,0:T(8,128)(2,1)S(1)}, bf16[64,4096]{1,0:T(8,128)(2,1)S(1)}, u32[]{:S(2)}, u32[]{:S(2)}) collective-permute-start(bf16[64,4096]{1,0:T(8,128)(2,1)S(1)} %get-tuple-element.187), channel_id=1, source_target_pairs={{0,4},{1,5},{2,6},{3,7},{12,8},{13,9},{14,10},{15,11},{16,20},{17,... | collective-permute-start | bytes 1572872 | tf_op jit(solution)/shard_map/move_I3A/ppermute | solution.py:73
  108.8 15.5 %collective-permute-start.25 = (bf16[64,4096]{1,0:T(8,128)(2,1)S(1)}, bf16[64,4096]{1,0:T(8,128)(2,1)S(1)}, u32[]{:S(2)}, u32[]{:S(2)}) collective-permute-start(bf16[64,4096]{1,0:T(8,128)(2,1)S(1)} %get-tuple-element.190), channel_id=1, source_target_pairs={{4,8},{5,9},{6,10},{7,11},{8,4},{9,5},{10,6},{11,7},{20,24},{21,25... | collective-permute-start | bytes 1572872 | tf_op jit(solution)/shard_map/move_S2B/ppermute | solution.py:73
  116.4 17.7 %collective-permute-start.28 = (bf16[64,4096]{1,0:T(8,128)(2,1)S(1)}, bf16[64,4096]{1,0:T(8,128)(2,1)S(1)}, u32[]{:S(2)}, u32[]{:S(2)}) collective-permute-start(bf16[64,4096]{1,0:T(8,128)(2,1)S(1)} %get-tuple-element.194), channel_id=1, source_target_pairs={{0,4},{1,5},{2,6},{3,7},{12,8},{13,9},{14,10},{15,11},{16,20},{17,... | collective-permute-start | bytes 1572872 | tf_op jit(solution)/shard_map/move_I3B/ppermute | solution.py:73
  123.6 12.1 %collective-permute-start.27 = (bf16[64,4096]{1,0:T(8,128)(2,1)S(1)}, bf16[64,4096]{1,0:T(8,128)(2,1)S(1)}, u32[]{:S(2)}, u32[]{:S(2)}) collective-permute-start(bf16[64,4096]{1,0:T(8,128)(2,1)S(1)} %get-tuple-element.193), channel_id=1, source_target_pairs={{4,8},{5,9},{6,10},{7,11},{8,4},{9,5},{10,6},{11,7},{20,24},{21,25... | collective-permute-start | bytes 1572872 | tf_op jit(solution)/shard_map/move_S3A/ppermute | solution.py:73
  130.3 12.5 %collective-permute-start.26 = (bf16[64,4096]{1,0:T(8,128)(2,1)S(1)}, bf16[64,4096]{1,0:T(8,128)(2,1)S(1)}, u32[]{:S(2)}, u32[]{:S(2)}) collective-permute-start(bf16[64,4096]{1,0:T(8,128)(2,1)S(1)} %get-tuple-element.192), channel_id=1, source_target_pairs={{0,2},{1,3},{2,0},{3,1},{4,6},{5,7},{6,4},{7,5},{8,10},{9,11},{10,... | collective-permute-start | bytes 1572872 | tf_op jit(solution)/shard_map/move_R1/ppermute | solution.py:16
  132.8 13.3 %collective-permute-start.31 = (bf16[64,4096]{1,0:T(8,128)(2,1)S(1)}, bf16[64,4096]{1,0:T(8,128)(2,1)S(1)}, u32[]{:S(2)}, u32[]{:S(2)}) collective-permute-start(bf16[64,4096]{1,0:T(8,128)(2,1)S(1)} %get-tuple-element.201), channel_id=1, source_target_pairs={{0,4},{1,5},{2,6},{3,7},{12,8},{13,9},{14,10},{15,11},{16,20},{17,... | collective-permute-start | bytes 1572872 | tf_op jit(solution)/shard_map/move_I2A/ppermute | solution.py:73
  135.0 12.6 %collective-permute-start.33 = (bf16[64,4096]{1,0:T(8,128)(2,1)S(1)}, bf16[64,4096]{1,0:T(8,128)(2,1)S(1)}, u32[]{:S(2)}, u32[]{:S(2)}) collective-permute-start(bf16[64,4096]{1,0:T(8,128)(2,1)S(1)} %get-tuple-element.205), channel_id=1, source_target_pairs={{4,8},{5,9},{6,10},{7,11},{8,4},{9,5},{10,6},{11,7},{20,24},{21,25... | collective-permute-start | bytes 1572872 | tf_op jit(solution)/shard_map/move_S3B/ppermute | solution.py:73
  143.7 9.5 %collective-permute-start.29 = (bf16[64,4096]{1,0:T(8,128)(2,1)S(1)}, bf16[64,4096]{1,0:T(8,128)(2,1)S(1)}, u32[]{:S(2)}, u32[]{:S(2)}) collective-permute-start(bf16[64,4096]{1,0:T(8,128)(2,1)S(1)} %get-tuple-element.198), channel_id=1, source_target_pairs={{0,2},{1,3},{2,0},{3,1},{4,6},{5,7},{6,4},{7,5},{8,10},{9,11},{10,... | collective-permute-start | bytes 1572872 | tf_op jit(solution)/shard_map/move_R0/ppermute | solution.py:16
  146.1 11.6 %collective-permute-start.30 = (bf16[64,4096]{1,0:T(8,128)(2,1)S(1)}, bf16[64,4096]{1,0:T(8,128)(2,1)S(1)}, u32[]{:S(2)}, u32[]{:S(2)}) collective-permute-start(bf16[64,4096]{1,0:T(8,128)(2,1)S(1)} %get-tuple-element.199), channel_id=1, source_target_pairs={{0,4},{1,5},{2,6},{3,7},{4,0},{5,1},{6,2},{7,3},{8,12},{9,13},{10,... | collective-permute-start | bytes 1572872 | tf_op jit(solution)/shard_map/move_S1A/ppermute | solution.py:73
  147.0 10.7 %collective-permute-start.32 = (bf16[64,4096]{1,0:T(8,128)(2,1)S(1)}, bf16[64,4096]{1,0:T(8,128)(2,1)S(1)}, u32[]{:S(2)}, u32[]{:S(2)}) collective-permute-start(bf16[64,4096]{1,0:T(8,128)(2,1)S(1)} %get-tuple-element.203), channel_id=1, source_target_pairs={{4,8},{5,9},{6,10},{7,11},{8,4},{9,5},{10,6},{11,7},{20,24},{21,25... | collective-permute-start | bytes 1572872 | tf_op jit(solution)/shard_map/move_S2A/ppermute | solution.py:73
  148.7 14.6 %collective-permute-start.34 = (bf16[64,4096]{1,0:T(8,128)(2,1)S(1)}, bf16[64,4096]{1,0:T(8,128)(2,1)S(1)}, u32[]{:S(2)}, u32[]{:S(2)}) collective-permute-start(bf16[64,4096]{1,0:T(8,128)(2,1)S(1)} %get-tuple-element.207), channel_id=1, source_target_pairs={{0,4},{1,5},{2,6},{3,7},{4,0},{5,1},{6,2},{7,3},{8,12},{9,13},{10,... | collective-permute-start | bytes 1572872 | tf_op jit(solution)/shard_map/move_S1B/ppermute | solution.py:73
  (6 other events, 96.7 us)

commit v4 on v2

--- a/solution.py
+++ b/solution.py
@@ -293,14 +293,14 @@
     ["F1", "R3A"],
     ["F3B", "+I2B"],
     ["D2B", "R3B"],
-    ["C3A", "I3A", "S2B"],
+    ["C3A", "I3A", "S2B", "R1"],
     ["F2A"],
     ["C3B", "I3B", "R2A", "+R3A"],
     ["D3A", "S3A"],
-    ["C2A", "R1", "I2A", "+S2B"],
+    ["C2A", "I2A", "+S2B", "+R1"],
     ["D3B", "S3B", "+R2A"],
     ["D1A", "S1A", "R0"],
-    ["D2A", "+R1"],
+    ["D2A"],
     ["D1B", "S2A", "S1B", "+I2A"],
     ["fin"],
 ]

time: 165 us -> 164 us (level)
  waiting for transfers between devices: 54 us -> 45 us
  starting transfers between devices: 46.2 us -> 54.5 us
    ppermute x15, waiting for transfers between devices: 26.1 us -> 7.51 us  [swapped(): lax.ppermute(x, axis, [(i, i ^ 1 << apart) for i in range(lax.axis_size(a...]
    ppermute x20, waiting for transfers between devices: 27.9 us -> 37.5 us  [along_line(): return lax.ppermute(x, 'expert', moves)]
    ppermute x20, starting transfers between devices: 31.8 us -> 36.9 us  [along_line(): return lax.ppermute(x, 'expert', moves)]
    ppermute x15, starting transfers between devices: 14.4 us -> 17.6 us  [swapped(): lax.ppermute(x, axis, [(i, i ^ 1 << apart) for i in range(lax.axis_size(a...]
  transfers between devices with their start and end apart: 35 -> 35, of which waited for: 11 -> 10; matrix products, arithmetic and copies ran while one was open for 0% -> 0% of each run, Pallas kernels for 37% -> 37%
where the time goes in v4:
time: 164 us
  Pallas kernels  63.4 us (39%)
  starting transfers between devices  54.5 us (33%)
  waiting for transfers between devices  45 us (27%)
    pallas_call x29, Pallas kernels, call(): pl.pallas_call(body, out_shape=[*outs, *(jax.ShapeDtypeStruct(x.shape, x....  63.4 us
    ppermute x20, waiting for transfers between devices, along_line(): return lax.ppermute(x, 'expert', moves)  37.5 us
    ppermute x20, starting transfers between devices, along_line(): return lax.ppermute(x, 'expert', moves)  36.9 us
    ppermute x15, starting transfers between devices, swapped(): lax.ppermute(x, axis, [(i, i ^ 1 << apart) for i in range(lax.axis_size(a...  17.6 us
    ppermute x15, waiting for transfers between devices, swapped(): lax.ppermute(x, axis, [(i, i ^ 1 << apart) for i in range(lax.axis_size(a...  7.51 us
  transfers between devices with their start and end apart: 35, of which 10 were waited for; matrix products, arithmetic and copies ran while one was open for 0% of the time, Pallas kernels for 37%

profile of v4, /device:TPU:0, one launch (start us, length us, event | category | flops | bytes accessed | tf_op | source)
XLA Modules:
  0.0 163.7 jit_solution(3943110984720112980)
XLA Ops:
  1.1 2.6 %prep.1 = (bf16[64,4224]{1,0:T(8,128)(2,1)S(1)}, bf16[64,4224]{1,0:T(8,128)(2,1)S(1)}, bf16[128,128]{1,0:T(8,128)(2,1)S(1)}, f32[8,128]{1,0:T(8,128)S(1)}) custom-call(s32[6]{0:T(128)S(1)} %stack.31.refs_0_, s32[4,128]{1,0:T(4,128)} %bitcast.24, f32[4,128]{1,0:T(4,128)} %bitcast.25, bf16[128,4096]{1,0:T(8,128)(2,1)} %refs_3_.1, ...), custom_call_target="tpu_custom_call", output_to_operand_aliasing={{3}: (4, {})} | custom-call | flops 1 | bytes 1 | tf_op jit(solution)/shard_map/prep/pallas_call | solution.py:259
  3.7 2.6 %collective-permute-start = (bf16[64,4224]{1,0:T(8,128)(2,1)S(1)}, bf16[64,4224]{1,0:T(8,128)(2,1)S(1)}, u32[]{:S(2)}, u32[]{:S(2)}) collective-permute-start(bf16[64,4224]{1,0:T(8,128)(2,1)S(1)} %get-tuple-element.106.refs_1_.refs_2_), channel_id=1, source_target_pairs={{0,4},{1,5},{2,6},{3,7},{4,0},{5,1},{6,2},{7,3},{8,12},{9,13},{10,... | collective-permute-start | bytes 1622024 | tf_op jit(solution)/shard_map/move_EA/ppermute | solution.py:73
  7.0 12.3 %collective-permute-done.refs_4_ = bf16[64,4224]{1,0:T(8,128)(2,1)S(1)} collective-permute-done((bf16[64,4224]{1,0:T(8,128)(2,1)S(1)}, bf16[64,4224]{1,0:T(8,128)(2,1)S(1)}, u32[]{:S(2)}, u32[]{:S(2)}) %collective-permute-start) | collective-permute-done | bytes 540704 | tf_op jit(solution)/shard_map/move_EA/ppermute | solution.py:73
  19.2 1.7 %collective-permute-start.7 = (bf16[64,4224]{1,0:T(8,128)(2,1)S(1)}, bf16[64,4224]{1,0:T(8,128)(2,1)S(1)}, u32[]{:S(2)}, u32[]{:S(2)}) collective-permute-start(bf16[64,4224]{1,0:T(8,128)(2,1)S(1)} %get-tuple-element.107.refs_2_), channel_id=1, source_target_pairs={{0,4},{1,5},{2,6},{3,7},{4,0},{5,1},{6,2},{7,3},{8,12},{9,13},{10,... | collective-permute-start | bytes 1622024 | tf_op jit(solution)/shard_map/move_EB/ppermute | solution.py:73
  24.8 1.6 collective-permute-start.1
  26.4 5.0 %W.1 = (bf16[448,4096]{1,0:T(8,128)(2,1)S(1)}, bf16[448,4096]{1,0:T(8,128)(2,1)S(1)}, bf16[896,2048]{1,0:T(8,128)(2,1)S(1)}, f32[8,128]{1,0:T(8,128)S(1)}) custom-call(s32[6]{0:T(128)S(1)} %stack.31.refs_0_, bf16[448,4096]{1,0:T(8,128)(2,1)} %get-tuple-element.113.refs_1_, ...), custom_call_target="tpu_custom_call", output_to_operand_aliasing={{3}: (4, {})} | custom-call | flops 1 | bytes 1 | tf_op jit(solution)/shard_map/W/pallas_call | solution.py:259
  32.8 1.6 collective-permute-done.7.refs_2_.refs_4_
  36.9 1.8 %collective-permute-start.11 = (bf16[64,4224]{1,0:T(8,128)(2,1)S(1)}, bf16[64,4224]{1,0:T(8,128)(2,1)S(1)}, u32[]{:S(2)}, u32[]{:S(2)}) collective-permute-start(bf16[64,4224]{1,0:T(8,128)(2,1)S(1)} %get-tuple-element.131), channel_id=1, source_target_pairs={{0,2},{1,3},{2,0},{3,1},{4,6},{5,7},{6,4},{7,5},{8,10},{9,11},{10,... | collective-permute-start | bytes 1622024 | tf_op jit(solution)/shard_map/move_Y1/ppermute | solution.py:16
  38.7 7.3 %collective-permute-done.6.refs_2_ = bf16[64,4224]{1,0:T(8,128)(2,1)S(1)} collective-permute-done((bf16[64,4224]{1,0:T(8,128)(2,1)S(1)}, bf16[64,4224]{1,0:T(8,128)(2,1)S(1)}, u32[]{:S(2)}, u32[]{:S(2)}) %collective-permute-start.6) | collective-permute-done | bytes 540704 | tf_op jit(solution)/shard_map/move_OB/ppermute | solution.py:73
  47.9 1.8 %collective-permute-start.12 = (bf16[40,4224]{1,0:T(8,128)(2,1)S(1)}, bf16[40,4224]{1,0:T(8,128)(2,1)S(1)}, u32[]{:S(2)}, u32[]{:S(2)}) collective-permute-start(bf16[40,4224]{1,0:T(8,128)(2,1)S(1)} %get-tuple-element.134), channel_id=1, source_target_pairs={{0,2},{1,3},{2,0},{3,1},{4,6},{5,7},{6,4},{7,5},{8,10},{9,11},{10,... | collective-permute-start | bytes 1013768 | tf_op jit(solution)/shard_map/move_Y2B/ppermute | solution.py:16
  49.7 5.9 %F0.1 = (bf16[64,4096]{1,0:T(8,128)(2,1)S(1)}, bf16[64,4096]{1,0:T(8,128)(2,1)S(1)}, f32[8,128]{1,0:T(8,128)S(1)}, bf16[64,4224]{1,0:T(8,128)(2,1)S(1)}) custom-call(s32[6]{0:T(128)S(1)} %stack.31.refs_0_, bf16[64,4224]{1,0:T(8,128)(2,1)S(1)} %get-tuple-element.110.refs_1_, ...), custom_call_target="tpu_custom_call", output_to_operand_aliasing={{2}: (9, {}), {3}: (10, {})} | custom-call | flops 1 | bytes 24150016 | tf_op jit(solution)/shard_map/F0/pallas_call | solution.py:259
  59.3 5.8 %F2B.1 = (bf16[64,4096]{1,0:T(8,128)(2,1)S(1)}, bf16[40,4096]{1,0:T(8,128)(2,1)S(1)}, f32[8,128]{1,0:T(8,128)S(1)}) custom-call(s32[6]{0:T(128)S(1)} %stack.31.refs_0_, bf16[64,4224]{1,0:T(8,128)(2,1)S(1)} %get-tuple-element.133.refs_1_, bf16[40,4224]{1,0:T(8,128)(2,1)S(1)} %collective-permute-done.12.refs_2_, ...), custom_call_target="tpu_custom_call", output_to_operand_aliasing={{2}: (9, {})} | custom-call | flops 1 | bytes 23750656 | tf_op jit(solution)/shard_map/F2B/pallas_call | solution.py:259
  65.1 1.6 collective-permute-done.14.refs_3_
  67.3 1.5 collective-permute-start.15
  72.8 5.8 %F3A.1 = (bf16[64,4096]{1,0:T(8,128)(2,1)S(1)}, bf16[40,4096]{1,0:T(8,128)(2,1)S(1)}, f32[8,128]{1,0:T(8,128)S(1)}) custom-call(s32[6]{0:T(128)S(1)} %stack.31.refs_0_, bf16[64,4224]{1,0:T(8,128)(2,1)S(1)} %get-tuple-element.143.refs_1_, bf16[40,4224]{1,0:T(8,128)(2,1)S(1)} %get-tuple-element.144.refs_2_, ...), custom_call_target="tpu_custom_call", output_to_operand_aliasing={{2}: (9, {})} | custom-call | flops 1 | bytes 23750656 | tf_op jit(solution)/shard_map/F3A/pallas_call | solution.py:259
  80.3 5.2 %collective-permute-start.21 = (bf16[64,4096]{1,0:T(8,128)(2,1)S(1)}, bf16[64,4096]{1,0:T(8,128)(2,1)S(1)}, u32[]{:S(2)}, u32[]{:S(2)}) collective-permute-start(bf16[64,4096]{1,0:T(8,128)(2,1)S(1)} %get-tuple-element.165), channel_id=1, source_target_pairs={{0,4},{1,5},{2,6},{3,7},{12,8},{13,9},{14,10},{15,11},{16,20},{17,... | collective-permute-start | bytes 1572872 | tf_op jit(solution)/shard_map/move_I2B/ppermute | solution.py:73
  86.8 1.9 %collective-permute-start.20 = (bf16[40,4224]{1,0:T(8,128)(2,1)S(1)}, bf16[40,4224]{1,0:T(8,128)(2,1)S(1)}, u32[]{:S(2)}, u32[]{:S(2)}) collective-permute-start(bf16[40,4224]{1,0:T(8,128)(2,1)S(1)} %get-tuple-element.163), channel_id=1, source_target_pairs={{0,2},{1,3},{2,0},{3,1},{4,6},{5,7},{6,4},{7,5},{8,10},{9,11},{10,... | collective-permute-start | bytes 1013768 | tf_op jit(solution)/shard_map/move_Y3B/ppermute | solution.py:16
  88.6 5.9 %F1.1 = (bf16[64,4096]{1,0:T(8,128)(2,1)S(1)}, bf16[64,4096]{1,0:T(8,128)(2,1)S(1)}, f32[8,128]{1,0:T(8,128)S(1)}, bf16[40,4096]{1,0:T(8,128)(2,1)S(1)}) custom-call(s32[6]{0:T(128)S(1)} %stack.31.refs_0_, bf16[64,4224]{1,0:T(8,128)(2,1)S(1)} %get-tuple-element.128.refs_1_, ...), custom_call_target="tpu_custom_call", output_to_operand_aliasing={{2}: (9, {}), {3}: (10, {})} | custom-call | flops 1 | bytes 24150016 | tf_op jit(solution)/shard_map/F1/pallas_call | solution.py:259
  96.2 5.8 %F3B.1 = (bf16[64,4096]{1,0:T(8,128)(2,1)S(1)}, bf16[40,4096]{1,0:T(8,128)(2,1)S(1)}, f32[8,128]{1,0:T(8,128)S(1)}, bf16[64,4096]{1,0:T(8,128)(2,1)S(1)}) custom-call(s32[6]{0:T(128)S(1)} %stack.31.refs_0_, bf16[64,4224]{1,0:T(8,128)(2,1)S(1)} %get-tuple-element.162.refs_1_, ...), custom_call_target="tpu_custom_call", output_to_operand_aliasing={{2}: (9, {}), {3}: (10, {})} | custom-call | flops 1 | bytes 23750656 | tf_op jit(solution)/shard_map/F3B/pallas_call | solution.py:259
  102.8 2.6 %collective-permute-start.22 = (bf16[40,4096]{1,0:T(8,128)(2,1)S(1)}, bf16[40,4096]{1,0:T(8,128)(2,1)S(1)}, u32[]{:S(2)}, u32[]{:S(2)}) collective-permute-start(bf16[40,4096]{1,0:T(8,128)(2,1)S(1)} %get-tuple-element.176), channel_id=1, source_target_pairs={{0,2},{1,3},{2,0},{3,1},{4,6},{5,7},{6,4},{7,5},{8,10},{9,11},{10,... | collective-permute-start | bytes 983048 | tf_op jit(solution)/shard_map/move_R3B/ppermute | solution.py:16
  106.3 1.9 %collective-permute-start.24 = (bf16[64,4096]{1,0:T(8,128)(2,1)S(1)}, bf16[64,4096]{1,0:T(8,128)(2,1)S(1)}, u32[]{:S(2)}, u32[]{:S(2)}) collective-permute-start(bf16[64,4096]{1,0:T(8,128)(2,1)S(1)} %get-tuple-element.181), channel_id=1, source_target_pairs={{0,4},{1,5},{2,6},{3,7},{12,8},{13,9},{14,10},{15,11},{16,20},{17,... | collective-permute-start | bytes 1572872 | tf_op jit(solution)/shard_map/move_I3A/ppermute | solution.py:73
  109.2 5.8 %F2A.1 = (bf16[64,4096]{1,0:T(8,128)(2,1)S(1)}, bf16[40,4096]{1,0:T(8,128)(2,1)S(1)}, f32[8,128]{1,0:T(8,128)S(1)}) custom-call(s32[6]{0:T(128)S(1)} %stack.31.refs_0_, bf16[64,4224]{1,0:T(8,128)(2,1)S(1)} %get-tuple-element.157.refs_1_, bf16[40,4224]{1,0:T(8,128)(2,1)S(1)} %get-tuple-element.158.refs_2_, ...), custom_call_target="tpu_custom_call", output_to_operand_aliasing={{2}: (9, {})} | custom-call | flops 1 | bytes 23750656 | tf_op jit(solution)/shard_map/F2A/pallas_call | solution.py:259
  115.9 4.1 %collective-permute-start.28 = (bf16[64,4096]{1,0:T(8,128)(2,1)S(1)}, bf16[64,4096]{1,0:T(8,128)(2,1)S(1)}, u32[]{:S(2)}, u32[]{:S(2)}) collective-permute-start(bf16[64,4096]{1,0:T(8,128)(2,1)S(1)} %get-tuple-element.188), channel_id=1, source_target_pairs={{0,4},{1,5},{2,6},{3,7},{12,8},{13,9},{14,10},{15,11},{16,20},{17,... | collective-permute-start | bytes 1572872 | tf_op jit(solution)/shard_map/move_I3B/ppermute | solution.py:73
  120.0 2.1 %collective-permute-start.23 = (bf16[40,4096]{1,0:T(8,128)(2,1)S(1)}, bf16[40,4096]{1,0:T(8,128)(2,1)S(1)}, u32[]{:S(2)}, u32[]{:S(2)}) collective-permute-start(bf16[40,4096]{1,0:T(8,128)(2,1)S(1)} %get-tuple-element.179), channel_id=1, source_target_pairs={{0,2},{1,3},{2,0},{3,1},{4,6},{5,7},{6,4},{7,5},{8,10},{9,11},{10,... | collective-permute-start | bytes 983048 | tf_op jit(solution)/shard_map/move_R2A/ppermute | solution.py:16
  123.7 3.6 %collective-permute-done.23.refs_3_.refs_6_ = bf16[40,4096]{1,0:T(8,128)(2,1)S(1)} collective-permute-done((bf16[40,4096]{1,0:T(8,128)(2,1)S(1)}, bf16[40,4096]{1,0:T(8,128)(2,1)S(1)}, u32[]{:S(2)}, u32[]{:S(2)}) %collective-permute-start.23) | collective-permute-done | bytes 327712 | tf_op jit(solution)/shard_map/move_R2A/ppermute | solution.py:16
  128.1 2.6 %collective-permute-start.32 = (bf16[64,4096]{1,0:T(8,128)(2,1)S(1)}, bf16[64,4096]{1,0:T(8,128)(2,1)S(1)}, u32[]{:S(2)}, u32[]{:S(2)}) collective-permute-start(bf16[64,4096]{1,0:T(8,128)(2,1)S(1)} %get-tuple-element.196), channel_id=1, source_target_pairs={{0,4},{1,5},{2,6},{3,7},{12,8},{13,9},{14,10},{15,11},{16,20},{17,... | collective-permute-start | bytes 1572872 | tf_op jit(solution)/shard_map/move_I2A/ppermute | solution.py:73
  134.6 2.1 %collective-permute-start.30 = (bf16[64,4096]{1,0:T(8,128)(2,1)S(1)}, bf16[64,4096]{1,0:T(8,128)(2,1)S(1)}, u32[]{:S(2)}, u32[]{:S(2)}) collective-permute-start(bf16[64,4096]{1,0:T(8,128)(2,1)S(1)} %get-tuple-element.193), channel_id=1, source_target_pairs={{0,4},{1,5},{2,6},{3,7},{4,0},{5,1},{6,2},{7,3},{8,12},{9,13},{10,... | collective-permute-start | bytes 1572872 | tf_op jit(solution)/shard_map/move_S1A/ppermute | solution.py:73
  136.8 6.3 %collective-permute-done.32.refs_4_.refs_7_ = bf16[64,4096]{1,0:T(8,128)(2,1)S(1)} collective-permute-done((bf16[64,4096]{1,0:T(8,128)(2,1)S(1)}, bf16[64,4096]{1,0:T(8,128)(2,1)S(1)}, u32[]{:S(2)}, u32[]{:S(2)}) %collective-permute-start.32) | collective-permute-done | bytes 524320 | tf_op jit(solution)/shard_map/move_I2A/ppermute | solution.py:73
  145.7 5.3 %collective-permute-start.34 = (bf16[64,4096]{1,0:T(8,128)(2,1)S(1)}, bf16[64,4096]{1,0:T(8,128)(2,1)S(1)}, u32[]{:S(2)}, u32[]{:S(2)}) collective-permute-start(bf16[64,4096]{1,0:T(8,128)(2,1)S(1)} %get-tuple-element.201), channel_id=1, source_target_pairs={{0,4},{1,5},{2,6},{3,7},{4,0},{5,1},{6,2},{7,3},{8,12},{9,13},{10,... | collective-permute-start | bytes 1572872 | tf_op jit(solution)/shard_map/move_S1B/ppermute | solution.py:73
  151.0 3.3 %collective-permute-done.30.refs_5_ = bf16[64,4096]{1,0:T(8,128)(2,1)S(1)} collective-permute-done((bf16[64,4096]{1,0:T(8,128)(2,1)S(1)}, bf16[64,4096]{1,0:T(8,128)(2,1)S(1)}, u32[]{:S(2)}, u32[]{:S(2)}) %collective-permute-start.30) | collective-permute-done | bytes 524320 | tf_op jit(solution)/shard_map/move_S1A/ppermute | solution.py:73
  154.3 6.7 %collective-permute-done.34.refs_7_ = bf16[64,4096]{1,0:T(8,128)(2,1)S(1)} collective-permute-done((bf16[64,4096]{1,0:T(8,128)(2,1)S(1)}, bf16[64,4096]{1,0:T(8,128)(2,1)S(1)}, u32[]{:S(2)}, u32[]{:S(2)}) %collective-permute-start.34) | collective-permute-done | bytes 524320 | tf_op jit(solution)/shard_map/move_S1B/ppermute | solution.py:73
  161.1 2.4 %fin.1 = (bf16[128,4096]{1,0:T(8,128)(2,1)}, f32[8,128]{1,0:T(8,128)S(1)}) custom-call(s32[6]{0:T(128)S(1)} %stack.31.refs_0_, bf16[128,128]{1,0:T(8,128)(2,1)S(1)} %get-tuple-element.105.refs_1_, bf16[128,128]{1,0:T(8,128)(2,1)S(1)} %get-tuple-element.109.refs_2_, bf16[64,4096]{1,0:T(8,128)(2,1)S(1)} %get-tuple-element.126.refs_3_, ...), custom_call_target="tpu_custom_call", output_to_operand_aliasing={{1}: (9, {})} | custom-call | flops 1 | bytes 1 | tf_op jit(solution)/shard_map/fin/pallas_call | solution.py:259
  (75 shorter events, 36.6 us)
Async XLA Ops:
  0.0 22.9 %collective-permute-start.3 = (bf16[448,4096]{1,0:T(8,128)(2,1)}, bf16[448,4096]{1,0:T(8,128)(2,1)}, u32[]{:S(2)}, u32[]{:S(2)}) collective-permute-start(bf16[448,4096]{1,0:T(8,128)(2,1)} %bitcast.10), channel_id=1, source_target_pairs={{0,1},{1,0},{2,3},{3,2},{4,5},{5,4},{6,7},{7,6},{8,9},{9,8},{10,11... | collective-permute-start | bytes 11010056 | tf_op jit(solution)/shard_map/move_wg/ppermute | solution.py:16
  0.5 22.5 %collective-permute-start.4 = (bf16[448,4096]{1,0:T(8,128)(2,1)}, bf16[448,4096]{1,0:T(8,128)(2,1)}, u32[]{:S(2)}, u32[]{:S(2)}) collective-permute-start(bf16[448,4096]{1,0:T(8,128)(2,1)} %bitcast.17), channel_id=1, source_target_pairs={{0,1},{1,0},{2,3},{3,2},{4,5},{5,4},{6,7},{7,6},{8,9},{9,8},{10,11... | collective-permute-start | bytes 11010056 | tf_op jit(solution)/shard_map/move_wu/ppermute | solution.py:16
  0.5 25.9 %collective-permute-start.5 = (bf16[896,2048]{1,0:T(8,128)(2,1)}, bf16[896,2048]{1,0:T(8,128)(2,1)}, u32[]{:S(2)}, u32[]{:S(2)}) collective-permute-start(bf16[896,2048]{1,0:T(8,128)(2,1)} %refs_7_.11), channel_id=1, source_target_pairs={{0,1},{1,0},{2,3},{3,2},{4,5},{5,4},{6,7},{7,6},{8,9},{9,8},{10,11... | collective-permute-start | bytes 11010056 | tf_op jit(solution)/shard_map/move_wd/ppermute | solution.py:16
  3.7 15.6 %collective-permute-start = (bf16[64,4224]{1,0:T(8,128)(2,1)S(1)}, bf16[64,4224]{1,0:T(8,128)(2,1)S(1)}, u32[]{:S(2)}, u32[]{:S(2)}) collective-permute-start(bf16[64,4224]{1,0:T(8,128)(2,1)S(1)} %get-tuple-element.106.refs_1_.refs_2_), channel_id=1, source_target_pairs={{0,4},{1,5},{2,6},{3,7},{4,0},{5,1},{6,2},{7,3},{8,12},{9,13},{10,... | collective-permute-start | bytes 1622024 | tf_op jit(solution)/shard_map/move_EA/ppermute | solution.py:73
  6.3 15.9 %collective-permute-start.2 = (bf16[64,4224]{1,0:T(8,128)(2,1)S(1)}, bf16[64,4224]{1,0:T(8,128)(2,1)S(1)}, u32[]{:S(2)}, u32[]{:S(2)}) collective-permute-start(bf16[64,4224]{1,0:T(8,128)(2,1)S(1)} %get-tuple-element.107.refs_2_), channel_id=1, source_target_pairs={{4,8},{5,9},{6,10},{7,11},{8,4},{9,5},{10,6},{11,7},{20,24},{21,25... | collective-permute-start | bytes 1622024 | tf_op jit(solution)/shard_map/move_MB/ppermute | solution.py:73
  19.2 15.2 %collective-permute-start.7 = (bf16[64,4224]{1,0:T(8,128)(2,1)S(1)}, bf16[64,4224]{1,0:T(8,128)(2,1)S(1)}, u32[]{:S(2)}, u32[]{:S(2)}) collective-permute-start(bf16[64,4224]{1,0:T(8,128)(2,1)S(1)} %get-tuple-element.107.refs_2_), channel_id=1, source_target_pairs={{0,4},{1,5},{2,6},{3,7},{4,0},{5,1},{6,2},{7,3},{8,12},{9,13},{10,... | collective-permute-start | bytes 1622024 | tf_op jit(solution)/shard_map/move_EB/ppermute | solution.py:73
  22.2 12.2 %collective-permute-start.8 = (bf16[64,4224]{1,0:T(8,128)(2,1)S(1)}, bf16[64,4224]{1,0:T(8,128)(2,1)S(1)}, u32[]{:S(2)}, u32[]{:S(2)}) collective-permute-start(bf16[64,4224]{1,0:T(8,128)(2,1)S(1)} %get-tuple-element.120.refs_1_), channel_id=1, source_target_pairs={{4,8},{5,9},{6,10},{7,11},{8,4},{9,5},{10,6},{11,7},{20,24},{21,25... | collective-permute-start | bytes 1622024 | tf_op jit(solution)/shard_map/move_NA/ppermute | solution.py:73
  23.5 22.5 %collective-permute-start.6 = (bf16[64,4224]{1,0:T(8,128)(2,1)S(1)}, bf16[64,4224]{1,0:T(8,128)(2,1)S(1)}, u32[]{:S(2)}, u32[]{:S(2)}) collective-permute-start(bf16[64,4224]{1,0:T(8,128)(2,1)S(1)} %get-tuple-element.119.refs_1_), channel_id=1, source_target_pairs={{4,0},{5,1},{6,2},{7,3},{8,12},{9,13},{10,14},{11,15},{20,16},{21,... | collective-permute-start | bytes 1622024 | tf_op jit(solution)/shard_map/move_OB/ppermute | solution.py:73
  24.8 23.1 %collective-permute-start.1 = (bf16[64,4224]{1,0:T(8,128)(2,1)S(1)}, bf16[64,4224]{1,0:T(8,128)(2,1)S(1)}, u32[]{:S(2)}, u32[]{:S(2)}) collective-permute-start(bf16[64,4224]{1,0:T(8,128)(2,1)S(1)} %get-tuple-element.111), channel_id=1, source_target_pairs={{0,2},{1,3},{2,0},{3,1},{4,6},{5,7},{6,4},{7,5},{8,10},{9,11},{10,... | collective-permute-start | bytes 1622024 | tf_op jit(solution)/shard_map/move_Y0/ppermute | solution.py:16
  32.0 17.7 %collective-permute-start.9 = (bf16[64,4224]{1,0:T(8,128)(2,1)S(1)}, bf16[64,4224]{1,0:T(8,128)(2,1)S(1)}, u32[]{:S(2)}, u32[]{:S(2)}) collective-permute-start(bf16[64,4224]{1,0:T(8,128)(2,1)S(1)} %get-tuple-element.125), channel_id=1, source_target_pairs={{4,8},{5,9},{6,10},{7,11},{8,4},{9,5},{10,6},{11,7},{20,24},{21,25... | collective-permute-start | bytes 1622024 | tf_op jit(solution)/shard_map/move_MA/ppermute | solution.py:73
  35.6 21.2 %collective-permute-start.10 = (bf16[64,4224]{1,0:T(8,128)(2,1)S(1)}, bf16[64,4224]{1,0:T(8,128)(2,1)S(1)}, u32[]{:S(2)}, u32[]{:S(2)}) collective-permute-start(bf16[64,4224]{1,0:T(8,128)(2,1)S(1)} %get-tuple-element.129.refs_1_), channel_id=1, source_target_pairs={{4,0},{5,1},{6,2},{7,3},{8,12},{9,13},{10,14},{11,15},{20,16},{21,... | collective-permute-start | bytes 1622024 | tf_op jit(solution)/shard_map/move_QA/ppermute | solution.py:73
  36.9 20.0 %collective-permute-start.11 = (bf16[64,4224]{1,0:T(8,128)(2,1)S(1)}, bf16[64,4224]{1,0:T(8,128)(2,1)S(1)}, u32[]{:S(2)}, u32[]{:S(2)}) collective-permute-start(bf16[64,4224]{1,0:T(8,128)(2,1)S(1)} %get-tuple-element.131), channel_id=1, source_target_pairs={{0,2},{1,3},{2,0},{3,1},{4,6},{5,7},{6,4},{7,5},{8,10},{9,11},{10,... | collective-permute-start | bytes 1622024 | tf_op jit(solution)/shard_map/move_Y1/ppermute | solution.py:16
  47.2 19.5 %collective-permute-start.13 = (bf16[64,4224]{1,0:T(8,128)(2,1)S(1)}, bf16[64,4224]{1,0:T(8,128)(2,1)S(1)}, u32[]{:S(2)}, u32[]{:S(2)}) collective-permute-start(bf16[64,4224]{1,0:T(8,128)(2,1)S(1)} %get-tuple-element.137), channel_id=1, source_target_pairs={{4,8},{5,9},{6,10},{7,11},{8,4},{9,5},{10,6},{11,7},{20,24},{21,25... | collective-permute-start | bytes 1622024 | tf_op jit(solution)/shard_map/move_NB/ppermute | solution.py:73
  47.9 11.4 %collective-permute-start.12 = (bf16[40,4224]{1,0:T(8,128)(2,1)S(1)}, bf16[40,4224]{1,0:T(8,128)(2,1)S(1)}, u32[]{:S(2)}, u32[]{:S(2)}) collective-permute-start(bf16[40,4224]{1,0:T(8,128)(2,1)S(1)} %get-tuple-element.134), channel_id=1, source_target_pairs={{0,2},{1,3},{2,0},{3,1},{4,6},{5,7},{6,4},{7,5},{8,10},{9,11},{10,... | collective-permute-start | bytes 1013768 | tf_op jit(solution)/shard_map/move_Y2B/ppermute | solution.py:16
  55.6 14.5 %collective-permute-start.17 = (bf16[64,4224]{1,0:T(8,128)(2,1)S(1)}, bf16[64,4224]{1,0:T(8,128)(2,1)S(1)}, u32[]{:S(2)}, u32[]{:S(2)}) collective-permute-start(bf16[64,4224]{1,0:T(8,128)(2,1)S(1)} %get-tuple-element.145.refs_1_), channel_id=1, source_target_pairs={{4,0},{5,1},{6,2},{7,3},{8,12},{9,13},{10,14},{11,15},{20,16},{21,... | collective-permute-start | bytes 1622024 | tf_op jit(solution)/shard_map/move_OA/ppermute | solution.py:73
  67.3 18.3 %collective-permute-start.15 = (bf16[64,4224]{1,0:T(8,128)(2,1)S(1)}, bf16[64,4224]{1,0:T(8,128)(2,1)S(1)}, u32[]{:S(2)}, u32[]{:S(2)}) collective-permute-start(bf16[64,4224]{1,0:T(8,128)(2,1)S(1)} %get-tuple-element.139.refs_1_), channel_id=1, source_target_pairs={{4,0},{5,1},{6,2},{7,3},{8,12},{9,13},{10,14},{11,15},{20,16},{21,... | collective-permute-start | bytes 1622024 | tf_op jit(solution)/shard_map/move_QB/ppermute | solution.py:73
  68.7 10.7 %collective-permute-start.16 = (bf16[40,4096]{1,0:T(8,128)(2,1)S(1)}, bf16[40,4096]{1,0:T(8,128)(2,1)S(1)}, u32[]{:S(2)}, u32[]{:S(2)}) collective-permute-start(bf16[40,4096]{1,0:T(8,128)(2,1)S(1)} %get-tuple-element.142), channel_id=1, source_target_pairs={{0,2},{1,3},{2,0},{3,1},{4,6},{5,7},{6,4},{7,5},{8,10},{9,11},{10,... | collective-permute-start | bytes 983048 | tf_op jit(solution)/shard_map/move_R2B/ppermute | solution.py:16
  71.8 13.7 %collective-permute-start.18 = (bf16[40,4224]{1,0:T(8,128)(2,1)S(1)}, bf16[40,4224]{1,0:T(8,128)(2,1)S(1)}, u32[]{:S(2)}, u32[]{:S(2)}) collective-permute-start(bf16[40,4224]{1,0:T(8,128)(2,1)S(1)} %get-tuple-element.152), channel_id=1, source_target_pairs={{0,2},{1,3},{2,0},{3,1},{4,6},{5,7},{6,4},{7,5},{8,10},{9,11},{10,... | collective-permute-start | bytes 1013768 | tf_op jit(solution)/shard_map/move_Y2A/ppermute | solution.py:16
  80.3 14.5 %collective-permute-start.21 = (bf16[64,4096]{1,0:T(8,128)(2,1)S(1)}, bf16[64,4096]{1,0:T(8,128)(2,1)S(1)}, u32[]{:S(2)}, u32[]{:S(2)}) collective-permute-start(bf16[64,4096]{1,0:T(8,128)(2,1)S(1)} %get-tuple-element.165), channel_id=1, source_target_pairs={{0,4},{1,5},{2,6},{3,7},{12,8},{13,9},{14,10},{15,11},{16,20},{17,... | collective-permute-start | bytes 1572872 | tf_op jit(solution)/shard_map/move_I2B/ppermute | solution.py:73
  86.8 9.4 %collective-permute-start.20 = (bf16[40,4224]{1,0:T(8,128)(2,1)S(1)}, bf16[40,4224]{1,0:T(8,128)(2,1)S(1)}, u32[]{:S(2)}, u32[]{:S(2)}) collective-permute-start(bf16[40,4224]{1,0:T(8,128)(2,1)S(1)} %get-tuple-element.163), channel_id=1, source_target_pairs={{0,2},{1,3},{2,0},{3,1},{4,6},{5,7},{6,4},{7,5},{8,10},{9,11},{10,... | collective-permute-start | bytes 1013768 | tf_op jit(solution)/shard_map/move_Y3B/ppermute | solution.py:16
  94.5 10.9 %collective-permute-start.19 = (bf16[40,4096]{1,0:T(8,128)(2,1)S(1)}, bf16[40,4096]{1,0:T(8,128)(2,1)S(1)}, u32[]{:S(2)}, u32[]{:S(2)}) collective-permute-start(bf16[40,4096]{1,0:T(8,128)(2,1)S(1)} %get-tuple-element.161), channel_id=1, source_target_pairs={{0,2},{1,3},{2,0},{3,1},{4,6},{5,7},{6,4},{7,5},{8,10},{9,11},{10,... | collective-permute-start | bytes 983048 | tf_op jit(solution)/shard_map/move_R3A/ppermute | solution.py:16
  102.8 12.2 %collective-permute-start.22 = (bf16[40,4096]{1,0:T(8,128)(2,1)S(1)}, bf16[40,4096]{1,0:T(8,128)(2,1)S(1)}, u32[]{:S(2)}, u32[]{:S(2)}) collective-permute-start(bf16[40,4096]{1,0:T(8,128)(2,1)S(1)} %get-tuple-element.176), channel_id=1, source_target_pairs={{0,2},{1,3},{2,0},{3,1},{4,6},{5,7},{6,4},{7,5},{8,10},{9,11},{10,... | collective-permute-start | bytes 983048 | tf_op jit(solution)/shard_map/move_R3B/ppermute | solution.py:16
  106.3 15.8 %collective-permute-start.24 = (bf16[64,4096]{1,0:T(8,128)(2,1)S(1)}, bf16[64,4096]{1,0:T(8,128)(2,1)S(1)}, u32[]{:S(2)}, u32[]{:S(2)}) collective-permute-start(bf16[64,4096]{1,0:T(8,128)(2,1)S(1)} %get-tuple-element.181), channel_id=1, source_target_pairs={{0,4},{1,5},{2,6},{3,7},{12,8},{13,9},{14,10},{15,11},{16,20},{17,... | collective-permute-start | bytes 1572872 | tf_op jit(solution)/shard_map/move_I3A/ppermute | solution.py:73
  108.2 15.4 %collective-permute-start.25 = (bf16[64,4096]{1,0:T(8,128)(2,1)S(1)}, bf16[64,4096]{1,0:T(8,128)(2,1)S(1)}, u32[]{:S(2)}, u32[]{:S(2)}) collective-permute-start(bf16[64,4096]{1,0:T(8,128)(2,1)S(1)} %get-tuple-element.184), channel_id=1, source_target_pairs={{0,2},{1,3},{2,0},{3,1},{4,6},{5,7},{6,4},{7,5},{8,10},{9,11},{10,... | collective-permute-start | bytes 1572872 | tf_op jit(solution)/shard_map/move_R1/ppermute | solution.py:16
  108.3 15.4 %collective-permute-start.26 = (bf16[64,4096]{1,0:T(8,128)(2,1)S(1)}, bf16[64,4096]{1,0:T(8,128)(2,1)S(1)}, u32[]{:S(2)}, u32[]{:S(2)}) collective-permute-start(bf16[64,4096]{1,0:T(8,128)(2,1)S(1)} %get-tuple-element.185), channel_id=1, source_target_pairs={{4,8},{5,9},{6,10},{7,11},{8,4},{9,5},{10,6},{11,7},{20,24},{21,25... | collective-permute-start | bytes 1572872 | tf_op jit(solution)/shard_map/move_S2B/ppermute | solution.py:73
  115.9 14.9 %collective-permute-start.28 = (bf16[64,4096]{1,0:T(8,128)(2,1)S(1)}, bf16[64,4096]{1,0:T(8,128)(2,1)S(1)}, u32[]{:S(2)}, u32[]{:S(2)}) collective-permute-start(bf16[64,4096]{1,0:T(8,128)(2,1)S(1)} %get-tuple-element.188), channel_id=1, source_target_pairs={{0,4},{1,5},{2,6},{3,7},{12,8},{13,9},{14,10},{15,11},{16,20},{17,... | collective-permute-start | bytes 1572872 | tf_op jit(solution)/shard_map/move_I3B/ppermute | solution.py:73
  122.9 9.4 %collective-permute-start.27 = (bf16[64,4096]{1,0:T(8,128)(2,1)S(1)}, bf16[64,4096]{1,0:T(8,128)(2,1)S(1)}, u32[]{:S(2)}, u32[]{:S(2)}) collective-permute-start(bf16[64,4096]{1,0:T(8,128)(2,1)S(1)} %get-tuple-element.187), channel_id=1, source_target_pairs={{4,8},{5,9},{6,10},{7,11},{8,4},{9,5},{10,6},{11,7},{20,24},{21,25... | collective-permute-start | bytes 1572872 | tf_op jit(solution)/shard_map/move_S3A/ppermute | solution.py:73
  128.1 15.0 %collective-permute-start.32 = (bf16[64,4096]{1,0:T(8,128)(2,1)S(1)}, bf16[64,4096]{1,0:T(8,128)(2,1)S(1)}, u32[]{:S(2)}, u32[]{:S(2)}) collective-permute-start(bf16[64,4096]{1,0:T(8,128)(2,1)S(1)} %get-tuple-element.196), channel_id=1, source_target_pairs={{0,4},{1,5},{2,6},{3,7},{12,8},{13,9},{14,10},{15,11},{16,20},{17,... | collective-permute-start | bytes 1572872 | tf_op jit(solution)/shard_map/move_I2A/ppermute | solution.py:73
  131.7 12.3 %collective-permute-start.31 = (bf16[64,4096]{1,0:T(8,128)(2,1)S(1)}, bf16[64,4096]{1,0:T(8,128)(2,1)S(1)}, u32[]{:S(2)}, u32[]{:S(2)}) collective-permute-start(bf16[64,4096]{1,0:T(8,128)(2,1)S(1)} %get-tuple-element.194), channel_id=1, source_target_pairs={{4,8},{5,9},{6,10},{7,11},{8,4},{9,5},{10,6},{11,7},{20,24},{21,25... | collective-permute-start | bytes 1572872 | tf_op jit(solution)/shard_map/move_S3B/ppermute | solution.py:73
  133.4 17.6 %collective-permute-start.29 = (bf16[64,4096]{1,0:T(8,128)(2,1)S(1)}, bf16[64,4096]{1,0:T(8,128)(2,1)S(1)}, u32[]{:S(2)}, u32[]{:S(2)}) collective-permute-start(bf16[64,4096]{1,0:T(8,128)(2,1)S(1)} %get-tuple-element.192), channel_id=1, source_target_pairs={{0,2},{1,3},{2,0},{3,1},{4,6},{5,7},{6,4},{7,5},{8,10},{9,11},{10,... | collective-permute-start | bytes 1572872 | tf_op jit(solution)/shard_map/move_R0/ppermute | solution.py:16
  134.6 19.7 %collective-permute-start.30 = (bf16[64,4096]{1,0:T(8,128)(2,1)S(1)}, bf16[64,4096]{1,0:T(8,128)(2,1)S(1)}, u32[]{:S(2)}, u32[]{:S(2)}) collective-permute-start(bf16[64,4096]{1,0:T(8,128)(2,1)S(1)} %get-tuple-element.193), channel_id=1, source_target_pairs={{0,4},{1,5},{2,6},{3,7},{4,0},{5,1},{6,2},{7,3},{8,12},{9,13},{10,... | collective-permute-start | bytes 1572872 | tf_op jit(solution)/shard_map/move_S1A/ppermute | solution.py:73
  145.7 15.4 %collective-permute-start.34 = (bf16[64,4096]{1,0:T(8,128)(2,1)S(1)}, bf16[64,4096]{1,0:T(8,128)(2,1)S(1)}, u32[]{:S(2)}, u32[]{:S(2)}) collective-permute-start(bf16[64,4096]{1,0:T(8,128)(2,1)S(1)} %get-tuple-element.201), channel_id=1, source_target_pairs={{0,4},{1,5},{2,6},{3,7},{4,0},{5,1},{6,2},{7,3},{8,12},{9,13},{10,... | collective-permute-start | bytes 1572872 | tf_op jit(solution)/shard_map/move_S1B/ppermute | solution.py:73
  (6 other events, 90.0 us)

commit v5 on v4

--- a/solution.py
+++ b/solution.py
@@ -212,7 +212,7 @@
         out[:, cols] = got.astype(jnp.bfloat16)
 
 
-def finish_kernel(half, idx, order, pick, own, cross, *refs):
+def finish_kernel(idx, order, pick, own, cross, *refs):
     *more, out, held, sems = refs
     width = own.shape[1]
     step = 1024
@@ -220,7 +220,7 @@
     for i, n in enumerate(range(0, width, step)):
         cols = slice(n, n + step)
         got = contract(pick[...], jnp.concatenate([own[:, cols], cross[:, cols]], 0), 0, 0)
-        sums = [sum(r[:, cols].astype(jnp.float32) for r in part) for part in (more[:half], more[half:])]
+        sums = [sum(r[:, cols].astype(jnp.float32) for r in part) for part in (more[::2], more[1::2])]
         got = (got + jnp.concatenate(sums, 0)).astype(jnp.bfloat16)
         held[i] = contract(order[...], got, 0, 0).astype(jnp.bfloat16)
         to = pl.ds(pl.multiple_of((idx[4] + n) % width, step), step)
@@ -378,11 +378,10 @@
             return fetch_kernel, outs, [], [pltpu.SemaphoreType.DMA((3,))]
         if name == "fin":
             made = [val["order"], val["pick0"], val["made0"], val["R0"]]
-            made += [val[s + q] for q in "AB" for s in ("S1", "S2", "X3") if s + q in val]
-            counts = [sum(s + q in val for s in ("S1", "S2", "X3")) for q in "AB"]
+            made += [val[s + q] for s in ("S1", "S2") for q in "AB"]
             parts = width // 1024
             scratch = [pltpu.VMEM((parts, tok_rows, 1024), bf16), pltpu.SemaphoreType.DMA((parts,))]
-            return functools.partial(finish_kernel, counts[0]), [like(tok_rows, width)], made, scratch
+            return finish_kernel, [like(tok_rows, width)], made, scratch
         slot = name[1:] if name[1:] in slots else name[1]
         made = [val[s + slot] for s in ("pick", "made", "R")]
         made += [val[x] for x in {"D2": ["I2" + q], "D3": ["I3" + q], "D1": ["S3" + q]}.get(kind, [])]

time: 164 us -> 164 us (level)
  waiting for transfers between devices: 45 us -> 47.8 us
  starting transfers between devices: 54.5 us -> 51.8 us
    ppermute x20, starting transfers between devices: 36.9 us -> 34.1 us  [along_line(): return lax.ppermute(x, 'expert', moves)]
    ppermute x20, waiting for transfers between devices: 37.5 us -> 40.3 us  [along_line(): return lax.ppermute(x, 'expert', moves)]
where the time goes in v5:
time: 164 us
  Pallas kernels  63.4 us (39%)
  starting transfers between devices  51.8 us (32%)
  waiting for transfers between devices  47.8 us (29%)
    pallas_call x29, Pallas kernels, call(): pl.pallas_call(body, out_shape=[*outs, *(jax.ShapeDtypeStruct(x.shape, x....  63.4 us
    ppermute x20, waiting for transfers between devices, along_line(): return lax.ppermute(x, 'expert', moves)  40.3 us
    ppermute x20, starting transfers between devices, along_line(): return lax.ppermute(x, 'expert', moves)  34.1 us
    ppermute x15, starting transfers between devices, swapped(): lax.ppermute(x, axis, [(i, i ^ 1 << apart) for i in range(lax.axis_size(a...  17.6 us
    ppermute x15, waiting for transfers between devices, swapped(): lax.ppermute(x, axis, [(i, i ^ 1 << apart) for i in range(lax.axis_size(a...  7.51 us
  transfers between devices with their start and end apart: 35, of which 10 were waited for; matrix products, arithmetic and copies ran while one was open for 0% of the time, Pallas kernels for 37%

profile of v5, /device:TPU:0, one launch (start us, length us, event | category | flops | bytes accessed | tf_op | source)
XLA Modules:
  0.0 163.7 jit_solution(7783309445323596204)
XLA Ops:
  1.1 2.6 %prep.1 = (bf16[64,4224]{1,0:T(8,128)(2,1)S(1)}, bf16[64,4224]{1,0:T(8,128)(2,1)S(1)}, bf16[128,128]{1,0:T(8,128)(2,1)S(1)}, f32[8,128]{1,0:T(8,128)S(1)}) custom-call(s32[6]{0:T(128)S(1)} %stack.31.refs_0_, s32[4,128]{1,0:T(4,128)} %bitcast.24, f32[4,128]{1,0:T(4,128)} %bitcast.25, bf16[128,4096]{1,0:T(8,128)(2,1)} %refs_3_.1, ...), custom_call_target="tpu_custom_call", output_to_operand_aliasing={{3}: (4, {})} | custom-call | flops 1 | bytes 1 | tf_op jit(solution)/shard_map/prep/pallas_call | solution.py:259
  3.7 2.6 %collective-permute-start = (bf16[64,4224]{1,0:T(8,128)(2,1)S(1)}, bf16[64,4224]{1,0:T(8,128)(2,1)S(1)}, u32[]{:S(2)}, u32[]{:S(2)}) collective-permute-start(bf16[64,4224]{1,0:T(8,128)(2,1)S(1)} %get-tuple-element.106.refs_1_.refs_2_), channel_id=1, source_target_pairs={{0,4},{1,5},{2,6},{3,7},{4,0},{5,1},{6,2},{7,3},{8,12},{9,13},{10,... | collective-permute-start | bytes 1622024 | tf_op jit(solution)/shard_map/move_EA/ppermute | solution.py:73
  7.0 12.3 %collective-permute-done.refs_4_ = bf16[64,4224]{1,0:T(8,128)(2,1)S(1)} collective-permute-done((bf16[64,4224]{1,0:T(8,128)(2,1)S(1)}, bf16[64,4224]{1,0:T(8,128)(2,1)S(1)}, u32[]{:S(2)}, u32[]{:S(2)}) %collective-permute-start) | collective-permute-done | bytes 540704 | tf_op jit(solution)/shard_map/move_EA/ppermute | solution.py:73
  19.2 1.7 %collective-permute-start.7 = (bf16[64,4224]{1,0:T(8,128)(2,1)S(1)}, bf16[64,4224]{1,0:T(8,128)(2,1)S(1)}, u32[]{:S(2)}, u32[]{:S(2)}) collective-permute-start(bf16[64,4224]{1,0:T(8,128)(2,1)S(1)} %get-tuple-element.107.refs_2_), channel_id=1, source_target_pairs={{0,4},{1,5},{2,6},{3,7},{4,0},{5,1},{6,2},{7,3},{8,12},{9,13},{10,... | collective-permute-start | bytes 1622024 | tf_op jit(solution)/shard_map/move_EB/ppermute | solution.py:73
  24.8 1.6 collective-permute-start.1
  26.4 5.0 %W.1 = (bf16[448,4096]{1,0:T(8,128)(2,1)S(1)}, bf16[448,4096]{1,0:T(8,128)(2,1)S(1)}, bf16[896,2048]{1,0:T(8,128)(2,1)S(1)}, f32[8,128]{1,0:T(8,128)S(1)}) custom-call(s32[6]{0:T(128)S(1)} %stack.31.refs_0_, bf16[448,4096]{1,0:T(8,128)(2,1)} %get-tuple-element.113.refs_1_, ...), custom_call_target="tpu_custom_call", output_to_operand_aliasing={{3}: (4, {})} | custom-call | flops 1 | bytes 1 | tf_op jit(solution)/shard_map/W/pallas_call | solution.py:259
  32.8 1.6 collective-permute-done.7.refs_2_.refs_4_
  36.9 1.8 %collective-permute-start.11 = (bf16[64,4224]{1,0:T(8,128)(2,1)S(1)}, bf16[64,4224]{1,0:T(8,128)(2,1)S(1)}, u32[]{:S(2)}, u32[]{:S(2)}) collective-permute-start(bf16[64,4224]{1,0:T(8,128)(2,1)S(1)} %get-tuple-element.131), channel_id=1, source_target_pairs={{0,2},{1,3},{2,0},{3,1},{4,6},{5,7},{6,4},{7,5},{8,10},{9,11},{10,... | collective-permute-start | bytes 1622024 | tf_op jit(solution)/shard_map/move_Y1/ppermute | solution.py:16
  38.7 7.3 %collective-permute-done.6.refs_2_ = bf16[64,4224]{1,0:T(8,128)(2,1)S(1)} collective-permute-done((bf16[64,4224]{1,0:T(8,128)(2,1)S(1)}, bf16[64,4224]{1,0:T(8,128)(2,1)S(1)}, u32[]{:S(2)}, u32[]{:S(2)}) %collective-permute-start.6) | collective-permute-done | bytes 540704 | tf_op jit(solution)/shard_map/move_OB/ppermute | solution.py:73
  47.9 1.8 %collective-permute-start.12 = (bf16[40,4224]{1,0:T(8,128)(2,1)S(1)}, bf16[40,4224]{1,0:T(8,128)(2,1)S(1)}, u32[]{:S(2)}, u32[]{:S(2)}) collective-permute-start(bf16[40,4224]{1,0:T(8,128)(2,1)S(1)} %get-tuple-element.134), channel_id=1, source_target_pairs={{0,2},{1,3},{2,0},{3,1},{4,6},{5,7},{6,4},{7,5},{8,10},{9,11},{10,... | collective-permute-start | bytes 1013768 | tf_op jit(solution)/shard_map/move_Y2B/ppermute | solution.py:16
  49.7 5.9 %F0.1 = (bf16[64,4096]{1,0:T(8,128)(2,1)S(1)}, bf16[64,4096]{1,0:T(8,128)(2,1)S(1)}, f32[8,128]{1,0:T(8,128)S(1)}, bf16[64,4224]{1,0:T(8,128)(2,1)S(1)}) custom-call(s32[6]{0:T(128)S(1)} %stack.31.refs_0_, bf16[64,4224]{1,0:T(8,128)(2,1)S(1)} %get-tuple-element.110.refs_1_, ...), custom_call_target="tpu_custom_call", output_to_operand_aliasing={{2}: (9, {}), {3}: (10, {})} | custom-call | flops 1 | bytes 24150016 | tf_op jit(solution)/shard_map/F0/pallas_call | solution.py:259
  59.3 5.8 %F2B.1 = (bf16[64,4096]{1,0:T(8,128)(2,1)S(1)}, bf16[40,4096]{1,0:T(8,128)(2,1)S(1)}, f32[8,128]{1,0:T(8,128)S(1)}) custom-call(s32[6]{0:T(128)S(1)} %stack.31.refs_0_, bf16[64,4224]{1,0:T(8,128)(2,1)S(1)} %get-tuple-element.133.refs_1_, bf16[40,4224]{1,0:T(8,128)(2,1)S(1)} %collective-permute-done.12.refs_2_, ...), custom_call_target="tpu_custom_call", output_to_operand_aliasing={{2}: (9, {})} | custom-call | flops 1 | bytes 23750656 | tf_op jit(solution)/shard_map/F2B/pallas_call | solution.py:259
  65.1 1.6 collective-permute-done.14.refs_3_
  67.3 1.5 collective-permute-start.15
  72.8 5.8 %F3A.1 = (bf16[64,4096]{1,0:T(8,128)(2,1)S(1)}, bf16[40,4096]{1,0:T(8,128)(2,1)S(1)}, f32[8,128]{1,0:T(8,128)S(1)}) custom-call(s32[6]{0:T(128)S(1)} %stack.31.refs_0_, bf16[64,4224]{1,0:T(8,128)(2,1)S(1)} %get-tuple-element.143.refs_1_, bf16[40,4224]{1,0:T(8,128)(2,1)S(1)} %get-tuple-element.144.refs_2_, ...), custom_call_target="tpu_custom_call", output_to_operand_aliasing={{2}: (9, {})} | custom-call | flops 1 | bytes 23750656 | tf_op jit(solution)/shard_map/F3A/pallas_call | solution.py:259
  80.3 5.2 %collective-permute-start.21 = (bf16[64,4096]{1,0:T(8,128)(2,1)S(1)}, bf16[64,4096]{1,0:T(8,128)(2,1)S(1)}, u32[]{:S(2)}, u32[]{:S(2)}) collective-permute-start(bf16[64,4096]{1,0:T(8,128)(2,1)S(1)} %get-tuple-element.165), channel_id=1, source_target_pairs={{0,4},{1,5},{2,6},{3,7},{12,8},{13,9},{14,10},{15,11},{16,20},{17,... | collective-permute-start | bytes 1572872 | tf_op jit(solution)/shard_map/move_I2B/ppermute | solution.py:73
  86.8 1.9 %collective-permute-start.20 = (bf16[40,4224]{1,0:T(8,128)(2,1)S(1)}, bf16[40,4224]{1,0:T(8,128)(2,1)S(1)}, u32[]{:S(2)}, u32[]{:S(2)}) collective-permute-start(bf16[40,4224]{1,0:T(8,128)(2,1)S(1)} %get-tuple-element.163), channel_id=1, source_target_pairs={{0,2},{1,3},{2,0},{3,1},{4,6},{5,7},{6,4},{7,5},{8,10},{9,11},{10,... | collective-permute-start | bytes 1013768 | tf_op jit(solution)/shard_map/move_Y3B/ppermute | solution.py:16
  88.6 5.9 %F1.1 = (bf16[64,4096]{1,0:T(8,128)(2,1)S(1)}, bf16[64,4096]{1,0:T(8,128)(2,1)S(1)}, f32[8,128]{1,0:T(8,128)S(1)}, bf16[40,4096]{1,0:T(8,128)(2,1)S(1)}) custom-call(s32[6]{0:T(128)S(1)} %stack.31.refs_0_, bf16[64,4224]{1,0:T(8,128)(2,1)S(1)} %get-tuple-element.128.refs_1_, ...), custom_call_target="tpu_custom_call", output_to_operand_aliasing={{2}: (9, {}), {3}: (10, {})} | custom-call | flops 1 | bytes 24150016 | tf_op jit(solution)/shard_map/F1/pallas_call | solution.py:259
  96.2 5.8 %F3B.1 = (bf16[64,4096]{1,0:T(8,128)(2,1)S(1)}, bf16[40,4096]{1,0:T(8,128)(2,1)S(1)}, f32[8,128]{1,0:T(8,128)S(1)}, bf16[64,4096]{1,0:T(8,128)(2,1)S(1)}) custom-call(s32[6]{0:T(128)S(1)} %stack.31.refs_0_, bf16[64,4224]{1,0:T(8,128)(2,1)S(1)} %get-tuple-element.162.refs_1_, ...), custom_call_target="tpu_custom_call", output_to_operand_aliasing={{2}: (9, {}), {3}: (10, {})} | custom-call | flops 1 | bytes 23750656 | tf_op jit(solution)/shard_map/F3B/pallas_call | solution.py:259
  102.8 2.6 %collective-permute-start.22 = (bf16[40,4096]{1,0:T(8,128)(2,1)S(1)}, bf16[40,4096]{1,0:T(8,128)(2,1)S(1)}, u32[]{:S(2)}, u32[]{:S(2)}) collective-permute-start(bf16[40,4096]{1,0:T(8,128)(2,1)S(1)} %get-tuple-element.176), channel_id=1, source_target_pairs={{0,2},{1,3},{2,0},{3,1},{4,6},{5,7},{6,4},{7,5},{8,10},{9,11},{10,... | collective-permute-start | bytes 983048 | tf_op jit(solution)/shard_map/move_R3B/ppermute | solution.py:16
  106.3 1.9 %collective-permute-start.24 = (bf16[64,4096]{1,0:T(8,128)(2,1)S(1)}, bf16[64,4096]{1,0:T(8,128)(2,1)S(1)}, u32[]{:S(2)}, u32[]{:S(2)}) collective-permute-start(bf16[64,4096]{1,0:T(8,128)(2,1)S(1)} %get-tuple-element.181), channel_id=1, source_target_pairs={{0,4},{1,5},{2,6},{3,7},{12,8},{13,9},{14,10},{15,11},{16,20},{17,... | collective-permute-start | bytes 1572872 | tf_op jit(solution)/shard_map/move_I3A/ppermute | solution.py:73
  109.2 5.8 %F2A.1 = (bf16[64,4096]{1,0:T(8,128)(2,1)S(1)}, bf16[40,4096]{1,0:T(8,128)(2,1)S(1)}, f32[8,128]{1,0:T(8,128)S(1)}) custom-call(s32[6]{0:T(128)S(1)} %stack.31.refs_0_, bf16[64,4224]{1,0:T(8,128)(2,1)S(1)} %get-tuple-element.157.refs_1_, bf16[40,4224]{1,0:T(8,128)(2,1)S(1)} %get-tuple-element.158.refs_2_, ...), custom_call_target="tpu_custom_call", output_to_operand_aliasing={{2}: (9, {})} | custom-call | flops 1 | bytes 23750656 | tf_op jit(solution)/shard_map/F2A/pallas_call | solution.py:259
  115.9 4.1 %collective-permute-start.28 = (bf16[64,4096]{1,0:T(8,128)(2,1)S(1)}, bf16[64,4096]{1,0:T(8,128)(2,1)S(1)}, u32[]{:S(2)}, u32[]{:S(2)}) collective-permute-start(bf16[64,4096]{1,0:T(8,128)(2,1)S(1)} %get-tuple-element.188), channel_id=1, source_target_pairs={{0,4},{1,5},{2,6},{3,7},{12,8},{13,9},{14,10},{15,11},{16,20},{17,... | collective-permute-start | bytes 1572872 | tf_op jit(solution)/shard_map/move_I3B/ppermute | solution.py:73
  120.0 2.1 %collective-permute-start.23 = (bf16[40,4096]{1,0:T(8,128)(2,1)S(1)}, bf16[40,4096]{1,0:T(8,128)(2,1)S(1)}, u32[]{:S(2)}, u32[]{:S(2)}) collective-permute-start(bf16[40,4096]{1,0:T(8,128)(2,1)S(1)} %get-tuple-element.179), channel_id=1, source_target_pairs={{0,2},{1,3},{2,0},{3,1},{4,6},{5,7},{6,4},{7,5},{8,10},{9,11},{10,... | collective-permute-start | bytes 983048 | tf_op jit(solution)/shard_map/move_R2A/ppermute | solution.py:16
  123.7 3.6 %collective-permute-done.23.refs_3_.refs_6_ = bf16[40,4096]{1,0:T(8,128)(2,1)S(1)} collective-permute-done((bf16[40,4096]{1,0:T(8,128)(2,1)S(1)}, bf16[40,4096]{1,0:T(8,128)(2,1)S(1)}, u32[]{:S(2)}, u32[]{:S(2)}) %collective-permute-start.23) | collective-permute-done | bytes 327712 | tf_op jit(solution)/shard_map/move_R2A/ppermute | solution.py:16
  128.1 2.6 %collective-permute-start.32 = (bf16[64,4096]{1,0:T(8,128)(2,1)S(1)}, bf16[64,4096]{1,0:T(8,128)(2,1)S(1)}, u32[]{:S(2)}, u32[]{:S(2)}) collective-permute-start(bf16[64,4096]{1,0:T(8,128)(2,1)S(1)} %get-tuple-element.196), channel_id=1, source_target_pairs={{0,4},{1,5},{2,6},{3,7},{12,8},{13,9},{14,10},{15,11},{16,20},{17,... | collective-permute-start | bytes 1572872 | tf_op jit(solution)/shard_map/move_I2A/ppermute | solution.py:73
  134.6 2.1 %collective-permute-start.30 = (bf16[64,4096]{1,0:T(8,128)(2,1)S(1)}, bf16[64,4096]{1,0:T(8,128)(2,1)S(1)}, u32[]{:S(2)}, u32[]{:S(2)}) collective-permute-start(bf16[64,4096]{1,0:T(8,128)(2,1)S(1)} %get-tuple-element.193), channel_id=1, source_target_pairs={{0,4},{1,5},{2,6},{3,7},{4,0},{5,1},{6,2},{7,3},{8,12},{9,13},{10,... | collective-permute-start | bytes 1572872 | tf_op jit(solution)/shard_map/move_S1A/ppermute | solution.py:73
  136.8 6.3 %collective-permute-done.32.refs_4_.refs_7_ = bf16[64,4096]{1,0:T(8,128)(2,1)S(1)} collective-permute-done((bf16[64,4096]{1,0:T(8,128)(2,1)S(1)}, bf16[64,4096]{1,0:T(8,128)(2,1)S(1)}, u32[]{:S(2)}, u32[]{:S(2)}) %collective-permute-start.32) | collective-permute-done | bytes 524320 | tf_op jit(solution)/shard_map/move_I2A/ppermute | solution.py:73
  145.0 2.6 %collective-permute-start.33 = (bf16[64,4096]{1,0:T(8,128)(2,1)S(1)}, bf16[64,4096]{1,0:T(8,128)(2,1)S(1)}, u32[]{:S(2)}, u32[]{:S(2)}) collective-permute-start(bf16[64,4096]{1,0:T(8,128)(2,1)S(1)} %get-tuple-element.200), channel_id=1, source_target_pairs={{0,4},{1,5},{2,6},{3,7},{4,0},{5,1},{6,2},{7,3},{8,12},{9,13},{10,... | collective-permute-start | bytes 1572872 | tf_op jit(solution)/shard_map/move_S1B/ppermute | solution.py:73
  148.3 6.1 %collective-permute-done.30.refs_5_ = bf16[64,4096]{1,0:T(8,128)(2,1)S(1)} collective-permute-done((bf16[64,4096]{1,0:T(8,128)(2,1)S(1)}, bf16[64,4096]{1,0:T(8,128)(2,1)S(1)}, u32[]{:S(2)}, u32[]{:S(2)}) %collective-permute-start.30) | collective-permute-done | bytes 524320 | tf_op jit(solution)/shard_map/move_S1A/ppermute | solution.py:73
  154.3 6.7 %collective-permute-done.33.refs_6_ = bf16[64,4096]{1,0:T(8,128)(2,1)S(1)} collective-permute-done((bf16[64,4096]{1,0:T(8,128)(2,1)S(1)}, bf16[64,4096]{1,0:T(8,128)(2,1)S(1)}, u32[]{:S(2)}, u32[]{:S(2)}) %collective-permute-start.33) | collective-permute-done | bytes 524320 | tf_op jit(solution)/shard_map/move_S1B/ppermute | solution.py:73
  161.1 2.4 %fin.1 = (bf16[128,4096]{1,0:T(8,128)(2,1)}, f32[8,128]{1,0:T(8,128)S(1)}) custom-call(s32[6]{0:T(128)S(1)} %stack.31.refs_0_, bf16[128,128]{1,0:T(8,128)(2,1)S(1)} %get-tuple-element.105.refs_1_, bf16[128,128]{1,0:T(8,128)(2,1)S(1)} %get-tuple-element.109.refs_2_, bf16[64,4096]{1,0:T(8,128)(2,1)S(1)} %get-tuple-element.126.refs_3_, ...), custom_call_target="tpu_custom_call", output_to_operand_aliasing={{1}: (9, {})} | custom-call | flops 1 | bytes 1 | tf_op jit(solution)/shard_map/fin/pallas_call | solution.py:259
  (75 shorter events, 36.6 us)
Async XLA Ops:
  0.0 22.9 %collective-permute-start.3 = (bf16[448,4096]{1,0:T(8,128)(2,1)}, bf16[448,4096]{1,0:T(8,128)(2,1)}, u32[]{:S(2)}, u32[]{:S(2)}) collective-permute-start(bf16[448,4096]{1,0:T(8,128)(2,1)} %bitcast.10), channel_id=1, source_target_pairs={{0,1},{1,0},{2,3},{3,2},{4,5},{5,4},{6,7},{7,6},{8,9},{9,8},{10,11... | collective-permute-start | bytes 11010056 | tf_op jit(solution)/shard_map/move_wg/ppermute | solution.py:16
  0.5 22.5 %collective-permute-start.4 = (bf16[448,4096]{1,0:T(8,128)(2,1)}, bf16[448,4096]{1,0:T(8,128)(2,1)}, u32[]{:S(2)}, u32[]{:S(2)}) collective-permute-start(bf16[448,4096]{1,0:T(8,128)(2,1)} %bitcast.17), channel_id=1, source_target_pairs={{0,1},{1,0},{2,3},{3,2},{4,5},{5,4},{6,7},{7,6},{8,9},{9,8},{10,11... | collective-permute-start | bytes 11010056 | tf_op jit(solution)/shard_map/move_wu/ppermute | solution.py:16
  0.5 25.9 %collective-permute-start.5 = (bf16[896,2048]{1,0:T(8,128)(2,1)}, bf16[896,2048]{1,0:T(8,128)(2,1)}, u32[]{:S(2)}, u32[]{:S(2)}) collective-permute-start(bf16[896,2048]{1,0:T(8,128)(2,1)} %refs_7_.11), channel_id=1, source_target_pairs={{0,1},{1,0},{2,3},{3,2},{4,5},{5,4},{6,7},{7,6},{8,9},{9,8},{10,11... | collective-permute-start | bytes 11010056 | tf_op jit(solution)/shard_map/move_wd/ppermute | solution.py:16
  3.7 15.6 %collective-permute-start = (bf16[64,4224]{1,0:T(8,128)(2,1)S(1)}, bf16[64,4224]{1,0:T(8,128)(2,1)S(1)}, u32[]{:S(2)}, u32[]{:S(2)}) collective-permute-start(bf16[64,4224]{1,0:T(8,128)(2,1)S(1)} %get-tuple-element.106.refs_1_.refs_2_), channel_id=1, source_target_pairs={{0,4},{1,5},{2,6},{3,7},{4,0},{5,1},{6,2},{7,3},{8,12},{9,13},{10,... | collective-permute-start | bytes 1622024 | tf_op jit(solution)/shard_map/move_EA/ppermute | solution.py:73
  6.3 15.9 %collective-permute-start.2 = (bf16[64,4224]{1,0:T(8,128)(2,1)S(1)}, bf16[64,4224]{1,0:T(8,128)(2,1)S(1)}, u32[]{:S(2)}, u32[]{:S(2)}) collective-permute-start(bf16[64,4224]{1,0:T(8,128)(2,1)S(1)} %get-tuple-element.107.refs_2_), channel_id=1, source_target_pairs={{4,8},{5,9},{6,10},{7,11},{8,4},{9,5},{10,6},{11,7},{20,24},{21,25... | collective-permute-start | bytes 1622024 | tf_op jit(solution)/shard_map/move_MB/ppermute | solution.py:73
  19.2 15.2 %collective-permute-start.7 = (bf16[64,4224]{1,0:T(8,128)(2,1)S(1)}, bf16[64,4224]{1,0:T(8,128)(2,1)S(1)}, u32[]{:S(2)}, u32[]{:S(2)}) collective-permute-start(bf16[64,4224]{1,0:T(8,128)(2,1)S(1)} %get-tuple-element.107.refs_2_), channel_id=1, source_target_pairs={{0,4},{1,5},{2,6},{3,7},{4,0},{5,1},{6,2},{7,3},{8,12},{9,13},{10,... | collective-permute-start | bytes 1622024 | tf_op jit(solution)/shard_map/move_EB/ppermute | solution.py:73
  22.2 12.2 %collective-permute-start.8 = (bf16[64,4224]{1,0:T(8,128)(2,1)S(1)}, bf16[64,4224]{1,0:T(8,128)(2,1)S(1)}, u32[]{:S(2)}, u32[]{:S(2)}) collective-permute-start(bf16[64,4224]{1,0:T(8,128)(2,1)S(1)} %get-tuple-element.120.refs_1_), channel_id=1, source_target_pairs={{4,8},{5,9},{6,10},{7,11},{8,4},{9,5},{10,6},{11,7},{20,24},{21,25... | collective-permute-start | bytes 1622024 | tf_op jit(solution)/shard_map/move_NA/ppermute | solution.py:73
  23.5 22.5 %collective-permute-start.6 = (bf16[64,4224]{1,0:T(8,128)(2,1)S(1)}, bf16[64,4224]{1,0:T(8,128)(2,1)S(1)}, u32[]{:S(2)}, u32[]{:S(2)}) collective-permute-start(bf16[64,4224]{1,0:T(8,128)(2,1)S(1)} %get-tuple-element.119.refs_1_), channel_id=1, source_target_pairs={{4,0},{5,1},{6,2},{7,3},{8,12},{9,13},{10,14},{11,15},{20,16},{21,... | collective-permute-start | bytes 1622024 | tf_op jit(solution)/shard_map/move_OB/ppermute | solution.py:73
  24.8 23.1 %collective-permute-start.1 = (bf16[64,4224]{1,0:T(8,128)(2,1)S(1)}, bf16[64,4224]{1,0:T(8,128)(2,1)S(1)}, u32[]{:S(2)}, u32[]{:S(2)}) collective-permute-start(bf16[64,4224]{1,0:T(8,128)(2,1)S(1)} %get-tuple-element.111), channel_id=1, source_target_pairs={{0,2},{1,3},{2,0},{3,1},{4,6},{5,7},{6,4},{7,5},{8,10},{9,11},{10,... | collective-permute-start | bytes 1622024 | tf_op jit(solution)/shard_map/move_Y0/ppermute | solution.py:16
  32.0 17.7 %collective-permute-start.9 = (bf16[64,4224]{1,0:T(8,128)(2,1)S(1)}, bf16[64,4224]{1,0:T(8,128)(2,1)S(1)}, u32[]{:S(2)}, u32[]{:S(2)}) collective-permute-start(bf16[64,4224]{1,0:T(8,128)(2,1)S(1)} %get-tuple-element.125), channel_id=1, source_target_pairs={{4,8},{5,9},{6,10},{7,11},{8,4},{9,5},{10,6},{11,7},{20,24},{21,25... | collective-permute-start | bytes 1622024 | tf_op jit(solution)/shard_map/move_MA/ppermute | solution.py:73
  35.6 21.2 %collective-permute-start.10 = (bf16[64,4224]{1,0:T(8,128)(2,1)S(1)}, bf16[64,4224]{1,0:T(8,128)(2,1)S(1)}, u32[]{:S(2)}, u32[]{:S(2)}) collective-permute-start(bf16[64,4224]{1,0:T(8,128)(2,1)S(1)} %get-tuple-element.129.refs_1_), channel_id=1, source_target_pairs={{4,0},{5,1},{6,2},{7,3},{8,12},{9,13},{10,14},{11,15},{20,16},{21,... | collective-permute-start | bytes 1622024 | tf_op jit(solution)/shard_map/move_QA/ppermute | solution.py:73
  36.9 20.0 %collective-permute-start.11 = (bf16[64,4224]{1,0:T(8,128)(2,1)S(1)}, bf16[64,4224]{1,0:T(8,128)(2,1)S(1)}, u32[]{:S(2)}, u32[]{:S(2)}) collective-permute-start(bf16[64,4224]{1,0:T(8,128)(2,1)S(1)} %get-tuple-element.131), channel_id=1, source_target_pairs={{0,2},{1,3},{2,0},{3,1},{4,6},{5,7},{6,4},{7,5},{8,10},{9,11},{10,... | collective-permute-start | bytes 1622024 | tf_op jit(solution)/shard_map/move_Y1/ppermute | solution.py:16
  47.2 19.5 %collective-permute-start.13 = (bf16[64,4224]{1,0:T(8,128)(2,1)S(1)}, bf16[64,4224]{1,0:T(8,128)(2,1)S(1)}, u32[]{:S(2)}, u32[]{:S(2)}) collective-permute-start(bf16[64,4224]{1,0:T(8,128)(2,1)S(1)} %get-tuple-element.137), channel_id=1, source_target_pairs={{4,8},{5,9},{6,10},{7,11},{8,4},{9,5},{10,6},{11,7},{20,24},{21,25... | collective-permute-start | bytes 1622024 | tf_op jit(solution)/shard_map/move_NB/ppermute | solution.py:73
  47.9 11.4 %collective-permute-start.12 = (bf16[40,4224]{1,0:T(8,128)(2,1)S(1)}, bf16[40,4224]{1,0:T(8,128)(2,1)S(1)}, u32[]{:S(2)}, u32[]{:S(2)}) collective-permute-start(bf16[40,4224]{1,0:T(8,128)(2,1)S(1)} %get-tuple-element.134), channel_id=1, source_target_pairs={{0,2},{1,3},{2,0},{3,1},{4,6},{5,7},{6,4},{7,5},{8,10},{9,11},{10,... | collective-permute-start | bytes 1013768 | tf_op jit(solution)/shard_map/move_Y2B/ppermute | solution.py:16
  55.6 14.5 %collective-permute-start.17 = (bf16[64,4224]{1,0:T(8,128)(2,1)S(1)}, bf16[64,4224]{1,0:T(8,128)(2,1)S(1)}, u32[]{:S(2)}, u32[]{:S(2)}) collective-permute-start(bf16[64,4224]{1,0:T(8,128)(2,1)S(1)} %get-tuple-element.145.refs_1_), channel_id=1, source_target_pairs={{4,0},{5,1},{6,2},{7,3},{8,12},{9,13},{10,14},{11,15},{20,16},{21,... | collective-permute-start | bytes 1622024 | tf_op jit(solution)/shard_map/move_OA/ppermute | solution.py:73
  67.3 18.3 %collective-permute-start.15 = (bf16[64,4224]{1,0:T(8,128)(2,1)S(1)}, bf16[64,4224]{1,0:T(8,128)(2,1)S(1)}, u32[]{:S(2)}, u32[]{:S(2)}) collective-permute-start(bf16[64,4224]{1,0:T(8,128)(2,1)S(1)} %get-tuple-element.139.refs_1_), channel_id=1, source_target_pairs={{4,0},{5,1},{6,2},{7,3},{8,12},{9,13},{10,14},{11,15},{20,16},{21,... | collective-permute-start | bytes 1622024 | tf_op jit(solution)/shard_map/move_QB/ppermute | solution.py:73
  68.7 10.7 %collective-permute-start.16 = (bf16[40,4096]{1,0:T(8,128)(2,1)S(1)}, bf16[40,4096]{1,0:T(8,128)(2,1)S(1)}, u32[]{:S(2)}, u32[]{:S(2)}) collective-permute-start(bf16[40,4096]{1,0:T(8,128)(2,1)S(1)} %get-tuple-element.142), channel_id=1, source_target_pairs={{0,2},{1,3},{2,0},{3,1},{4,6},{5,7},{6,4},{7,5},{8,10},{9,11},{10,... | collective-permute-start | bytes 983048 | tf_op jit(solution)/shard_map/move_R2B/ppermute | solution.py:16
  71.8 13.7 %collective-permute-start.18 = (bf16[40,4224]{1,0:T(8,128)(2,1)S(1)}, bf16[40,4224]{1,0:T(8,128)(2,1)S(1)}, u32[]{:S(2)}, u32[]{:S(2)}) collective-permute-start(bf16[40,4224]{1,0:T(8,128)(2,1)S(1)} %get-tuple-element.152), channel_id=1, source_target_pairs={{0,2},{1,3},{2,0},{3,1},{4,6},{5,7},{6,4},{7,5},{8,10},{9,11},{10,... | collective-permute-start | bytes 1013768 | tf_op jit(solution)/shard_map/move_Y2A/ppermute | solution.py:16
  80.3 14.5 %collective-permute-start.21 = (bf16[64,4096]{1,0:T(8,128)(2,1)S(1)}, bf16[64,4096]{1,0:T(8,128)(2,1)S(1)}, u32[]{:S(2)}, u32[]{:S(2)}) collective-permute-start(bf16[64,4096]{1,0:T(8,128)(2,1)S(1)} %get-tuple-element.165), channel_id=1, source_target_pairs={{0,4},{1,5},{2,6},{3,7},{12,8},{13,9},{14,10},{15,11},{16,20},{17,... | collective-permute-start | bytes 1572872 | tf_op jit(solution)/shard_map/move_I2B/ppermute | solution.py:73
  94.5 10.9 %collective-permute-start.19 = (bf16[40,4096]{1,0:T(8,128)(2,1)S(1)}, bf16[40,4096]{1,0:T(8,128)(2,1)S(1)}, u32[]{:S(2)}, u32[]{:S(2)}) collective-permute-start(bf16[40,4096]{1,0:T(8,128)(2,1)S(1)} %get-tuple-element.161), channel_id=1, source_target_pairs={{0,2},{1,3},{2,0},{3,1},{4,6},{5,7},{6,4},{7,5},{8,10},{9,11},{10,... | collective-permute-start | bytes 983048 | tf_op jit(solution)/shard_map/move_R3A/ppermute | solution.py:16
  102.8 12.2 %collective-permute-start.22 = (bf16[40,4096]{1,0:T(8,128)(2,1)S(1)}, bf16[40,4096]{1,0:T(8,128)(2,1)S(1)}, u32[]{:S(2)}, u32[]{:S(2)}) collective-permute-start(bf16[40,4096]{1,0:T(8,128)(2,1)S(1)} %get-tuple-element.176), channel_id=1, source_target_pairs={{0,2},{1,3},{2,0},{3,1},{4,6},{5,7},{6,4},{7,5},{8,10},{9,11},{10,... | collective-permute-start | bytes 983048 | tf_op jit(solution)/shard_map/move_R3B/ppermute | solution.py:16
  106.3 15.8 %collective-permute-start.24 = (bf16[64,4096]{1,0:T(8,128)(2,1)S(1)}, bf16[64,4096]{1,0:T(8,128)(2,1)S(1)}, u32[]{:S(2)}, u32[]{:S(2)}) collective-permute-start(bf16[64,4096]{1,0:T(8,128)(2,1)S(1)} %get-tuple-element.181), channel_id=1, source_target_pairs={{0,4},{1,5},{2,6},{3,7},{12,8},{13,9},{14,10},{15,11},{16,20},{17,... | collective-permute-start | bytes 1572872 | tf_op jit(solution)/shard_map/move_I3A/ppermute | solution.py:73
  108.2 15.4 %collective-permute-start.25 = (bf16[64,4096]{1,0:T(8,128)(2,1)S(1)}, bf16[64,4096]{1,0:T(8,128)(2,1)S(1)}, u32[]{:S(2)}, u32[]{:S(2)}) collective-permute-start(bf16[64,4096]{1,0:T(8,128)(2,1)S(1)} %get-tuple-element.184), channel_id=1, source_target_pairs={{0,2},{1,3},{2,0},{3,1},{4,6},{5,7},{6,4},{7,5},{8,10},{9,11},{10,... | collective-permute-start | bytes 1572872 | tf_op jit(solution)/shard_map/move_R1/ppermute | solution.py:16
  108.3 15.4 %collective-permute-start.26 = (bf16[64,4096]{1,0:T(8,128)(2,1)S(1)}, bf16[64,4096]{1,0:T(8,128)(2,1)S(1)}, u32[]{:S(2)}, u32[]{:S(2)}) collective-permute-start(bf16[64,4096]{1,0:T(8,128)(2,1)S(1)} %get-tuple-element.185), channel_id=1, source_target_pairs={{4,8},{5,9},{6,10},{7,11},{8,4},{9,5},{10,6},{11,7},{20,24},{21,25... | collective-permute-start | bytes 1572872 | tf_op jit(solution)/shard_map/move_S2B/ppermute | solution.py:73
  115.9 14.9 %collective-permute-start.28 = (bf16[64,4096]{1,0:T(8,128)(2,1)S(1)}, bf16[64,4096]{1,0:T(8,128)(2,1)S(1)}, u32[]{:S(2)}, u32[]{:S(2)}) collective-permute-start(bf16[64,4096]{1,0:T(8,128)(2,1)S(1)} %get-tuple-element.188), channel_id=1, source_target_pairs={{0,4},{1,5},{2,6},{3,7},{12,8},{13,9},{14,10},{15,11},{16,20},{17,... | collective-permute-start | bytes 1572872 | tf_op jit(solution)/shard_map/move_I3B/ppermute | solution.py:73
  122.9 9.4 %collective-permute-start.27 = (bf16[64,4096]{1,0:T(8,128)(2,1)S(1)}, bf16[64,4096]{1,0:T(8,128)(2,1)S(1)}, u32[]{:S(2)}, u32[]{:S(2)}) collective-permute-start(bf16[64,4096]{1,0:T(8,128)(2,1)S(1)} %get-tuple-element.187), channel_id=1, source_target_pairs={{4,8},{5,9},{6,10},{7,11},{8,4},{9,5},{10,6},{11,7},{20,24},{21,25... | collective-permute-start | bytes 1572872 | tf_op jit(solution)/shard_map/move_S3A/ppermute | solution.py:73
  128.1 15.0 %collective-permute-start.32 = (bf16[64,4096]{1,0:T(8,128)(2,1)S(1)}, bf16[64,4096]{1,0:T(8,128)(2,1)S(1)}, u32[]{:S(2)}, u32[]{:S(2)}) collective-permute-start(bf16[64,4096]{1,0:T(8,128)(2,1)S(1)} %get-tuple-element.196), channel_id=1, source_target_pairs={{0,4},{1,5},{2,6},{3,7},{12,8},{13,9},{14,10},{15,11},{16,20},{17,... | collective-permute-start | bytes 1572872 | tf_op jit(solution)/shard_map/move_I2A/ppermute | solution.py:73
  131.7 12.3 %collective-permute-start.31 = (bf16[64,4096]{1,0:T(8,128)(2,1)S(1)}, bf16[64,4096]{1,0:T(8,128)(2,1)S(1)}, u32[]{:S(2)}, u32[]{:S(2)}) collective-permute-start(bf16[64,4096]{1,0:T(8,128)(2,1)S(1)} %get-tuple-element.194), channel_id=1, source_target_pairs={{4,8},{5,9},{6,10},{7,11},{8,4},{9,5},{10,6},{11,7},{20,24},{21,25... | collective-permute-start | bytes 1572872 | tf_op jit(solution)/shard_map/move_S3B/ppermute | solution.py:73
  133.4 14.9 %collective-permute-start.29 = (bf16[64,4096]{1,0:T(8,128)(2,1)S(1)}, bf16[64,4096]{1,0:T(8,128)(2,1)S(1)}, u32[]{:S(2)}, u32[]{:S(2)}) collective-permute-start(bf16[64,4096]{1,0:T(8,128)(2,1)S(1)} %get-tuple-element.192), channel_id=1, source_target_pairs={{0,2},{1,3},{2,0},{3,1},{4,6},{5,7},{6,4},{7,5},{8,10},{9,11},{10,... | collective-permute-start | bytes 1572872 | tf_op jit(solution)/shard_map/move_R0/ppermute | solution.py:16
  134.6 19.7 %collective-permute-start.30 = (bf16[64,4096]{1,0:T(8,128)(2,1)S(1)}, bf16[64,4096]{1,0:T(8,128)(2,1)S(1)}, u32[]{:S(2)}, u32[]{:S(2)}) collective-permute-start(bf16[64,4096]{1,0:T(8,128)(2,1)S(1)} %get-tuple-element.193), channel_id=1, source_target_pairs={{0,4},{1,5},{2,6},{3,7},{4,0},{5,1},{6,2},{7,3},{8,12},{9,13},{10,... | collective-permute-start | bytes 1572872 | tf_op jit(solution)/shard_map/move_S1A/ppermute | solution.py:73
  145.0 16.1 %collective-permute-start.33 = (bf16[64,4096]{1,0:T(8,128)(2,1)S(1)}, bf16[64,4096]{1,0:T(8,128)(2,1)S(1)}, u32[]{:S(2)}, u32[]{:S(2)}) collective-permute-start(bf16[64,4096]{1,0:T(8,128)(2,1)S(1)} %get-tuple-element.200), channel_id=1, source_target_pairs={{0,4},{1,5},{2,6},{3,7},{4,0},{5,1},{6,2},{7,3},{8,12},{9,13},{10,... | collective-permute-start | bytes 1572872 | tf_op jit(solution)/shard_map/move_S1B/ppermute | solution.py:73
  147.6 13.5 %collective-permute-start.34 = (bf16[64,4096]{1,0:T(8,128)(2,1)S(1)}, bf16[64,4096]{1,0:T(8,128)(2,1)S(1)}, u32[]{:S(2)}, u32[]{:S(2)}) collective-permute-start(bf16[64,4096]{1,0:T(8,128)(2,1)S(1)} %get-tuple-element.201), channel_id=1, source_target_pairs={{4,8},{5,9},{6,10},{7,11},{8,4},{9,5},{10,6},{11,7},{20,24},{21,25... | collective-permute-start | bytes 1572872 | tf_op jit(solution)/shard_map/move_S2A/ppermute | solution.py:73
  (6 other events, 90.1 us)
